TPU v7x, 512 devices: a whole 4x4x16 slice. The times are simulated.
512 devices in a mesh: pt: 32 (over z, core), ctr: 16 (over y, x).
Axes of the slice: x: 4, y: 4, z: 16, core: 2. Of those that a mesh axis runs over, the one named last changes fastest.
Arguments:
- points: bfloat16 [32768, 128], P('pt'), may hold values from -1.56 to 1.56
- centres: bfloat16 [65536, 128], P(('pt', 'ctr')), may hold values from -1.56 to 1.56
- factor: float32 [65536, 128], P(('pt', 'ctr')), as said below
- solution: float32 [65536, 64], P(('pt', 'ctr')), may hold values from -4 to 4
- residual: float32 [65536, 64], P(('pt', 'ctr')), may hold values from -6 to 6
- direction: float32 [65536, 64], P(('pt', 'ctr')), may hold values from -6 to 6
Outputs:
- solution_out: float32 [65536, 64], P(('pt', 'ctr'))
- residual_out: float32 [65536, 64], P(('pt', 'ctr'))
Inputs may be any that keep to these rules, and one draw needn't show every extreme that they name: `factor`: each block of 128 rows is lower triangular with a diagonal between 1 and 2.
All inputs are finite; a program needn't handle non-finite values.
Results may differ from a plain program's by a relative error of at most 0.0046.
Values may be sent and summed in bfloat16 or wider, within the bound.
No kernel may reach another device: no remote copies, remote signals or barrier semaphores. Data moves between devices by JAX's collectives and lax.ppermute only.
A program may use at most 64 MiB of HBM per device.

v0:
```python
import math

import jax
import jax.numpy as jnp
from jax import lax
from jax.sharding import PartitionSpec as P

ITERS = 2


GAMMA_SCALE = 0.8
RIDGE = 64.0


def row_gaps(rows):
    wide = rows.astype(jnp.float32)
    return rows.shape[1] - jnp.sum(wide * wide, axis=1)


def kernel_block(pts, gap_p, cen, gap_c, gamma):
    cross = lax.dot_general(pts, cen, (((1,), (1,)), ((), ())), preferred_element_type=jnp.float32)
    return jnp.exp(gamma * (2.0 * cross + gap_p[:, None] + gap_c[None, :])).astype(jnp.bfloat16)


def precondition(factor, resid):
    width = factor.shape[1]
    blocks = factor.reshape(-1, width, width)
    rhs = resid.reshape(blocks.shape[0], width, resid.shape[1])
    lower = lax.linalg.triangular_solve(blocks, rhs, left_side=True, lower=True)
    upper = lax.linalg.triangular_solve(blocks, lower, left_side=True, lower=True, transpose_a=True)
    return upper.reshape(resid.shape)


def body(points, centres, factor, solution, residual, direction):
    gamma = GAMMA_SCALE / math.sqrt(points.shape[1])
    total_points = points.shape[0] * lax.axis_size("pt")
    cen_all = lax.all_gather(centres, "pt", axis=0, tiled=True)
    gap_p = row_gaps(points)
    gap_c = row_gaps(cen_all)

    def tile_cols():
        return kernel_block(points, gap_p, cen_all, gap_c, gamma)

    def inner(left, right):
        local = jnp.sum(left * right)
        return lax.psum(local, ("pt", "ctr"))

    coeffs, resid, search, blocks = (solution, residual, direction, factor)
    precond = precondition(blocks, resid)
    rz_now = inner(resid, precond)
    for step_index in range(ITERS):
        vec_b = search.astype(jnp.bfloat16)
        partial_value = jnp.dot(
            tile_cols(),
            lax.all_gather(vec_b, "pt", axis=0, tiled=True),
            preferred_element_type=jnp.float32,
        )
        point_vals = lax.psum(partial_value, "ctr").astype(jnp.bfloat16)
        grads = lax.psum_scatter(
            lax.dot_general(
                tile_cols(),
                point_vals,
                (((0,), (0,)), ((), ())),
                preferred_element_type=jnp.float32,
            ),
            "pt",
            scatter_dimension=0,
            tiled=True,
        )
        image = grads / total_points + RIDGE * search
        alpha = rz_now / inner(search, image)
        coeffs = coeffs + alpha * search
        resid = resid - alpha * image
        if step_index + 1 < ITERS:
            precond = precondition(blocks, resid)
            rz_next = inner(resid, precond)
            search = precond + rz_next / rz_now * search
            rz_now = rz_next
    return (coeffs, resid)


def solution(mesh):
    placed = (
        P("pt", None),
        P(("pt", "ctr"), None),
        P(("pt", "ctr"), None),
        P(("pt", "ctr"), None),
        P(("pt", "ctr"), None),
        P(("pt", "ctr"), None),
    )
    return jax.shard_map(
        body,
        mesh=mesh,
        in_specs=placed,
        out_specs=(P(("pt", "ctr"), None), P(("pt", "ctr"), None)),
        check_vma=False,
    )
```

profile of v0, /device:TPU:1, one launch (start us, length us, event | category | flops | bytes accessed | tf_op | source)
XLA Modules:
  0.0 829.9 jit_solution(6011042456321412024)
XLA Ops:
  7.2 0.0 all-gather.2.cloned.1.call-start
  7.2 0.7 all-gather.2.cloned.1.call-update
  7.9 0.0 reduce-scatter.3.cloned.1.call-start
  7.9 0.8 convert_element_type.27
  8.7 1.2 multiply_reduce_fusion.1
  9.9 39.1 %all_gather.10 = bf16[4096,64]{0,1:T(8,128)(2,1)S(1)} all-gather(bf16[128,64]{0,1:T(8,128)(2,1)S(1)} %convert_element_type.27), channel_id=1, replica_groups=mesh['pt'=32,'ctr'=16] {'pt'}, dimensions={0}, use_global_device_ids=true | all-gather | bytes 540672 | tf_op jit(solution)/shard_map/all_gather | solution.py:55
  49.0 37.6 %all-gather.2.cloned.1.call-done = bf16[4096,128]{1,0:T(8,128)(2,1)} async-done(((bf16[128,128]{1,0:T(8,128)(2,1)}), bf16[4096,128]{1,0:T(8,128)(2,1)}) %all-gather.2.cloned.1.call-update) | async-done | bytes 1048592 | tf_op jit(solution)/shard_map/all_gather | solution.py:37
  86.5 1.8 multiply_reduce_fusion
  88.4 5.6 exponential_convert_fusion
  94.0 3.2 copy-done
  97.2 2.3 fusion.14
  99.6 65.6 %all-reduce.3 = bf16[1024,64]{1,0:T(8,128)(2,1)S(1)} all-reduce(f32[1024,64]{1,0:T(8,128)S(1)} %fusion.14), channel_id=1, replica_groups=mesh['pt'=32,'ctr'=16] {'ctr'}, use_global_device_ids=true, to_apply=%region_4.7 | all-reduce | flops 65536 | bytes 393216 | tf_op jit(solution)/shard_map/psum | solution.py:58
  165.2 6.1 fusion.17
  171.3 0.0 reduce-scatter.5.cloned.1.call-start
  171.4 9.8 %custom-call.9 = f32[1,1,128,128]{2,3,1,0:T(8,128)S(1)} custom-call(f32[1,1,128,128]{3,2,1,0:T(8,128)S(1)} %fusion.12), custom_call_target="InvertDiagBlocksLowerTriangular" | custom-call | tf_op jit(solution)/shard_map/triangular_solve/custom-call.0 | solution.py:30
  181.2 0.2 fusion.9
  181.4 0.8 fusion
  182.2 101.6 %reduce-scatter.3.cloned.1.call-done = f32[128,64]{0,1:T(8,128)} async-done(((f32[4096,64]{0,1:T(8,128)}), f32[128,64]{0,1:T(8,128)}) %reduce-scatter.3.cloned.1.call-update) | async-done | bytes 32784 | tf_op jit(solution)/shard_map/reduce_scatter | solution.py:59
  283.8 1.4 multiply_reduce_fusion.4
  285.2 106.0 %all-reduce = (f32[]{:T(128)}, f32[]{:T(128)}) all-reduce(f32[]{:T(128)} %fusion, f32[]{:T(128)} %multiply_reduce_fusion.4), channel_id=1, replica_groups=mesh['pt'=32,'ctr'=16] {'pt','ctr'}, use_global_device_ids=true, to_apply=%region_1.4 | all-reduce | flops 2 | bytes 16 | tf_op jit(solution)/shard_map/psum | solution.py:46
  392.6 0.8 multiply_subtract_fusion.1
  393.3 0.2 fusion.5
  393.5 0.8 multiply_reduce_fusion.3
  394.4 98.6 %psum.45 = f32[]{:T(128)} all-reduce(f32[]{:T(128)} %get-tuple-element.10), channel_id=1, replica_groups=mesh['pt'=32,'ctr'=16] {'pt','ctr'}, use_global_device_ids=true, to_apply=%region_9.12 | all-reduce | flops 1 | bytes 8 | tf_op jit(solution)/shard_map/psum | solution.py:46
  494.4 32.0 %all_gather.11 = bf16[4096,64]{0,1:T(8,128)(2,1)S(1)} all-gather(bf16[128,64]{0,1:T(8,128)(2,1)S(1)} %get-tuple-element.6), channel_id=1, replica_groups=mesh['pt'=32,'ctr'=16] {'pt'}, dimensions={0}, use_global_device_ids=true | all-gather | bytes 540672 | tf_op jit(solution)/shard_map/all_gather | solution.py:55
  526.4 5.7 fusion.15
  532.1 63.0 %all-reduce.4 = bf16[1024,64]{1,0:T(8,128)(2,1)S(1)} all-reduce(f32[1024,64]{1,0:T(8,128)S(1)} %fusion.15), channel_id=1, replica_groups=mesh['pt'=32,'ctr'=16] {'ctr'}, use_global_device_ids=true, to_apply=%region_10.13 | all-reduce | flops 65536 | bytes 393216 | tf_op jit(solution)/shard_map/psum | solution.py:58
  595.1 6.1 fusion.16
  601.2 112.1 %reduce-scatter.5.cloned.1.call-done = f32[128,64]{0,1:T(8,128)} async-done(((f32[4096,64]{0,1:T(8,128)}), f32[128,64]{0,1:T(8,128)}) %reduce-scatter.5.cloned.1.call-update) | async-done | bytes 32784 | tf_op jit(solution)/shard_map/reduce_scatter | solution.py:59
  713.3 1.4 multiply_reduce_fusion.2
  714.6 106.0 %psum.47 = f32[]{:T(128)} all-reduce(f32[]{:T(128)} %multiply_reduce_fusion.2), channel_id=1, replica_groups=mesh['pt'=32,'ctr'=16] {'pt','ctr'}, use_global_device_ids=true, to_apply=%region_13.16 | all-reduce | flops 1 | bytes 8 | tf_op jit(solution)/shard_map/psum | solution.py:46
  822.0 1.4 multiply_subtract_fusion
  (15 shorter events, 0.1 us)
Async XLA Ops:
  7.2 79.4 %all-gather.2.cloned.1.call-start = ((), (), s32[]{:S(2)}) async-start(), calls=%async_computation.2 | async-start | bytes 1081344 | tf_op jit(solution)/shard_map/all_gather | solution.py:37
  7.9 275.9 %reduce-scatter.3.cloned.1.call-start = ((), (), s32[]{:S(2)}) async-start(), calls=%async_computation.3 | async-start | bytes 1081344 | tf_op jit(solution)/shard_map/reduce_scatter | solution.py:59
  94.0 3.2 copy-start
  99.5 71.8 %copy-start.3 = (f32[128,128]{1,0:T(8,128)S(1)}, f32[128,128]{1,0:T(8,128)}, u32[]{:S(2)}) copy-start(f32[128,128]{1,0:T(8,128)} %param.12) | copy-start | bytes 196612
  99.5 81.7 %copy-start.2 = (f32[128,64]{0,1:T(8,128)S(1)}, f32[128,64]{0,1:T(8,128)}, u32[]{:S(2)}) copy-start(f32[128,64]{0,1:T(8,128)} %param.14) | copy-start | bytes 98308
  99.6 184.3 %copy-start.1 = (f32[128,64]{0,1:T(8,128)S(1)}, f32[128,64]{0,1:T(8,128)}, u32[]{:S(2)}) copy-start(f32[128,64]{0,1:T(8,128)} %param.15) | copy-start | bytes 98308
  171.3 542.0 %reduce-scatter.5.cloned.1.call-start = ((), (), s32[]{:S(2)}) async-start(), calls=%async_computation.4 | async-start | bytes 1081344 | tf_op jit(solution)/shard_map/reduce_scatter | solution.py:59
  532.1 289.9 %copy-start.4 = (f32[128,64]{0,1:T(8,128)S(1)}, f32[128,64]{0,1:T(8,128)}, u32[]{:S(2)}) copy-start(f32[128,64]{0,1:T(8,128)} %param.13) | copy-start | bytes 98308
Sparse Core Ops, SparseCore 0:
  10.1 76.3 all-gather.1
  171.4 112.3 reduce-scatter.2
  601.3 111.9 reduce-scatter.4
where the time goes:
time: 831 us; the launch traced here: 830 us
  blocking collectives  510 us (61%)
  waiting for transfers between devices  252 us (30%)
  matrix products  27.8 us (3%)
  other arithmetic  18.5 us (2%)
  between operations  17.9 us (2%)
    psum x3, blocking collectives, inner(): return lax.psum(local, ('pt', 'ctr'))  311 us
    reduce_scatter x2, waiting for transfers between devices, body(): lax.psum_scatter(lax.dot_general(tile_cols(), point_vals, (((0,), (0,)),...  214 us
    psum x2, blocking collectives, body(): point_vals = lax.psum(partial_value, 'ctr').astype(jnp.bfloat16)  129 us
    all_gather x2, blocking collectives, body(): lax.all_gather(vec_b, 'pt', axis=0, tiled=True)  71.1 us
    all_gather x1, waiting for transfers between devices, body(): cen_all = lax.all_gather(centres, 'pt', axis=0, tiled=True)  37.6 us
  transfers between devices with their start and end apart: 3, of which 3 were waited for; matrix products, arithmetic and copies ran while one was open for 2% of the time, Pallas kernels for 0%

commit v1 on v0

v1 whole, which is shorter than its diff:
```python
import math

import jax
import jax.numpy as jnp
from jax import lax
from jax.sharding import Mesh, PartitionSpec as P

ITERS = 2
GAMMA_SCALE = 0.8
RIDGE = 64.0
CORES = 2
ROWS = 16
BF = jnp.bfloat16
F32 = jnp.float32


def row_gaps(rows):
    wide = rows.astype(F32)
    return rows.shape[1] - jnp.sum(wide * wide, axis=1)


def precondition(factor, resid):
    lower = lax.linalg.triangular_solve(factor, resid, left_side=True, lower=True)
    return lax.linalg.triangular_solve(factor, lower, left_side=True, lower=True, transpose_a=True)


def exchange(blocks, axes):
    return lax.all_to_all(blocks, axes, 0, 0, tiled=True)


def spread(block, axes):
    count = lax.axis_size(axes)
    return exchange(jnp.broadcast_to(block[None], (count,) + block.shape), axes)


def pack(scalars):
    values = jnp.stack(scalars)
    pieces = []
    for _ in range(3):
        piece = lax.reduce_precision(values, 8, 7)
        pieces.append(piece)
        values = values - piece
    flat = jnp.concatenate(pieces).astype(BF)
    return jnp.zeros((ROWS, 128), BF).at[0, : flat.shape[0]].set(flat)


def unpack(rows, count):
    wide = rows[:, 0, : 3 * count].astype(F32)
    return jnp.sum(wide.reshape(-1, 3, count), axis=(0, 1))


def body(points, centres, factor, solution, residual, direction):
    dim = points.shape[1]
    gamma = GAMMA_SCALE / math.sqrt(dim)
    outs = direction.shape[1]
    n_z, n_ctr = lax.axis_size("z"), lax.axis_size("ctr")
    n_a = CORES * n_ctr
    total_points = points.shape[0] * n_z * CORES
    share = points.shape[0] // n_ctr

    mine = lax.dynamic_slice_in_dim(points, lax.axis_index("ctr") * share, share, 0)
    pts = spread(mine, "z").reshape(n_z * share, dim)

    p0 = direction.T
    got = spread(jnp.concatenate([centres, p0.astype(BF)], 0), "ctr")
    got = lax.all_gather(got, "core", axis=0, tiled=True)
    cen = got[:, :dim].reshape(-1, dim)
    p0_all = got[:, dim:]

    gap_p, gap_c = row_gaps(pts), row_gaps(cen)
    cross = lax.dot_general(pts, cen, (((1,), (1,)), ((), ())), preferred_element_type=F32)
    tile = jnp.exp(gamma * (2.0 * cross + gap_p[:, None] + gap_c[None, :])).astype(BF)

    def apply(v_all, scalars):
        v = v_all.transpose(1, 0, 2).reshape(outs, -1)
        u = lax.dot_general(v, tile, (((1,), (1,)), ((), ())), preferred_element_type=F32)
        u = u.reshape(outs, -1, 128).transpose(1, 0, 2).reshape(n_z, -1, 128)
        u = jnp.sum(exchange(u, "z"), axis=0).astype(BF)
        u = spread(jnp.concatenate([u, pack(scalars)], 0), "z")
        local = unpack(u[:, -ROWS:], len(scalars))
        u = u[:, :-ROWS].reshape(-1, outs, 128).transpose(1, 0, 2).reshape(outs, -1)
        return u, local

    def back(u, scalars):
        v = jnp.dot(u, tile, preferred_element_type=F32)
        v = v.reshape(outs, n_a, 128).transpose(1, 0, 2)
        ride = jnp.zeros((8, 128), F32).at[0, : len(scalars)].set(jnp.stack(scalars))
        ride = jnp.broadcast_to(ride[None], (n_a, 8, 128))
        v = jnp.sum(exchange(jnp.concatenate([v, ride], 1), ("core", "ctr")), axis=0)
        return v[:-8] / total_points, v[-8, : len(scalars)]

    def dots(left, right):
        return jnp.sum(left.astype(F32) * right.astype(F32))

    def total(value):
        block = jnp.full((8, 128), value, F32)
        for axes in ("z", ("core", "ctr")):
            block = jnp.sum(spread(block, axes), axis=0)
        return block[0, 0]

    z0 = precondition(factor, residual)
    u0, s = apply(p0_all, [jnp.sum(residual * z0), dots(p0, p0)])
    v0, s = back(u0, [s[0], s[1], dots(u0, u0)])
    rz0 = s[0]
    q0 = v0 + RIDGE * p0
    alpha0 = rz0 / (s[2] / total_points + RIDGE * s[1])
    r1 = residual.T - alpha0 * q0
    z1 = precondition(factor, r1.T).T
    rz1 = total(dots(r1, z1))
    p1 = z1 + rz1 / rz0 * p0

    p1_all = spread(p1.astype(BF), "ctr")
    p1_all = lax.all_gather(p1_all, "core", axis=0, tiled=True)
    u1, s = apply(p1_all, [dots(p1, p1)])
    v1, s = back(u1, [s[0], dots(u1, u1)])
    q1 = v1 + RIDGE * p1
    alpha1 = rz1 / (s[1] / total_points + RIDGE * s[0])
    x2 = solution + (alpha0 * p0 + alpha1 * p1).T
    r2 = (r1 - alpha1 * q1).T
    return x2, r2


def solution(mesh):
    shape = (mesh.shape["pt"] // CORES, CORES, mesh.shape["ctr"])
    fine = Mesh(mesh.devices.reshape(shape), ("z", "core", "ctr"))
    rows = P(("z", "core", "ctr"), None)
    return jax.shard_map(
        body,
        mesh=fine,
        in_specs=(P(("z", "core"), None),) + (rows,) * 5,
        out_specs=(rows, rows),
        check_vma=False,
    )
```

time: 831 us -> 306 us (0.37)
  blocking collectives: 510 us -> 172 us
  waiting for transfers between devices: 252 us -> 8.66 us
  starting transfers between devices: 0.12 us -> 24.5 us
  local copies, waits for them, and re-layouts: 3.24 us -> 22.6 us
    psum x5 -> x0, blocking collectives: 439 us -> none  [the longest x3 311 us: inner(): return lax.psum(local, ('pt', 'ctr'))]
    reduce_scatter x2 -> x0, waiting for transfers between devices: 214 us -> none  [body(): lax.psum_scatter(lax.dot_general(tile_cols(), point_vals, (((0,), (0,)),...]
    all_to_all x0 -> x8, blocking collectives: none -> 169 us  [exchange(): return lax.all_to_all(blocks, axes, 0, 0, tiled=True)]
    all_gather x2 -> x1, blocking collectives: 71.1 us -> 3.34 us  [body(): p1_all = lax.all_gather(p1_all, 'core', axis=0, tiled=True)]
    all_gather x1, waiting for transfers between devices: 37.6 us -> 0.01 us  [body(): got = lax.all_gather(got, 'core', axis=0, tiled=True)]
    all_to_all x0 -> x3, starting transfers between devices: none -> 24.5 us  [exchange(): return lax.all_to_all(blocks, axes, 0, 0, tiled=True)]
    dot_general x0 -> x1, local copies, waits for them, and re-layouts: none -> 12 us  [back(): v = jnp.dot(u, tile, preferred_element_type=F32)]
    all_to_all x0 -> x3, waiting for transfers between devices: none -> 8.64 us  [exchange(): return lax.all_to_all(blocks, axes, 0, 0, tiled=True)]
  transfers between devices with their start and end apart: 3 -> 4, of which waited for: 3 -> 3; matrix products, arithmetic and copies ran while one was open for 2% -> 9% of each run, Pallas kernels for 0% -> 0%
where the time goes in v1:
time: 306 us; the launch traced here: 304 us
  blocking collectives  172 us (56%)
  matrix products  28.5 us (9%)
  between operations  24.7 us (8%)
  starting transfers between devices  24.5 us (8%)
  other arithmetic  22.8 us (7%)
  local copies, waits for them, and re-layouts  22.6 us (7%)
  waiting for transfers between devices  8.66 us (3%)
    all_to_all x8, blocking collectives, exchange(): return lax.all_to_all(blocks, axes, 0, 0, tiled=True)  169 us
    all_to_all x3, starting transfers between devices, exchange(): return lax.all_to_all(blocks, axes, 0, 0, tiled=True)  24.5 us
    dot_general x2, matrix products, back(): v = jnp.dot(u, tile, preferred_element_type=F32)  12.1 us
    dot_general x1, local copies, waits for them, and re-layouts, back(): v = jnp.dot(u, tile, preferred_element_type=F32)  12 us
    dot_general x2, matrix products, apply(): lax.dot_general(v, tile, (((1,), (1,)), ((), ())), preferred_element_type...  10.1 us
    another operation x2, other arithmetic, precondition(): lax.linalg.triangular_solve(factor, lower, left_side=True, lower=True, tr...  9.82 us
    all_to_all x3, waiting for transfers between devices, exchange(): return lax.all_to_all(blocks, axes, 0, 0, tiled=True)  8.64 us
  transfers between devices with their start and end apart: 4, of which 3 were waited for; matrix products, arithmetic and copies ran while one was open for 9% of the time, Pallas kernels for 0%

profile of v1, /device:TPU:1, one launch (start us, length us, event | category | flops | bytes accessed | tf_op | source)
XLA Modules:
  0.0 304.2 jit_solution(1848007374791722050)
XLA Ops:
  7.2 1.4 convert_bitcast_fusion
  8.7 0.8 pad_maximum_fusion.2
  9.6 19.3 %all_to_all.55 = bf16[16,192,128]{2,1,0:T(8,128)(2,1)} all-to-all(bf16[16,192,128]{2,1,0:T(8,128)(2,1)S(1)} %broadcast_in_dim.20), channel_id=1, replica_groups=mesh['z'=16,'core'=2,'ctr'=16] {'ctr'}, dimensions={0} | all-to-all | bytes 1572864 | tf_op jit(solution)/shard_map/all_to_all | solution.py:28
  29.0 29.2 %all_to_all.56 = bf16[16,64,128]{2,1,0:T(8,128)(2,1)S(1)} all-to-all(bf16[16,64,128]{2,1,0:T(8,128)(2,1)S(1)} %broadcast_in_dim.21), channel_id=1, replica_groups=mesh['z'=16,'core'=2,'ctr'=16] {'z'}, dimensions={0} | all-to-all | bytes 524288 | tf_op jit(solution)/shard_map/all_to_all | solution.py:28
  58.5 1.8 multiply_reduce_fusion
  60.3 1.1 slice_bitcast_fusion
  62.0 1.3 slice.144
  63.3 4.3 %exponential_convert_fusion = bf16[1024,4096]{1,0:T(8,128)(2,1)S(1)} fusion(bf16[1024,128]{1,0:T(8,128)(2,1)S(1)} %bitcast.113, bf16[4096,128]{1,0:T(8,128)(2,1)S(1)} %bitcast.112, f32[4096]{0:T(1024)S(1)} %subtract_bitcast_fusion, f32[1024]{0:T(1024)S(1)} %sub.58), kind=kOutput, calls=%fused_computation | convolution fusion | flops 1094713344 | bytes 9719808 | tf_op jit(solution)/shard_map/dot_general | solution.py:71
  67.7 3.2 %copy-done.1 = bf16[1024,4096]{1,0:T(8,128)(2,1)} copy-done((bf16[1024,4096]{1,0:T(8,128)(2,1)}, bf16[1024,4096]{1,0:T(8,128)(2,1)S(1)}, u32[]{:S(2)}) %copy-start.1) | copy-done | bytes 8388632
  70.9 3.4 %fusion.45 = f32[64,8,128]{2,0,1:T(8,128)} fusion(bf16[64,4096,1]{1,0,2:T(8,128)(2,1)S(1)} %reshape.346, bf16[8,128,4096]{2,1,0:T(8,128)(2,1)S(1)} %bitcast.102), kind=kOutput, calls=%fused_computation.85 | convolution fusion | flops 536870912 | bytes 9175040 | tf_op jit(solution)/shard_map/dot_general | solution.py:76
  74.2 9.9 %all-to-all-start.2 = ((f32[16,32,128]{2,1,0:T(8,128)}), f32[16,32,128]{2,1,0:T(8,128)S(1)}, u32[]{:S(2)}, u32[]{:S(2)}) async-start(f32[16,32,128]{2,1,0:T(8,128)} %bitcast.7), calls=%async_computation.2 | async-start | bytes 524288 | tf_op jit(solution)/shard_map/all_to_all | solution.py:28
  84.1 9.8 %custom-call.9 = f32[1,128,128]{1,2,0:T(8,128)S(1)} custom-call(f32[1,128,128]{2,1,0:T(8,128)S(1)} %select_bitcast_fusion), custom_call_target="InvertDiagBlocksLowerTriangular" | custom-call | tf_op jit(solution)/shard_map/triangular_solve/custom-call.0 | solution.py:24
  94.2 0.8 fusion
  95.0 1.4 fusion.37
  97.6 11.0 %all-to-all-start.3 = ((bf16[16,48,128]{2,1,0:T(8,128)(2,1)}), bf16[16,48,128]{2,1,0:T(8,128)(2,1)S(1)}, u32[]{:S(2)}, u32[]{:S(2)}) async-start(bf16[16,48,128]{2,1,0:T(8,128)(2,1)} %broadcast_in_dim.22), calls=%async_computation.3 | async-start | bytes 393216 | tf_op jit(solution)/shard_map/all_to_all | solution.py:28
  108.7 12.0 %copy.33 = bf16[4096,1024]{1,0:T(8,128)(2,1)} copy(bf16[4096,1024]{0,1:T(8,128)(2,1)} %bitcast.103) | data formatting | bytes 16777216 | tf_op jit(solution)/shard_map/dot_general | solution.py:85
  122.0 0.7 maximum_bitcast_fusion
  122.7 6.0 %convolution_bitcast_fusion.1 = f32[32,64,128]{2,1,0:T(8,128)S(1)} fusion(bf16[64,1024,1]{1,0,2:T(8,128)(2,1)S(1)} %reshape.347, bf16[32,128,1024]{2,1,0:T(8,128)(2,1)} %bitcast.105), kind=kOutput, calls=%fused_computation.3 | convolution fusion | flops 536870912 | bytes 9568256 | tf_op jit(solution)/shard_map/dot_general | solution.py:85
  128.9 28.8 %all_to_all.57 = f32[32,72,128]{2,1,0:T(8,128)S(1)} all-to-all(f32[32,72,128]{2,1,0:T(8,128)S(1)} %pad_maximum_fusion), channel_id=1, replica_groups=mesh['z'=16,'core'=2,'ctr'=16] {'core','ctr'}, dimensions={0} | all-to-all | bytes 2359296 | tf_op jit(solution)/shard_map/all_to_all | solution.py:28
  160.4 0.8 fusion.15
  161.9 19.2 %all_to_all.58 = f32[16,8,128]{2,1,0:T(8,128)S(1)} all-to-all(f32[16,8,128]{2,1,0:T(8,128)S(1)} %broadcast_in_dim_broadcast_in_dim_broadcast_in_dim.3), channel_id=1, replica_groups=mesh['z'=16,'core'=2,'ctr'=16] {'z'}, dimensions={0} | all-to-all | bytes 131072 | tf_op jit(solution)/shard_map/all_to_all | solution.py:28
  181.1 13.0 %all_to_all.59 = f32[32,8,128]{2,1,0:T(8,128)S(1)} all-to-all(f32[32,8,128]{2,1,0:T(8,128)S(1)} %broadcast_in_dim.26), channel_id=1, replica_groups=mesh['z'=16,'core'=2,'ctr'=16] {'core','ctr'}, dimensions={0} | all-to-all | bytes 262144 | tf_op jit(solution)/shard_map/all_to_all | solution.py:28
  195.9 11.1 %all_to_all.60 = bf16[16,64,128]{2,1,0:T(8,128)(2,1)S(1)} all-to-all(bf16[16,64,128]{2,1,0:T(8,128)(2,1)S(1)} %broadcast_in_dim.27), channel_id=1, replica_groups=mesh['z'=16,'core'=2,'ctr'=16] {'ctr'}, dimensions={0} | all-to-all | bytes 524288 | tf_op jit(solution)/shard_map/all_to_all | solution.py:28
  207.0 3.3 %all_gather.7 = bf16[32,64,128]{2,1,0:T(8,128)(2,1)S(1)} all-gather(bf16[16,64,128]{2,1,0:T(8,128)(2,1)S(1)} %all_to_all.60), channel_id=1, replica_groups=mesh['z'=16,'core'=2,'ctr'=16] {'core'}, dimensions={0}, use_global_device_ids=true | all-gather | bytes 786432 | tf_op jit(solution)/shard_map/all_gather | solution.py:113
  210.9 6.7 %fusion.46 = f32[64,8,128]{2,0,1:T(8,128)} fusion(bf16[64,4096,1]{1,0,2:T(8,128)(2,1)S(1)} %reshape.348, bf16[8,128,4096]{2,1,0:T(8,128)(2,1)} %bitcast.104), kind=kOutput, calls=%fused_computation.86 | convolution fusion | flops 536870912 | bytes 9175040 | tf_op jit(solution)/shard_map/dot_general | solution.py:76
  217.6 3.5 %all-to-all-start.8 = ((f32[16,32,128]{2,1,0:T(8,128)}), f32[16,32,128]{2,1,0:T(8,128)S(1)}, u32[]{:S(2)}, u32[]{:S(2)}) async-start(f32[16,32,128]{2,1,0:T(8,128)} %bitcast.38), calls=%async_computation.8 | async-start | bytes 524288 | tf_op jit(solution)/shard_map/all_to_all | solution.py:28
  227.0 0.7 fusion.34
  227.7 7.8 %all-to-all-done.8 = f32[16,32,128]{2,1,0:T(8,128)S(1)} async-done(((f32[16,32,128]{2,1,0:T(8,128)}), f32[16,32,128]{2,1,0:T(8,128)S(1)}, u32[]{:S(2)}, u32[]{:S(2)}) %all-to-all-start.8) | async-done | bytes 262176 | tf_op jit(solution)/shard_map/all_to_all | solution.py:28
  235.6 22.2 %all_to_all.61 = bf16[16,48,128]{2,1,0:T(8,128)(2,1)S(1)} all-to-all(bf16[16,48,128]{2,1,0:T(8,128)(2,1)S(1)} %broadcast_in_dim.28), channel_id=1, replica_groups=mesh['z'=16,'core'=2,'ctr'=16] {'z'}, dimensions={0} | all-to-all | bytes 393216 | tf_op jit(solution)/shard_map/all_to_all | solution.py:28
  258.7 6.0 %convolution_bitcast_fusion = f32[32,64,128]{2,1,0:T(8,128)S(1)} fusion(bf16[64,1024,1]{1,0,2:T(8,128)(2,1)S(1)} %reshape.349, bf16[32,128,1024]{2,1,0:T(8,128)(2,1)} %bitcast.106), kind=kOutput, calls=%fused_computation.2 | convolution fusion | flops 536870912 | bytes 9568256 | tf_op jit(solution)/shard_map/dot_general | solution.py:85
  265.5 1.4 maximum_bitcast_fusion.1
  267.0 26.4 %all_to_all.62 = f32[32,72,128]{2,1,0:T(8,128)S(1)} all-to-all(f32[32,72,128]{2,1,0:T(8,128)S(1)} %pad_maximum_fusion.1), channel_id=1, replica_groups=mesh['z'=16,'core'=2,'ctr'=16] {'core','ctr'}, dimensions={0} | all-to-all | bytes 2359296 | tf_op jit(solution)/shard_map/all_to_all | solution.py:28
  (71 shorter events, 11.0 us)
Async XLA Ops:
  7.2 21.7 %copy-start = (bf16[1024,128]{1,0:T(8,128)(2,1)S(1)}, bf16[1024,128]{1,0:T(8,128)(2,1)}, u32[]{:S(2)}) copy-start(bf16[1024,128]{1,0:T(8,128)(2,1)} %param.18) | copy-start | bytes 786436
  7.2 51.3 %all-gather.2.cloned.1.call-start = ((), (), s32[]{:S(2)}) async-start(), calls=%async_computation.11 | async-start | bytes 2359296 | tf_op jit(solution)/shard_map/all_gather | solution.py:66
  67.6 3.2 %copy-start.1 = (bf16[1024,4096]{1,0:T(8,128)(2,1)}, bf16[1024,4096]{1,0:T(8,128)(2,1)S(1)}, u32[]{:S(2)}) copy-start(bf16[1024,4096]{1,0:T(8,128)(2,1)S(1)} %exponential_convert_fusion) | copy-start | bytes 25165828
  67.7 16.5 %copy-start.4 = (f32[128,128]{1,0:T(8,128)S(1)}, f32[128,128]{1,0:T(8,128)}, u32[]{:S(2)}) copy-start(f32[128,128]{1,0:T(8,128)} %param.20) | copy-start | bytes 196612
  67.7 26.3 %copy-start.3 = (f32[128,64]{0,1:T(8,128)S(1)}, f32[128,64]{0,1:T(8,128)}, u32[]{:S(2)}) copy-start(f32[128,64]{0,1:T(8,128)} %param.22) | copy-start | bytes 98308
  74.2 22.7 %all-to-all-start.2 = ((f32[16,32,128]{2,1,0:T(8,128)}), f32[16,32,128]{2,1,0:T(8,128)S(1)}, u32[]{:S(2)}, u32[]{:S(2)}) async-start(f32[16,32,128]{2,1,0:T(8,128)} %bitcast.7), calls=%async_computation.2 | async-start | bytes 524288 | tf_op jit(solution)/shard_map/all_to_all | solution.py:28
  97.6 23.4 %all-to-all-start.3 = ((bf16[16,48,128]{2,1,0:T(8,128)(2,1)}), bf16[16,48,128]{2,1,0:T(8,128)(2,1)S(1)}, u32[]{:S(2)}, u32[]{:S(2)}) async-start(bf16[16,48,128]{2,1,0:T(8,128)(2,1)} %broadcast_in_dim.22), calls=%async_computation.3 | async-start | bytes 393216 | tf_op jit(solution)/shard_map/all_to_all | solution.py:28
  120.6 39.6 %copy-start.2 = (f32[128,64]{0,1:T(8,128)S(1)}, f32[128,64]{0,1:T(8,128)}, u32[]{:S(2)}) copy-start(f32[128,64]{0,1:T(8,128)} %param.23) | copy-start | bytes 98308
  217.6 17.9 %all-to-all-start.8 = ((f32[16,32,128]{2,1,0:T(8,128)}), f32[16,32,128]{2,1,0:T(8,128)S(1)}, u32[]{:S(2)}, u32[]{:S(2)}) async-start(f32[16,32,128]{2,1,0:T(8,128)} %bitcast.38), calls=%async_computation.8 | async-start | bytes 524288 | tf_op jit(solution)/shard_map/all_to_all | solution.py:28
  257.9 38.9 %copy-start.5 = (f32[128,64]{0,1:T(8,128)S(1)}, f32[128,64]{0,1:T(8,128)}, u32[]{:S(2)}) copy-start(f32[128,64]{0,1:T(8,128)} %param.21) | copy-start | bytes 98308
Sparse Core Ops, SparseCore 0:
  29.0 25.0 all-gather.1

commit v2 on v1

v2 whole, which is shorter than its diff:
```python
import functools
import math

import jax
import jax.numpy as jnp
from jax import lax
from jax.experimental import pallas as pl
from jax.experimental.pallas import tpu as pltpu
from jax.sharding import Mesh, PartitionSpec as P

GAMMA_SCALE = 0.8
RIDGE = 64.0
CORES = 2
LANES = 128
GROUP = 2
ROWS = 16
RIDE = 8
BF = jnp.bfloat16
F32 = jnp.float32
PARAMS = pltpu.CompilerParams(vmem_limit_bytes=40 * 1024 * 1024)


def row_gaps(rows):
    wide = rows.astype(F32)
    return rows.shape[1] - jnp.sum(wide * wide, axis=1)


def precondition(factor, resid):
    lower = lax.linalg.triangular_solve(factor, resid, left_side=True, lower=True)
    return lax.linalg.triangular_solve(factor, lower, left_side=True, lower=True, transpose_a=True)


def exchange(blocks, axes):
    return lax.all_to_all(blocks, axes, 0, 0, tiled=True)


def spread(block, axes):
    count = lax.axis_size(axes)
    return exchange(jnp.broadcast_to(block[None], (count,) + block.shape), axes)


def other_core(block):
    return lax.ppermute(block, "core", [(0, 1), (1, 0)])


def pack(rows):
    pieces = []
    for row in rows:
        for _ in range(3):
            piece = lax.reduce_precision(row, 8, 7)
            pieces.append(piece)
            row = row - piece
    pieces += [jnp.zeros_like(pieces[0])] * (ROWS - len(pieces))
    return jnp.stack(pieces).astype(BF)


def chunks_of(total):
    half = total.shape[0] // 2
    return [
        total[part * half : (part + 1) * half, at : at + LANES]
        for at in range(0, total.shape[1], LANES)
        for part in range(2)
    ]


def add_up(step, part, before_ref, u_ref, acc):
    @pl.when(step == 0)
    def _():
        acc[...] = part

    @pl.when(step > 0)
    def _():
        acc[...] += part

    @pl.when(step == pl.num_programs(0) - 1)
    def _():
        for at, piece in enumerate(chunks_of(acc[...])):
            u_ref[at] = piece if before_ref is None else piece + before_ref[at]


def build_kernel(gamma, first, pts_ref, gap_ref, blk_ref, *rest):
    before_ref = None if first else rest[0]
    tile_ref, u_ref, acc = rest[-3:]
    dim = pts_ref.shape[1]
    blk = blk_ref[...]
    cen = jnp.concatenate([blk[g, :LANES] for g in range(GROUP)], axis=0)
    vec = jnp.concatenate([blk[g, LANES:] for g in range(GROUP)], axis=1)
    wide = cen.astype(F32)
    gap_c = dim - jnp.sum(wide * wide, axis=1, keepdims=True)
    cross = lax.dot_general(cen, pts_ref[...], (((1,), (1,)), ((), ())), preferred_element_type=F32)
    tile = jnp.exp(gamma * (2.0 * cross + gap_c + gap_ref[...])).astype(BF)
    tile_ref[...] = tile
    part = jnp.dot(vec, tile, preferred_element_type=F32)
    add_up(pl.program_id(0), part, before_ref, u_ref, acc)


def apply_kernel(first, blk_ref, tile_ref, *rest):
    before_ref = None if first else rest[0]
    u_ref, acc = rest[-2:]
    blk = blk_ref[...]
    vec = jnp.concatenate([blk[g] for g in range(GROUP)], axis=1)
    part = jnp.dot(vec, tile_ref[...], preferred_element_type=F32)
    add_up(pl.program_id(0), part, before_ref, u_ref, acc)


def back_kernel(count, u_ref, tile_ref, v_ref, ub, ride):
    outs = ub.shape[0]
    half = outs // 2

    @pl.when(pl.program_id(0) == 0)
    def _():
        squares = jnp.zeros((half, LANES), F32)
        for at in range(u_ref.shape[0]):
            piece = u_ref[at, :half]
            low = (at % 2) * half
            ub[low : low + half, (at // 2) * LANES : (at // 2 + 1) * LANES] = piece
            squares += piece.astype(F32) * piece.astype(F32)
        packed = jnp.sum(u_ref[:, half:].astype(F32), axis=0)
        rows = [packed[3 * k : 3 * k + 1] + packed[3 * k + 1 : 3 * k + 2] + packed[3 * k + 2 : 3 * k + 3] for k in range(count)]
        rows.append(jnp.sum(squares, axis=0, keepdims=True))
        rows.append(jnp.zeros((RIDE - count - 1, LANES), F32))
        ride[...] = jnp.concatenate(rows, axis=0)

    v = lax.dot_general(ub[...], tile_ref[...], (((1,), (1,)), ((), ())), preferred_element_type=F32)
    for g in range(GROUP):
        v_ref[g, :outs] = v[:, g * LANES : (g + 1) * LANES]
        v_ref[g, outs:] = ride[...]


def body(points, centres, factor, solution, residual, direction):
    dim = points.shape[1]
    gamma = GAMMA_SCALE / math.sqrt(dim)
    outs = direction.shape[1]
    n_z, n_ctr = lax.axis_size("z"), lax.axis_size("ctr")
    total_points = points.shape[0] * n_z * CORES
    n_pts = points.shape[0]
    share = n_pts // n_ctr
    wide = GROUP * LANES
    grid = (n_ctr // GROUP,)
    u_shape = jax.ShapeDtypeStruct((2 * n_pts // LANES, outs // 2, LANES), F32)
    whole = lambda shape: pl.BlockSpec(shape, lambda i: (0,) * len(shape))
    blocks = lambda rows: pl.BlockSpec((GROUP, rows, LANES), lambda i: (i, 0, 0))
    tiles = pl.BlockSpec((wide, n_pts), lambda i: (i, 0))
    acc = pltpu.VMEM((outs, n_pts), F32)
    work = n_ctr * LANES * n_pts

    def cost(flops, exps, size):
        return pl.CostEstimate(flops=flops, transcendentals=exps, bytes_accessed=size)

    def build(pts, gap, blk, before):
        first = before is None
        extra = [] if first else [before]
        return pl.pallas_call(
            functools.partial(build_kernel, gamma, first),
            grid=grid,
            in_specs=[whole(pts.shape), whole(gap.shape), blocks(blk.shape[1])] + [whole(u_shape.shape)] * len(extra),
            out_specs=[tiles, whole(u_shape.shape)],
            out_shape=[jax.ShapeDtypeStruct((n_ctr * LANES, n_pts), BF), u_shape],
            scratch_shapes=[acc],
            compiler_params=PARAMS,
            cost_estimate=cost(2 * work * (dim + outs), work, 2 * work),
            name="build_tile",
        )(pts, gap, blk, *extra)

    def apply(blk, tile, before):
        first = before is None
        extra = [] if first else [before]
        return pl.pallas_call(
            functools.partial(apply_kernel, first),
            grid=grid,
            in_specs=[blocks(outs), tiles] + [whole(u_shape.shape)] * len(extra),
            out_specs=whole(u_shape.shape),
            out_shape=u_shape,
            scratch_shapes=[acc],
            compiler_params=PARAMS,
            cost_estimate=cost(2 * work * outs, 0, 2 * work),
            name="apply_tile",
        )(blk, tile, *extra)

    def back(u, tile, count):
        return pl.pallas_call(
            functools.partial(back_kernel, count),
            grid=grid,
            in_specs=[whole(u.shape), tiles],
            out_specs=blocks(outs + RIDE),
            out_shape=jax.ShapeDtypeStruct((n_ctr, outs + RIDE, LANES), F32),
            scratch_shapes=[pltpu.VMEM((outs, n_pts), BF), pltpu.VMEM((RIDE, LANES), F32)],
            compiler_params=PARAMS,
            cost_estimate=cost(2 * work * outs, 0, 2 * work),
            name="back_tile",
        )(u, tile)

    def reduce_points(u, rows):
        u = jnp.sum(exchange(u, "z"), axis=0).astype(BF)
        return spread(jnp.concatenate([u, pack(rows)], 0), "z")

    def reduce_centres(u, tile, tile_other, count):
        v = other_core(back(u, tile_other, count))
        v = back(u, tile, count) + v
        v = jnp.sum(exchange(v, "ctr"), axis=0)
        return v[:outs] / total_points, jnp.sum(v[outs : outs + count + 1], axis=1)

    def lanes(left, right):
        return jnp.sum(left * right, axis=0)

    mine = lax.dynamic_slice_in_dim(points, lax.axis_index("ctr") * share, share, 0)
    pts = spread(mine, "z").reshape(n_pts, dim)
    gap = row_gaps(pts)[None]
    p0 = direction.T
    own = spread(jnp.concatenate([centres, p0.astype(BF)], 0), "ctr")
    other = other_core(own)

    tile, u0 = build(pts, gap, own, None)
    tile_other, u0 = build(pts, gap, other, u0)
    z0 = precondition(factor, residual)
    u0 = reduce_points(u0, [lanes(residual.T, z0.T), lanes(p0, p0)])
    v0, s = reduce_centres(u0, tile, tile_other, 2)
    rz0 = s[0]
    q0 = v0 + RIDGE * p0
    alpha0 = rz0 / (s[2] / total_points + RIDGE * s[1])
    r1 = residual.T - alpha0 * q0
    z1 = precondition(factor, r1.T).T
    block = jnp.broadcast_to(lanes(r1, z1)[None], (RIDE, LANES))
    for axes in ("z", ("core", "ctr")):
        block = jnp.sum(spread(block, axes), axis=0)
    rz1 = jnp.sum(block[0])
    p1 = z1 + rz1 / rz0 * p0

    own = spread(p1.astype(BF), "ctr")
    other = other_core(own)
    u1 = apply(own, tile, None)
    u1 = apply(other, tile_other, u1)
    u1 = reduce_points(u1, [lanes(p1, p1)])
    v1, s = reduce_centres(u1, tile, tile_other, 1)
    q1 = v1 + RIDGE * p1
    alpha1 = rz1 / (s[1] / total_points + RIDGE * s[0])
    x2 = solution + (alpha0 * p0 + alpha1 * p1).T
    r2 = (r1 - alpha1 * q1).T
    return x2, r2


def solution(mesh):
    shape = (mesh.shape["pt"] // CORES, CORES, mesh.shape["ctr"])
    fine = Mesh(mesh.devices.reshape(shape), ("z", "core", "ctr"))
    rows = P(("z", "core", "ctr"), None)
    return jax.shard_map(
        body,
        mesh=fine,
        in_specs=(P(("z", "core"), None),) + (rows,) * 5,
        out_specs=(rows, rows),
        check_vma=False,
    )
```

time: 306 us -> 275 us (0.90)
  blocking collectives: 172 us -> 117 us
  starting transfers between devices: 24.5 us -> 59.2 us
  waiting for transfers between devices: 8.66 us -> 37.9 us
  matrix products: 28.5 us -> 1.14 us
  Pallas kernels: 0 us -> 24.2 us
  between operations: 24.7 us -> 6.15 us
  other arithmetic: 22.8 us -> 14.1 us
  local copies, waits for them, and re-layouts: 22.6 us -> 14.1 us
    all_to_all x8 -> x7, blocking collectives: 169 us -> 117 us  [exchange(): return lax.all_to_all(blocks, axes, 0, 0, tiled=True)]
    all_to_all x3 -> x4, waiting for transfers between devices: 8.64 us -> 37.9 us  [exchange(): return lax.all_to_all(blocks, axes, 0, 0, tiled=True)]
    dot_general x5 -> x0, matrix products: 26.5 us -> none  [the longest x2 12.1 us: back(): v = jnp.dot(u, tile, preferred_element_type=F32)]
    pallas_call x0 -> x8, Pallas kernels: none -> 24.2 us  [the longest x2 10.2 us: build(): pl.pallas_call(functools.partial(build_kernel, gamma, first), grid=grid,...]
    ppermute x0 -> x4, starting transfers between devices: none -> 21.8 us  [other_core(): return lax.ppermute(block, 'core', [(0, 1), (1, 0)])]
    all_to_all x3 -> x4, starting transfers between devices: 24.5 us -> 37.4 us  [exchange(): return lax.all_to_all(blocks, axes, 0, 0, tiled=True)]
    dot_general x1 -> x0, local copies, waits for them, and re-layouts: 12 us -> none  [back(): v = jnp.dot(u, tile, preferred_element_type=F32)]
    unnamed x12 -> x26, local copies, waits for them, and re-layouts: 3.21 us -> 10.7 us
  transfers between devices with their start and end apart: 4 -> 8, of which waited for: 3 -> 4; matrix products, arithmetic and copies ran while one was open for 9% -> 4% of each run, Pallas kernels for 0% -> 4%
where the time goes in v2:
time: 275 us; the launch traced here: 274 us
  blocking collectives  117 us (43%)
  starting transfers between devices  59.2 us (22%)
  waiting for transfers between devices  37.9 us (14%)
  Pallas kernels  24.2 us (9%)
  local copies, waits for them, and re-layouts  14.1 us (5%)
  other arithmetic  14.1 us (5%)
  between operations  6.15 us (2%)
    all_to_all x7, blocking collectives, exchange(): return lax.all_to_all(blocks, axes, 0, 0, tiled=True)  117 us
    all_to_all x4, waiting for transfers between devices, exchange(): return lax.all_to_all(blocks, axes, 0, 0, tiled=True)  37.9 us
    all_to_all x4, starting transfers between devices, exchange(): return lax.all_to_all(blocks, axes, 0, 0, tiled=True)  37.4 us
    ppermute x4, starting transfers between devices, other_core(): return lax.ppermute(block, 'core', [(0, 1), (1, 0)])  21.8 us
    unnamed x26, local copies, waits for them, and re-layouts  10.7 us
    pallas_call x2, Pallas kernels, build(): pl.pallas_call(functools.partial(build_kernel, gamma, first), grid=grid,...  10.2 us
    another operation x2, other arithmetic, precondition(): lax.linalg.triangular_solve(factor, lower, left_side=True, lower=True, tr...  9.82 us
    pallas_call x4, Pallas kernels, back(): pl.pallas_call(functools.partial(back_kernel, count), grid=grid, in_specs...  9.41 us
  transfers between devices with their start and end apart: 8, of which 4 were waited for; matrix products, arithmetic and copies ran while one was open for 4% of the time, Pallas kernels for 4%

profile of v2, /device:TPU:1, one launch (start us, length us, event | category | flops | bytes accessed | tf_op | source)
XLA Modules:
  0.0 273.7 jit_solution(3336463364282806606)
XLA Ops:
  3.3 7.6 %all-to-all-start.1 = ((bf16[16,192,128]{2,1,0:T(8,128)(2,1)}), bf16[16,192,128]{2,1,0:T(8,128)(2,1)S(1)}, u32[]{:S(2)}, u32[]{:S(2)}) async-start(bf16[16,192,128]{2,1,0:T(8,128)(2,1)} %broadcast_in_dim.13), calls=%async_computation.1 | async-start | bytes 1572864 | tf_op jit(solution)/shard_map/all_to_all | solution.py:34
  10.9 11.8 %all-to-all-done.1.blk_ref = bf16[16,192,128]{2,1,0:T(8,128)(2,1)S(1)} async-done(((bf16[16,192,128]{2,1,0:T(8,128)(2,1)}), bf16[16,192,128]{2,1,0:T(8,128)(2,1)S(1)}, u32[]{:S(2)}, u32[]{:S(2)}) %all-to-all-start.1) | async-done | bytes 786464 | tf_op jit(solution)/shard_map/all_to_all | solution.py:34
  23.4 16.3 %all-to-all-start = ((bf16[16,64,128]{2,1,0:T(8,128)(2,1)}), bf16[16,64,128]{2,1,0:T(8,128)(2,1)S(1)}, u32[]{:S(2)}, u32[]{:S(2)}) async-start(bf16[16,64,128]{2,1,0:T(8,128)(2,1)} %broadcast_in_dim.12), calls=%async_computation | async-start | bytes 524288 | tf_op jit(solution)/shard_map/all_to_all | solution.py:34
  39.7 4.5 %collective-permute-start = (bf16[16,192,128]{2,1,0:T(8,128)(2,1)S(1)}, bf16[16,192,128]{2,1,0:T(8,128)(2,1)S(1)}, u32[]{:S(2)}, u32[]{:S(2)}) collective-permute-start(bf16[16,192,128]{2,1,0:T(8,128)(2,1)S(1)} %all-to-all-done.1.blk_ref), channel_id=1, source_target_pairs={{0,16},{16,0},{1,17},{17,1},{2,18},{18,2},{3,19},{19,3},{4,20},{20... | collective-permute-start | bytes 2359304 | tf_op jit(solution)/shard_map/ppermute | solution.py:43
  44.2 8.3 %all-to-all-done = bf16[16,64,128]{2,1,0:T(8,128)(2,1)S(1)} async-done(((bf16[16,64,128]{2,1,0:T(8,128)(2,1)}), bf16[16,64,128]{2,1,0:T(8,128)(2,1)S(1)}, u32[]{:S(2)}, u32[]{:S(2)}) %all-to-all-start) | async-done | bytes 262176 | tf_op jit(solution)/shard_map/all_to_all | solution.py:34
  52.8 4.7 %build_tile.2 = (bf16[2048,1024]{1,0:T(8,128)(2,1)S(1)}, f32[16,32,128]{2,1,0:T(8,128)S(1)}) custom-call(bf16[1024,128]{1,0:T(8,128)(2,1)S(1)} %bitcast.74, f32[1,1024]{1,0:T(1,128)S(1)} %sub.96.gap_ref, bf16[16,192,128]{2,1,0:T(8,128)(2,1)S(1)} %all-to-all-done.1.blk_ref), custom_call_target="tpu_custom_call" | custom-call | flops 805306368 | bytes 4194304 | tf_op jit(solution)/shard_map/build_tile/pallas_call | solution.py:153
  59.5 5.5 %build_tile.3 = (bf16[2048,1024]{1,0:T(8,128)(2,1)S(1)}, f32[16,32,128]{2,1,0:T(8,128)}) custom-call(bf16[1024,128]{1,0:T(8,128)(2,1)S(1)} %bitcast.75, f32[1,1024]{1,0:T(1,128)S(1)} %sub.96.gap_ref, bf16[16,192,128]{2,1,0:T(8,128)(2,1)S(1)} %collective-permute-done.blk_ref, f32[16,32,128]{2,1,0:T(8,128)S(1)} %get-tuple-element.8.rest_0_), custom_call_target="tpu_custom_call" | custom-call | flops 805306368 | bytes 4194304 | tf_op jit(solution)/shard_map/build_tile/pallas_call | solution.py:153
  64.9 2.0 copy-done.5
  66.9 10.0 %all-to-all-start.2 = ((f32[16,32,128]{2,1,0:T(8,128)}), f32[16,32,128]{2,1,0:T(8,128)S(1)}, u32[]{:S(2)}, u32[]{:S(2)}) async-start(f32[16,32,128]{2,1,0:T(8,128)} %get-tuple-element.9), calls=%async_computation.2 | async-start | bytes 524288 | tf_op jit(solution)/shard_map/all_to_all | solution.py:34
  76.9 9.8 %custom-call.9 = f32[1,128,128]{1,2,0:T(8,128)S(1)} custom-call(f32[1,128,128]{2,1,0:T(8,128)S(1)} %select_bitcast_fusion), custom_call_target="InvertDiagBlocksLowerTriangular" | custom-call | tf_op jit(solution)/shard_map/triangular_solve/custom-call.0 | solution.py:30
  87.3 2.3 all-to-all-done.2
  89.8 22.2 %all_to_all.55.u_ref = bf16[16,48,128]{2,1,0:T(8,128)(2,1)S(1)} all-to-all(bf16[16,48,128]{2,1,0:T(8,128)(2,1)S(1)} %broadcast_in_dim.14), channel_id=1, replica_groups=mesh['z'=16,'core'=2,'ctr'=16] {'z'}, dimensions={0} | all-to-all | bytes 393216 | tf_op jit(solution)/shard_map/all_to_all | solution.py:34
  112.0 2.2 copy-done.6
  114.2 2.3 back_tile.5
  116.6 7.3 %collective-permute-start.1 = (f32[16,72,128]{2,1,0:T(8,128)S(1)}, f32[16,72,128]{2,1,0:T(8,128)S(1)}, u32[]{:S(2)}, u32[]{:S(2)}) collective-permute-start(f32[16,72,128]{2,1,0:T(8,128)S(1)} %back_tile.5), channel_id=1, source_target_pairs={{0,16},{16,0},{1,17},{17,1},{2,18},{18,2},{3,19},{19,3},{4,20},{20... | collective-permute-start | bytes 1769480 | tf_op jit(solution)/shard_map/ppermute | solution.py:43
  124.0 2.4 back_tile.4
  126.4 18.1 %all_to_all.56 = f32[16,72,128]{2,1,0:T(8,128)S(1)} all-to-all(f32[16,72,128]{2,1,0:T(8,128)S(1)} %add.43), channel_id=1, replica_groups=mesh['z'=16,'core'=2,'ctr'=16] {'ctr'}, dimensions={0} | all-to-all | bytes 1179648 | tf_op jit(solution)/shard_map/all_to_all | solution.py:34
  147.8 16.0 %all_to_all.57 = f32[16,8,128]{2,1,0:T(8,128)S(1)} all-to-all(f32[16,8,128]{2,1,0:T(8,128)S(1)} %broadcast_in_dim_broadcast_in_dim_broadcast_in_dim.2), channel_id=1, replica_groups=mesh['z'=16,'core'=2,'ctr'=16] {'z'}, dimensions={0} | all-to-all | bytes 131072 | tf_op jit(solution)/shard_map/all_to_all | solution.py:34
  163.8 13.4 %all_to_all.58 = f32[32,8,128]{2,1,0:T(8,128)S(1)} all-to-all(f32[32,8,128]{2,1,0:T(8,128)S(1)} %broadcast_in_dim.15), channel_id=1, replica_groups=mesh['z'=16,'core'=2,'ctr'=16] {'core','ctr'}, dimensions={0} | all-to-all | bytes 262144 | tf_op jit(solution)/shard_map/all_to_all | solution.py:34
  179.2 11.1 %all_to_all.59.blk_ref = bf16[16,64,128]{2,1,0:T(8,128)(2,1)S(1)} all-to-all(bf16[16,64,128]{2,1,0:T(8,128)(2,1)S(1)} %broadcast_in_dim.16), channel_id=1, replica_groups=mesh['z'=16,'core'=2,'ctr'=16] {'ctr'}, dimensions={0} | all-to-all | bytes 524288 | tf_op jit(solution)/shard_map/all_to_all | solution.py:34
  190.2 3.4 %collective-permute-start.2 = (bf16[16,64,128]{2,1,0:T(8,128)(2,1)S(1)}, bf16[16,64,128]{2,1,0:T(8,128)(2,1)S(1)}, u32[]{:S(2)}, u32[]{:S(2)}) collective-permute-start(bf16[16,64,128]{2,1,0:T(8,128)(2,1)S(1)} %all_to_all.59.blk_ref), channel_id=1, source_target_pairs={{0,16},{16,0},{1,17},{17,1},{2,18},{18,2},{3,19},{19,3},{4,20},{20... | collective-permute-start | bytes 786440 | tf_op jit(solution)/shard_map/ppermute | solution.py:43
  193.7 2.2 copy-done.3
  195.9 1.9 apply_tile.2.rest_0_
  198.1 2.7 apply_tile.3
  200.7 3.5 %all-to-all-start.8 = ((f32[16,32,128]{2,1,0:T(8,128)}), f32[16,32,128]{2,1,0:T(8,128)S(1)}, u32[]{:S(2)}, u32[]{:S(2)}) async-start(f32[16,32,128]{2,1,0:T(8,128)} %apply_tile.3), calls=%async_computation.8 | async-start | bytes 524288 | tf_op jit(solution)/shard_map/all_to_all | solution.py:34
  204.3 15.5 %all-to-all-done.8 = f32[16,32,128]{2,1,0:T(8,128)S(1)} async-done(((f32[16,32,128]{2,1,0:T(8,128)}), f32[16,32,128]{2,1,0:T(8,128)S(1)}, u32[]{:S(2)}, u32[]{:S(2)}) %all-to-all-start.8) | async-done | bytes 262176 | tf_op jit(solution)/shard_map/all_to_all | solution.py:34
  219.9 21.3 %all_to_all.60.u_ref = bf16[16,48,128]{2,1,0:T(8,128)(2,1)S(1)} all-to-all(bf16[16,48,128]{2,1,0:T(8,128)(2,1)S(1)} %broadcast_in_dim.17), channel_id=1, replica_groups=mesh['z'=16,'core'=2,'ctr'=16] {'z'}, dimensions={0} | all-to-all | bytes 393216 | tf_op jit(solution)/shard_map/all_to_all | solution.py:34
  241.3 2.2 copy-done.8
  243.5 2.3 back_tile.7
  245.8 6.6 %collective-permute-start.3 = (f32[16,72,128]{2,1,0:T(8,128)S(1)}, f32[16,72,128]{2,1,0:T(8,128)S(1)}, u32[]{:S(2)}, u32[]{:S(2)}) collective-permute-start(f32[16,72,128]{2,1,0:T(8,128)S(1)} %back_tile.7), channel_id=1, source_target_pairs={{0,16},{16,0},{1,17},{17,1},{2,18},{18,2},{3,19},{19,3},{4,20},{20... | collective-permute-start | bytes 1769480 | tf_op jit(solution)/shard_map/ppermute | solution.py:43
  252.4 2.4 back_tile.6
  254.9 14.7 %all_to_all.61 = f32[16,72,128]{2,1,0:T(8,128)S(1)} all-to-all(f32[16,72,128]{2,1,0:T(8,128)S(1)} %add.48), channel_id=1, replica_groups=mesh['z'=16,'core'=2,'ctr'=16] {'ctr'}, dimensions={0} | all-to-all | bytes 1179648 | tf_op jit(solution)/shard_map/all_to_all | solution.py:34
  (71 shorter events, 11.0 us)
Async XLA Ops:
  0.6 10.3 %copy-start = (bf16[1024,128]{1,0:T(8,128)(2,1)S(1)}, bf16[1024,128]{1,0:T(8,128)(2,1)}, u32[]{:S(2)}) copy-start(bf16[1024,128]{1,0:T(8,128)(2,1)} %param.10) | copy-start | bytes 786436
  3.3 19.4 %all-to-all-start.1 = ((bf16[16,192,128]{2,1,0:T(8,128)(2,1)}), bf16[16,192,128]{2,1,0:T(8,128)(2,1)S(1)}, u32[]{:S(2)}, u32[]{:S(2)}) async-start(bf16[16,192,128]{2,1,0:T(8,128)(2,1)} %broadcast_in_dim.13), calls=%async_computation.1 | async-start | bytes 1572864 | tf_op jit(solution)/shard_map/all_to_all | solution.py:34
  23.4 29.1 %all-to-all-start = ((bf16[16,64,128]{2,1,0:T(8,128)(2,1)}), bf16[16,64,128]{2,1,0:T(8,128)(2,1)S(1)}, u32[]{:S(2)}, u32[]{:S(2)}) async-start(bf16[16,64,128]{2,1,0:T(8,128)(2,1)} %broadcast_in_dim.12), calls=%async_computation | async-start | bytes 524288 | tf_op jit(solution)/shard_map/all_to_all | solution.py:34
  39.7 19.7 %collective-permute-start = (bf16[16,192,128]{2,1,0:T(8,128)(2,1)S(1)}, bf16[16,192,128]{2,1,0:T(8,128)(2,1)S(1)}, u32[]{:S(2)}, u32[]{:S(2)}) collective-permute-start(bf16[16,192,128]{2,1,0:T(8,128)(2,1)S(1)} %all-to-all-done.1.blk_ref), channel_id=1, source_target_pairs={{0,16},{16,0},{1,17},{17,1},{2,18},{18,2},{3,19},{19,3},{4,20},{20... | collective-permute-start | bytes 2359304 | tf_op jit(solution)/shard_map/ppermute | solution.py:43
  52.8 24.1 %copy-start.11 = (f32[128,128]{1,0:T(8,128)S(1)}, f32[128,128]{1,0:T(8,128)}, u32[]{:S(2)}) copy-start(f32[128,128]{1,0:T(8,128)} %param.12) | copy-start | bytes 196612
  52.8 33.9 %copy-start.10 = (f32[128,64]{0,1:T(8,128)S(1)}, f32[128,64]{0,1:T(8,128)}, u32[]{:S(2)}) copy-start(f32[128,64]{0,1:T(8,128)} %param.14) | copy-start | bytes 98308
  57.5 1.9 copy-start.1
  64.9 2.0 copy-start.5
  66.9 22.8 %all-to-all-start.2 = ((f32[16,32,128]{2,1,0:T(8,128)}), f32[16,32,128]{2,1,0:T(8,128)S(1)}, u32[]{:S(2)}, u32[]{:S(2)}) async-start(f32[16,32,128]{2,1,0:T(8,128)} %get-tuple-element.9), calls=%async_computation.2 | async-start | bytes 524288 | tf_op jit(solution)/shard_map/all_to_all | solution.py:34
  89.8 34.2 %copy-start.2 = (bf16[2048,1024]{1,0:T(8,128)(2,1)S(1)}, bf16[2048,1024]{1,0:T(8,128)(2,1)}, u32[]{:S(2)}) copy-start(bf16[2048,1024]{1,0:T(8,128)(2,1)} %copy-done.1) | copy-start | bytes 12582916
  112.0 2.2 copy-start.6
  116.6 9.8 %collective-permute-start.1 = (f32[16,72,128]{2,1,0:T(8,128)S(1)}, f32[16,72,128]{2,1,0:T(8,128)S(1)}, u32[]{:S(2)}, u32[]{:S(2)}) collective-permute-start(f32[16,72,128]{2,1,0:T(8,128)S(1)} %back_tile.5), channel_id=1, source_target_pairs={{0,16},{16,0},{1,17},{17,1},{2,18},{18,2},{3,19},{19,3},{4,20},{20... | collective-permute-start | bytes 1769480 | tf_op jit(solution)/shard_map/ppermute | solution.py:43
  123.9 23.2 %copy-start.9 = (f32[128,64]{0,1:T(8,128)S(1)}, f32[128,64]{0,1:T(8,128)}, u32[]{:S(2)}) copy-start(f32[128,64]{0,1:T(8,128)} %param.15) | copy-start | bytes 98308
  190.2 7.6 %collective-permute-start.2 = (bf16[16,64,128]{2,1,0:T(8,128)(2,1)S(1)}, bf16[16,64,128]{2,1,0:T(8,128)(2,1)S(1)}, u32[]{:S(2)}, u32[]{:S(2)}) collective-permute-start(bf16[16,64,128]{2,1,0:T(8,128)(2,1)S(1)} %all_to_all.59.blk_ref), channel_id=1, source_target_pairs={{0,16},{16,0},{1,17},{17,1},{2,18},{18,2},{3,19},{19,3},{4,20},{20... | collective-permute-start | bytes 786440 | tf_op jit(solution)/shard_map/ppermute | solution.py:43
  193.7 2.2 copy-start.3
  195.9 2.2 copy-start.7
  200.7 19.1 %all-to-all-start.8 = ((f32[16,32,128]{2,1,0:T(8,128)}), f32[16,32,128]{2,1,0:T(8,128)S(1)}, u32[]{:S(2)}, u32[]{:S(2)}) async-start(f32[16,32,128]{2,1,0:T(8,128)} %apply_tile.3), calls=%async_computation.8 | async-start | bytes 524288 | tf_op jit(solution)/shard_map/all_to_all | solution.py:34
  219.9 32.5 %copy-start.4 = (bf16[2048,1024]{1,0:T(8,128)(2,1)S(1)}, bf16[2048,1024]{1,0:T(8,128)(2,1)}, u32[]{:S(2)}) copy-start(bf16[2048,1024]{1,0:T(8,128)(2,1)} %copy-done.1) | copy-start | bytes 12582916
  241.3 2.2 copy-start.8
  245.8 27.2 %copy-start.12 = (f32[128,64]{0,1:T(8,128)S(1)}, f32[128,64]{0,1:T(8,128)}, u32[]{:S(2)}) copy-start(f32[128,64]{0,1:T(8,128)} %param.13) | copy-start | bytes 98308
  245.8 9.0 %collective-permute-start.3 = (f32[16,72,128]{2,1,0:T(8,128)S(1)}, f32[16,72,128]{2,1,0:T(8,128)S(1)}, u32[]{:S(2)}, u32[]{:S(2)}) collective-permute-start(f32[16,72,128]{2,1,0:T(8,128)S(1)} %back_tile.7), channel_id=1, source_target_pairs={{0,16},{16,0},{1,17},{17,1},{2,18},{18,2},{3,19},{19,3},{4,20},{20... | collective-permute-start | bytes 1769480 | tf_op jit(solution)/shard_map/ppermute | solution.py:43

commit v3 on v2

--- a/solution.py
+++ b/solution.py
@@ -17,7 +17,7 @@
 RIDE = 8
 BF = jnp.bfloat16
 F32 = jnp.float32
-PARAMS = pltpu.CompilerParams(vmem_limit_bytes=40 * 1024 * 1024)
+PARAMS = pltpu.CompilerParams(vmem_limit_bytes=60 * 1024 * 1024)
 
 
 def row_gaps(rows):
@@ -115,7 +115,7 @@
             low = (at % 2) * half
             ub[low : low + half, (at // 2) * LANES : (at // 2 + 1) * LANES] = piece
             squares += piece.astype(F32) * piece.astype(F32)
-        packed = jnp.sum(u_ref[:, half:].astype(F32), axis=0)
+        packed = jnp.sum(u_ref[:, half:].astype(F32), axis=0) if count else None
         rows = [packed[3 * k : 3 * k + 1] + packed[3 * k + 1 : 3 * k + 2] + packed[3 * k + 2 : 3 * k + 3] for k in range(count)]
         rows.append(jnp.sum(squares, axis=0, keepdims=True))
         rows.append(jnp.zeros((RIDE - count - 1, LANES), F32))
@@ -192,7 +192,7 @@
 
     def reduce_points(u, rows):
         u = jnp.sum(exchange(u, "z"), axis=0).astype(BF)
-        return spread(jnp.concatenate([u, pack(rows)], 0), "z")
+        return spread(jnp.concatenate([u, pack(rows)], 0) if rows else u, "z")
 
     def reduce_centres(u, tile, tile_other, count):
         v = other_core(back(u, tile_other, count))
@@ -220,20 +220,22 @@
     alpha0 = rz0 / (s[2] / total_points + RIDGE * s[1])
     r1 = residual.T - alpha0 * q0
     z1 = precondition(factor, r1.T).T
-    block = jnp.broadcast_to(lanes(r1, z1)[None], (RIDE, LANES))
+    block = jnp.stack([lanes(r1, z1), lanes(z1, z1), lanes(z1, p0)] + [jnp.zeros((LANES,), F32)] * (RIDE - 3))
     for axes in ("z", ("core", "ctr")):
         block = jnp.sum(spread(block, axes), axis=0)
-    rz1 = jnp.sum(block[0])
-    p1 = z1 + rz1 / rz0 * p0
+    rz1, zz, zp = [jnp.sum(block[k]) for k in range(3)]
+    beta = rz1 / rz0
+    p1 = z1 + beta * p0
+    pp = zz + beta * (2.0 * zp + beta * s[1])
 
     own = spread(p1.astype(BF), "ctr")
     other = other_core(own)
     u1 = apply(own, tile, None)
     u1 = apply(other, tile_other, u1)
-    u1 = reduce_points(u1, [lanes(p1, p1)])
-    v1, s = reduce_centres(u1, tile, tile_other, 1)
+    u1 = reduce_points(u1, [])
+    v1, s = reduce_centres(u1, tile, tile_other, 0)
     q1 = v1 + RIDGE * p1
-    alpha1 = rz1 / (s[1] / total_points + RIDGE * s[0])
+    alpha1 = rz1 / (s[0] / total_points + RIDGE * pp)
     x2 = solution + (alpha0 * p0 + alpha1 * p1).T
     r2 = (r1 - alpha1 * q1).T
     return x2, r2

time: 275 us -> 301 us (1.095)
  Pallas kernels: 24.2 us -> 56.4 us
  local copies, waits for them, and re-layouts: 14.1 us -> 4.98 us
  waiting for transfers between devices: 37.9 us -> 32.6 us
  other arithmetic: 14.1 us -> 17.5 us
    pallas_call x4, Pallas kernels: 9.41 us -> 27.3 us  [back(): pl.pallas_call(functools.partial(back_kernel, count), grid=grid, in_specs...]
    unnamed x26 -> x20, local copies, waits for them, and re-layouts: 10.7 us -> 1.67 us
    pallas_call x2, Pallas kernels: 4.6 us -> 12.7 us  [apply(): pl.pallas_call(functools.partial(apply_kernel, first), grid=grid, in_spec...]
    pallas_call x2, Pallas kernels: 10.2 us -> 16.4 us  [build(): pl.pallas_call(functools.partial(build_kernel, gamma, first), grid=grid,...]
    all_to_all x4, waiting for transfers between devices: 37.9 us -> 32.5 us  [exchange(): return lax.all_to_all(blocks, axes, 0, 0, tiled=True)]
    all_to_all x7, blocking collectives: 117 us -> 120 us  [exchange(): return lax.all_to_all(blocks, axes, 0, 0, tiled=True)]
  transfers between devices with their start and end apart: 8 -> 8, of which waited for: 4 -> 4; matrix products, arithmetic and copies ran while one was open for 4% -> 4% of each run, Pallas kernels for 4% -> 9%
where the time goes in v3:
time: 301 us; the launch traced here: 298 us
  blocking collectives  120 us (40%)
  starting transfers between devices  58.1 us (19%)
  Pallas kernels  56.4 us (19%)
  waiting for transfers between devices  32.6 us (11%)
  other arithmetic  17.5 us (6%)
  between operations  7.12 us (2%)
  local copies, waits for them, and re-layouts  4.98 us (2%)
    all_to_all x7, blocking collectives, exchange(): return lax.all_to_all(blocks, axes, 0, 0, tiled=True)  120 us
    all_to_all x4, starting transfers between devices, exchange(): return lax.all_to_all(blocks, axes, 0, 0, tiled=True)  37.4 us
    all_to_all x4, waiting for transfers between devices, exchange(): return lax.all_to_all(blocks, axes, 0, 0, tiled=True)  32.5 us
    pallas_call x4, Pallas kernels, back(): pl.pallas_call(functools.partial(back_kernel, count), grid=grid, in_specs...  27.3 us
    ppermute x4, starting transfers between devices, other_core(): return lax.ppermute(block, 'core', [(0, 1), (1, 0)])  20.7 us
    pallas_call x2, Pallas kernels, build(): pl.pallas_call(functools.partial(build_kernel, gamma, first), grid=grid,...  16.4 us
    pallas_call x2, Pallas kernels, apply(): pl.pallas_call(functools.partial(apply_kernel, first), grid=grid, in_spec...  12.7 us
    another operation x2, other arithmetic, precondition(): lax.linalg.triangular_solve(factor, lower, left_side=True, lower=True, tr...  9.82 us
  transfers between devices with their start and end apart: 8, of which 4 were waited for; matrix products, arithmetic and copies ran while one was open for 4% of the time, Pallas kernels for 9%

profile of v3, /device:TPU:1, one launch (start us, length us, event | category | flops | bytes accessed | tf_op | source)
XLA Modules:
  0.0 298.2 jit_solution(5771346543666138991)
XLA Ops:
  2.2 1.0 broadcast_in_dim.15
  3.2 7.6 %all-to-all-start.1 = ((bf16[16,192,128]{2,1,0:T(8,128)(2,1)}), bf16[16,192,128]{2,1,0:T(8,128)(2,1)S(1)}, u32[]{:S(2)}, u32[]{:S(2)}) async-start(bf16[16,192,128]{2,1,0:T(8,128)(2,1)} %broadcast_in_dim.15), calls=%async_computation.1 | async-start | bytes 1572864 | tf_op jit(solution)/shard_map/all_to_all | solution.py:34
  10.9 11.8 %all-to-all-done.1.blk_ref = bf16[16,192,128]{2,1,0:T(8,128)(2,1)S(1)} async-done(((bf16[16,192,128]{2,1,0:T(8,128)(2,1)}), bf16[16,192,128]{2,1,0:T(8,128)(2,1)S(1)}, u32[]{:S(2)}, u32[]{:S(2)}) %all-to-all-start.1) | async-done | bytes 786464 | tf_op jit(solution)/shard_map/all_to_all | solution.py:34
  23.5 16.3 %all-to-all-start = ((bf16[16,64,128]{2,1,0:T(8,128)(2,1)}), bf16[16,64,128]{2,1,0:T(8,128)(2,1)S(1)}, u32[]{:S(2)}, u32[]{:S(2)}) async-start(bf16[16,64,128]{2,1,0:T(8,128)(2,1)} %broadcast_in_dim.14), calls=%async_computation | async-start | bytes 524288 | tf_op jit(solution)/shard_map/all_to_all | solution.py:34
  39.7 4.5 %collective-permute-start = (bf16[16,192,128]{2,1,0:T(8,128)(2,1)S(1)}, bf16[16,192,128]{2,1,0:T(8,128)(2,1)S(1)}, u32[]{:S(2)}, u32[]{:S(2)}) collective-permute-start(bf16[16,192,128]{2,1,0:T(8,128)(2,1)S(1)} %all-to-all-done.1.blk_ref), channel_id=1, source_target_pairs={{0,16},{16,0},{1,17},{17,1},{2,18},{18,2},{3,19},{19,3},{4,20},{20... | collective-permute-start | bytes 2359304 | tf_op jit(solution)/shard_map/ppermute | solution.py:43
  44.2 8.3 %all-to-all-done = bf16[16,64,128]{2,1,0:T(8,128)(2,1)S(1)} async-done(((bf16[16,64,128]{2,1,0:T(8,128)(2,1)}), bf16[16,64,128]{2,1,0:T(8,128)(2,1)S(1)}, u32[]{:S(2)}, u32[]{:S(2)}) %all-to-all-start) | async-done | bytes 262176 | tf_op jit(solution)/shard_map/all_to_all | solution.py:34
  53.4 8.2 %build_tile.2 = (bf16[2048,1024]{1,0:T(8,128)(2,1)}, f32[16,32,128]{2,1,0:T(8,128)}) custom-call(bf16[1024,128]{1,0:T(8,128)(2,1)} %bitcast.88, f32[1,1024]{1,0:T(1,128)} %sub.72.gap_ref, bf16[16,192,128]{2,1,0:T(8,128)(2,1)} %copy-done.4), custom_call_target="tpu_custom_call" | custom-call | flops 805306368 | bytes 4194304 | tf_op jit(solution)/shard_map/build_tile/pallas_call | solution.py:153
  61.6 0.9 copy-done.9
  62.5 8.3 %build_tile.3 = (bf16[2048,1024]{1,0:T(8,128)(2,1)}, f32[16,32,128]{2,1,0:T(8,128)}) custom-call(bf16[1024,128]{1,0:T(8,128)(2,1)} %bitcast.89, f32[1,1024]{1,0:T(1,128)} %sub.72.gap_ref, bf16[16,192,128]{2,1,0:T(8,128)(2,1)} %copy-done.9, f32[16,32,128]{2,1,0:T(8,128)} %get-tuple-element.8.rest_0_), custom_call_target="tpu_custom_call" | custom-call | flops 805306368 | bytes 4194304 | tf_op jit(solution)/shard_map/build_tile/pallas_call | solution.py:153
  70.8 10.0 %all-to-all-start.2 = ((f32[16,32,128]{2,1,0:T(8,128)}), f32[16,32,128]{2,1,0:T(8,128)S(1)}, u32[]{:S(2)}, u32[]{:S(2)}) async-start(f32[16,32,128]{2,1,0:T(8,128)} %get-tuple-element.9), calls=%async_computation.2 | async-start | bytes 524288 | tf_op jit(solution)/shard_map/all_to_all | solution.py:34
  80.8 9.8 %custom-call.9 = f32[1,128,128]{1,2,0:T(8,128)S(1)} custom-call(f32[1,128,128]{2,1,0:T(8,128)S(1)} %select_bitcast_fusion), custom_call_target="InvertDiagBlocksLowerTriangular" | custom-call | tf_op jit(solution)/shard_map/triangular_solve/custom-call.0 | solution.py:30
  91.3 2.3 all-to-all-done.2
  93.7 22.1 %all_to_all.55.u_ref = bf16[16,48,128]{2,1,0:T(8,128)(2,1)} all-to-all(bf16[16,48,128]{2,1,0:T(8,128)(2,1)S(1)} %broadcast_in_dim.16), channel_id=1, replica_groups=mesh['z'=16,'core'=2,'ctr'=16] {'z'}, dimensions={0} | all-to-all | bytes 393216 | tf_op jit(solution)/shard_map/all_to_all | solution.py:34
  115.8 6.8 %back_tile.5 = f32[16,72,128]{2,1,0:T(8,128)} custom-call(bf16[16,48,128]{2,1,0:T(8,128)(2,1)} %all_to_all.55.u_ref, bf16[2048,1024]{1,0:T(8,128)(2,1)} %get-tuple-element.11.tile_ref), custom_call_target="tpu_custom_call" | custom-call | flops 268435456 | bytes 4194304 | tf_op jit(solution)/shard_map/back_tile/pallas_call | solution.py:181
  122.6 7.3 %collective-permute-start.1 = (f32[16,72,128]{2,1,0:T(8,128)}, f32[16,72,128]{2,1,0:T(8,128)S(1)}, u32[]{:S(2)}, u32[]{:S(2)}) collective-permute-start(f32[16,72,128]{2,1,0:T(8,128)} %back_tile.5), channel_id=1, source_target_pairs={{0,16},{16,0},{1,17},{17,1},{2,18},{18,2},{3,19},{19,3},{4,20},{20... | collective-permute-start | bytes 1769480 | tf_op jit(solution)/shard_map/ppermute | solution.py:43
  130.0 6.9 %back_tile.4 = f32[16,72,128]{2,1,0:T(8,128)} custom-call(bf16[16,48,128]{2,1,0:T(8,128)(2,1)} %all_to_all.55.u_ref, bf16[2048,1024]{1,0:T(8,128)(2,1)} %get-tuple-element.10.tile_ref), custom_call_target="tpu_custom_call" | custom-call | flops 268435456 | bytes 4194304 | tf_op jit(solution)/shard_map/back_tile/pallas_call | solution.py:181
  136.8 1.1 add.43
  137.9 18.1 %all_to_all.56 = f32[16,72,128]{2,1,0:T(8,128)S(1)} all-to-all(f32[16,72,128]{2,1,0:T(8,128)S(1)} %add.43), channel_id=1, replica_groups=mesh['z'=16,'core'=2,'ctr'=16] {'ctr'}, dimensions={0} | all-to-all | bytes 1179648 | tf_op jit(solution)/shard_map/all_to_all | solution.py:34
  159.3 16.0 %all_to_all.57 = f32[16,8,128]{2,1,0:T(8,128)S(1)} all-to-all(f32[16,8,128]{2,1,0:T(8,128)S(1)} %broadcast_in_dim.17), channel_id=1, replica_groups=mesh['z'=16,'core'=2,'ctr'=16] {'z'}, dimensions={0} | all-to-all | bytes 131072 | tf_op jit(solution)/shard_map/all_to_all | solution.py:34
  175.4 13.4 %all_to_all.58 = f32[32,8,128]{2,1,0:T(8,128)S(1)} all-to-all(f32[32,8,128]{2,1,0:T(8,128)S(1)} %broadcast_in_dim.18), channel_id=1, replica_groups=mesh['z'=16,'core'=2,'ctr'=16] {'core','ctr'}, dimensions={0} | all-to-all | bytes 262144 | tf_op jit(solution)/shard_map/all_to_all | solution.py:34
  190.7 11.1 %all_to_all.59.blk_ref = bf16[16,64,128]{2,1,0:T(8,128)(2,1)S(1)} all-to-all(bf16[16,64,128]{2,1,0:T(8,128)(2,1)S(1)} %broadcast_in_dim.19), channel_id=1, replica_groups=mesh['z'=16,'core'=2,'ctr'=16] {'ctr'}, dimensions={0} | all-to-all | bytes 524288 | tf_op jit(solution)/shard_map/all_to_all | solution.py:34
  201.8 3.4 %collective-permute-start.2 = (bf16[16,64,128]{2,1,0:T(8,128)(2,1)S(1)}, bf16[16,64,128]{2,1,0:T(8,128)(2,1)S(1)}, u32[]{:S(2)}, u32[]{:S(2)}) collective-permute-start(bf16[16,64,128]{2,1,0:T(8,128)(2,1)S(1)} %all_to_all.59.blk_ref), channel_id=1, source_target_pairs={{0,16},{16,0},{1,17},{17,1},{2,18},{18,2},{3,19},{19,3},{4,20},{20... | collective-permute-start | bytes 786440 | tf_op jit(solution)/shard_map/ppermute | solution.py:43
  205.2 6.3 %apply_tile.2.rest_0_ = f32[16,32,128]{2,1,0:T(8,128)} custom-call(bf16[16,64,128]{2,1,0:T(8,128)(2,1)} %copy-done.2, bf16[2048,1024]{1,0:T(8,128)(2,1)} %get-tuple-element.10.tile_ref), custom_call_target="tpu_custom_call" | custom-call | flops 268435456 | bytes 4194304 | tf_op jit(solution)/shard_map/apply_tile/pallas_call | solution.py:168
  212.2 6.4 %apply_tile.3 = f32[16,32,128]{2,1,0:T(8,128)} custom-call(bf16[16,64,128]{2,1,0:T(8,128)(2,1)} %copy-done.6, bf16[2048,1024]{1,0:T(8,128)(2,1)} %get-tuple-element.11.tile_ref, f32[16,32,128]{2,1,0:T(8,128)} %apply_tile.2.rest_0_), custom_call_target="tpu_custom_call" | custom-call | flops 268435456 | bytes 4194304 | tf_op jit(solution)/shard_map/apply_tile/pallas_call | solution.py:168
  218.6 19.1 %all_to_all.60 = f32[16,32,128]{2,1,0:T(8,128)S(1)} all-to-all(f32[16,32,128]{2,1,0:T(8,128)} %apply_tile.3), channel_id=1, replica_groups=mesh['z'=16,'core'=2,'ctr'=16] {'z'}, dimensions={0} | all-to-all | bytes 524288 | tf_op jit(solution)/shard_map/all_to_all | solution.py:34
  237.7 20.7 %all_to_all.61.u_ref = bf16[16,32,128]{2,1,0:T(8,128)(2,1)} all-to-all(bf16[16,32,128]{2,1,0:T(8,128)(2,1)S(1)} %broadcast_in_dim.20), channel_id=1, replica_groups=mesh['z'=16,'core'=2,'ctr'=16] {'z'}, dimensions={0} | all-to-all | bytes 262144 | tf_op jit(solution)/shard_map/all_to_all | solution.py:34
  258.4 6.8 %back_tile.7 = f32[16,72,128]{2,1,0:T(8,128)} custom-call(bf16[16,32,128]{2,1,0:T(8,128)(2,1)} %all_to_all.61.u_ref, bf16[2048,1024]{1,0:T(8,128)(2,1)} %get-tuple-element.11.tile_ref), custom_call_target="tpu_custom_call" | custom-call | flops 268435456 | bytes 4194304 | tf_op jit(solution)/shard_map/back_tile/pallas_call | solution.py:181
  265.2 5.4 %collective-permute-start.3 = (f32[16,72,128]{2,1,0:T(8,128)}, f32[16,72,128]{2,1,0:T(8,128)S(1)}, u32[]{:S(2)}, u32[]{:S(2)}) collective-permute-start(f32[16,72,128]{2,1,0:T(8,128)} %back_tile.7), channel_id=1, source_target_pairs={{0,16},{16,0},{1,17},{17,1},{2,18},{18,2},{3,19},{19,3},{4,20},{20... | collective-permute-start | bytes 1769480 | tf_op jit(solution)/shard_map/ppermute | solution.py:43
  270.6 6.8 %back_tile.6 = f32[16,72,128]{2,1,0:T(8,128)} custom-call(bf16[16,32,128]{2,1,0:T(8,128)(2,1)} %all_to_all.61.u_ref, bf16[2048,1024]{1,0:T(8,128)(2,1)} %get-tuple-element.10.tile_ref), custom_call_target="tpu_custom_call" | custom-call | flops 268435456 | bytes 4194304 | tf_op jit(solution)/shard_map/back_tile/pallas_call | solution.py:181
  277.4 1.9 add.47
  279.4 3.6 %all-to-all-start.10 = ((f32[16,72,128]{2,1,0:T(8,128)}), f32[16,72,128]{2,1,0:T(8,128)S(1)}, u32[]{:S(2)}, u32[]{:S(2)}) async-start(f32[16,72,128]{2,1,0:T(8,128)} %add.47), calls=%async_computation.10 | async-start | bytes 1179648 | tf_op jit(solution)/shard_map/all_to_all | solution.py:34
  284.9 10.2 %all-to-all-done.10 = f32[16,72,128]{2,1,0:T(8,128)S(1)} async-done(((f32[16,72,128]{2,1,0:T(8,128)}), f32[16,72,128]{2,1,0:T(8,128)S(1)}, u32[]{:S(2)}, u32[]{:S(2)}) %all-to-all-start.10) | async-done | bytes 589856 | tf_op jit(solution)/shard_map/all_to_all | solution.py:34
  (63 shorter events, 8.8 us)
Async XLA Ops:
  0.6 10.2 %copy-start = (bf16[1024,128]{1,0:T(8,128)(2,1)S(1)}, bf16[1024,128]{1,0:T(8,128)(2,1)}, u32[]{:S(2)}) copy-start(bf16[1024,128]{1,0:T(8,128)(2,1)} %param.10) | copy-start | bytes 786436
  3.2 19.4 %all-to-all-start.1 = ((bf16[16,192,128]{2,1,0:T(8,128)(2,1)}), bf16[16,192,128]{2,1,0:T(8,128)(2,1)S(1)}, u32[]{:S(2)}, u32[]{:S(2)}) async-start(bf16[16,192,128]{2,1,0:T(8,128)(2,1)} %broadcast_in_dim.15), calls=%async_computation.1 | async-start | bytes 1572864 | tf_op jit(solution)/shard_map/all_to_all | solution.py:34
  22.6 30.8 %copy-start.4 = (bf16[16,192,128]{2,1,0:T(8,128)(2,1)}, bf16[16,192,128]{2,1,0:T(8,128)(2,1)S(1)}, u32[]{:S(2)}) copy-start(bf16[16,192,128]{2,1,0:T(8,128)(2,1)S(1)} %all-to-all-done.1.blk_ref) | copy-start | bytes 2359300
  23.5 29.1 %all-to-all-start = ((bf16[16,64,128]{2,1,0:T(8,128)(2,1)}), bf16[16,64,128]{2,1,0:T(8,128)(2,1)S(1)}, u32[]{:S(2)}, u32[]{:S(2)}) async-start(bf16[16,64,128]{2,1,0:T(8,128)(2,1)} %broadcast_in_dim.14), calls=%async_computation | async-start | bytes 524288 | tf_op jit(solution)/shard_map/all_to_all | solution.py:34
  39.7 21.9 %collective-permute-start = (bf16[16,192,128]{2,1,0:T(8,128)(2,1)S(1)}, bf16[16,192,128]{2,1,0:T(8,128)(2,1)S(1)}, u32[]{:S(2)}, u32[]{:S(2)}) collective-permute-start(bf16[16,192,128]{2,1,0:T(8,128)(2,1)S(1)} %all-to-all-done.1.blk_ref), channel_id=1, source_target_pairs={{0,16},{16,0},{1,17},{17,1},{2,18},{18,2},{3,19},{19,3},{4,20},{20... | collective-permute-start | bytes 2359304 | tf_op jit(solution)/shard_map/ppermute | solution.py:43
  52.5 0.9 copy-start.3
  53.4 27.4 %copy-start.7 = (f32[128,128]{1,0:T(8,128)S(1)}, f32[128,128]{1,0:T(8,128)}, u32[]{:S(2)}) copy-start(f32[128,128]{1,0:T(8,128)} %param.12) | copy-start | bytes 196612
  53.4 37.2 %copy-start.1 = (f32[128,64]{0,1:T(8,128)S(1)}, f32[128,64]{0,1:T(8,128)}, u32[]{:S(2)}) copy-start(f32[128,64]{0,1:T(8,128)} %param.15) | copy-start | bytes 98308
  53.4 37.2 %copy-start.5 = (f32[128,64]{0,1:T(8,128)S(1)}, f32[128,64]{0,1:T(8,128)}, u32[]{:S(2)}) copy-start(f32[128,64]{0,1:T(8,128)} %param.14) | copy-start | bytes 98308
  61.6 0.9 copy-start.9
  70.8 22.8 %all-to-all-start.2 = ((f32[16,32,128]{2,1,0:T(8,128)}), f32[16,32,128]{2,1,0:T(8,128)S(1)}, u32[]{:S(2)}, u32[]{:S(2)}) async-start(f32[16,32,128]{2,1,0:T(8,128)} %get-tuple-element.9), calls=%async_computation.2 | async-start | bytes 524288 | tf_op jit(solution)/shard_map/all_to_all | solution.py:34
  122.6 14.2 %collective-permute-start.1 = (f32[16,72,128]{2,1,0:T(8,128)}, f32[16,72,128]{2,1,0:T(8,128)S(1)}, u32[]{:S(2)}, u32[]{:S(2)}) collective-permute-start(f32[16,72,128]{2,1,0:T(8,128)} %back_tile.5), channel_id=1, source_target_pairs={{0,16},{16,0},{1,17},{17,1},{2,18},{18,2},{3,19},{19,3},{4,20},{20... | collective-permute-start | bytes 1769480 | tf_op jit(solution)/shard_map/ppermute | solution.py:43
  201.7 3.5 %copy-start.2 = (bf16[16,64,128]{2,1,0:T(8,128)(2,1)}, bf16[16,64,128]{2,1,0:T(8,128)(2,1)S(1)}, u32[]{:S(2)}) copy-start(bf16[16,64,128]{2,1,0:T(8,128)(2,1)S(1)} %all_to_all.59.blk_ref) | copy-start | bytes 786436
  201.8 9.8 %collective-permute-start.2 = (bf16[16,64,128]{2,1,0:T(8,128)(2,1)S(1)}, bf16[16,64,128]{2,1,0:T(8,128)(2,1)S(1)}, u32[]{:S(2)}, u32[]{:S(2)}) collective-permute-start(bf16[16,64,128]{2,1,0:T(8,128)(2,1)S(1)} %all_to_all.59.blk_ref), channel_id=1, source_target_pairs={{0,16},{16,0},{1,17},{17,1},{2,18},{18,2},{3,19},{19,3},{4,20},{20... | collective-permute-start | bytes 786440 | tf_op jit(solution)/shard_map/ppermute | solution.py:43
  211.5 0.7 copy-start.6
  265.2 32.4 %copy-start.8 = (f32[128,64]{0,1:T(8,128)S(1)}, f32[128,64]{0,1:T(8,128)}, u32[]{:S(2)}) copy-start(f32[128,64]{0,1:T(8,128)} %param.13) | copy-start | bytes 98308
  265.2 12.3 %collective-permute-start.3 = (f32[16,72,128]{2,1,0:T(8,128)}, f32[16,72,128]{2,1,0:T(8,128)S(1)}, u32[]{:S(2)}, u32[]{:S(2)}) collective-permute-start(f32[16,72,128]{2,1,0:T(8,128)} %back_tile.7), channel_id=1, source_target_pairs={{0,16},{16,0},{1,17},{17,1},{2,18},{18,2},{3,19},{19,3},{4,20},{20... | collective-permute-start | bytes 1769480 | tf_op jit(solution)/shard_map/ppermute | solution.py:43
  279.4 15.7 %all-to-all-start.10 = ((f32[16,72,128]{2,1,0:T(8,128)}), f32[16,72,128]{2,1,0:T(8,128)S(1)}, u32[]{:S(2)}, u32[]{:S(2)}) async-start(f32[16,72,128]{2,1,0:T(8,128)} %add.47), calls=%async_computation.10 | async-start | bytes 1179648 | tf_op jit(solution)/shard_map/all_to_all | solution.py:34

commit v4 on v3

--- a/solution.py
+++ b/solution.py
@@ -17,7 +17,7 @@
 RIDE = 8
 BF = jnp.bfloat16
 F32 = jnp.float32
-PARAMS = pltpu.CompilerParams(vmem_limit_bytes=60 * 1024 * 1024)
+PARAMS = pltpu.CompilerParams(vmem_limit_bytes=16 * 1024 * 1024)
 
 
 def row_gaps(rows):

time: 301 us -> 272 us (0.904)
  Pallas kernels: 56.4 us -> 23.5 us
  local copies, waits for them, and re-layouts: 4.98 us -> 13.4 us
    pallas_call x4, Pallas kernels: 27.3 us -> 9.39 us  [back(): pl.pallas_call(functools.partial(back_kernel, count), grid=grid, in_specs...]
    unnamed x20 -> x26, local copies, waits for them, and re-layouts: 1.67 us -> 10.7 us
    pallas_call x2, Pallas kernels: 12.7 us -> 3.88 us  [apply(): pl.pallas_call(functools.partial(apply_kernel, first), grid=grid, in_spec...]
    pallas_call x2, Pallas kernels: 16.4 us -> 10.2 us  [build(): pl.pallas_call(functools.partial(build_kernel, gamma, first), grid=grid,...]
  transfers between devices with their start and end apart: 8 -> 8, of which waited for: 4 -> 4; matrix products, arithmetic and copies ran while one was open for 4% -> 4% of each run, Pallas kernels for 9% -> 4%
where the time goes in v4:
time: 272 us; the launch traced here: 271 us
  blocking collectives  120 us (44%)
  starting transfers between devices  58.2 us (21%)
  waiting for transfers between devices  32.5 us (12%)
  Pallas kernels  23.5 us (9%)
  other arithmetic  15.4 us (6%)
  local copies, waits for them, and re-layouts  13.4 us (5%)
  between operations  7.24 us (3%)
    all_to_all x7, blocking collectives, exchange(): return lax.all_to_all(blocks, axes, 0, 0, tiled=True)  120 us
    all_to_all x4, starting transfers between devices, exchange(): return lax.all_to_all(blocks, axes, 0, 0, tiled=True)  37.4 us
    all_to_all x4, waiting for transfers between devices, exchange(): return lax.all_to_all(blocks, axes, 0, 0, tiled=True)  32.5 us
    ppermute x4, starting transfers between devices, other_core(): return lax.ppermute(block, 'core', [(0, 1), (1, 0)])  20.7 us
    unnamed x26, local copies, waits for them, and re-layouts  10.7 us
    pallas_call x2, Pallas kernels, build(): pl.pallas_call(functools.partial(build_kernel, gamma, first), grid=grid,...  10.2 us
    another operation x2, other arithmetic, precondition(): lax.linalg.triangular_solve(factor, lower, left_side=True, lower=True, tr...  9.82 us
    pallas_call x4, Pallas kernels, back(): pl.pallas_call(functools.partial(back_kernel, count), grid=grid, in_specs...  9.39 us
  transfers between devices with their start and end apart: 8, of which 4 were waited for; matrix products, arithmetic and copies ran while one was open for 4% of the time, Pallas kernels for 4%

profile of v4, /device:TPU:1, one launch (start us, length us, event | category | flops | bytes accessed | tf_op | source)
XLA Modules:
  0.0 271.0 jit_solution(2654922705223617225)
XLA Ops:
  3.2 7.6 %all-to-all-start.1 = ((bf16[16,192,128]{2,1,0:T(8,128)(2,1)}), bf16[16,192,128]{2,1,0:T(8,128)(2,1)S(1)}, u32[]{:S(2)}, u32[]{:S(2)}) async-start(bf16[16,192,128]{2,1,0:T(8,128)(2,1)} %broadcast_in_dim.15), calls=%async_computation.1 | async-start | bytes 1572864 | tf_op jit(solution)/shard_map/all_to_all | solution.py:34
  10.9 11.8 %all-to-all-done.1.blk_ref = bf16[16,192,128]{2,1,0:T(8,128)(2,1)S(1)} async-done(((bf16[16,192,128]{2,1,0:T(8,128)(2,1)}), bf16[16,192,128]{2,1,0:T(8,128)(2,1)S(1)}, u32[]{:S(2)}, u32[]{:S(2)}) %all-to-all-start.1) | async-done | bytes 786464 | tf_op jit(solution)/shard_map/all_to_all | solution.py:34
  23.4 16.3 %all-to-all-start = ((bf16[16,64,128]{2,1,0:T(8,128)(2,1)}), bf16[16,64,128]{2,1,0:T(8,128)(2,1)S(1)}, u32[]{:S(2)}, u32[]{:S(2)}) async-start(bf16[16,64,128]{2,1,0:T(8,128)(2,1)} %broadcast_in_dim.14), calls=%async_computation | async-start | bytes 524288 | tf_op jit(solution)/shard_map/all_to_all | solution.py:34
  39.7 4.5 %collective-permute-start = (bf16[16,192,128]{2,1,0:T(8,128)(2,1)S(1)}, bf16[16,192,128]{2,1,0:T(8,128)(2,1)S(1)}, u32[]{:S(2)}, u32[]{:S(2)}) collective-permute-start(bf16[16,192,128]{2,1,0:T(8,128)(2,1)S(1)} %all-to-all-done.1.blk_ref), channel_id=1, source_target_pairs={{0,16},{16,0},{1,17},{17,1},{2,18},{18,2},{3,19},{19,3},{4,20},{20... | collective-permute-start | bytes 2359304 | tf_op jit(solution)/shard_map/ppermute | solution.py:43
  44.1 8.3 %all-to-all-done = bf16[16,64,128]{2,1,0:T(8,128)(2,1)S(1)} async-done(((bf16[16,64,128]{2,1,0:T(8,128)(2,1)}), bf16[16,64,128]{2,1,0:T(8,128)(2,1)S(1)}, u32[]{:S(2)}, u32[]{:S(2)}) %all-to-all-start) | async-done | bytes 262176 | tf_op jit(solution)/shard_map/all_to_all | solution.py:34
  52.8 4.7 %build_tile.2 = (bf16[2048,1024]{1,0:T(8,128)(2,1)S(1)}, f32[16,32,128]{2,1,0:T(8,128)S(1)}) custom-call(bf16[1024,128]{1,0:T(8,128)(2,1)S(1)} %bitcast.88, f32[1,1024]{1,0:T(1,128)S(1)} %sub.72.gap_ref, bf16[16,192,128]{2,1,0:T(8,128)(2,1)S(1)} %all-to-all-done.1.blk_ref), custom_call_target="tpu_custom_call" | custom-call | flops 805306368 | bytes 4194304 | tf_op jit(solution)/shard_map/build_tile/pallas_call | solution.py:153
  59.4 5.5 %build_tile.3 = (bf16[2048,1024]{1,0:T(8,128)(2,1)S(1)}, f32[16,32,128]{2,1,0:T(8,128)}) custom-call(bf16[1024,128]{1,0:T(8,128)(2,1)S(1)} %bitcast.89, f32[1,1024]{1,0:T(1,128)S(1)} %sub.72.gap_ref, bf16[16,192,128]{2,1,0:T(8,128)(2,1)S(1)} %collective-permute-done.blk_ref, f32[16,32,128]{2,1,0:T(8,128)S(1)} %get-tuple-element.8.rest_0_), custom_call_target="tpu_custom_call" | custom-call | flops 805306368 | bytes 4194304 | tf_op jit(solution)/shard_map/build_tile/pallas_call | solution.py:153
  64.9 2.0 copy-done.5
  66.9 10.0 %all-to-all-start.2 = ((f32[16,32,128]{2,1,0:T(8,128)}), f32[16,32,128]{2,1,0:T(8,128)S(1)}, u32[]{:S(2)}, u32[]{:S(2)}) async-start(f32[16,32,128]{2,1,0:T(8,128)} %get-tuple-element.9), calls=%async_computation.2 | async-start | bytes 524288 | tf_op jit(solution)/shard_map/all_to_all | solution.py:34
  76.9 9.8 %custom-call.9 = f32[1,128,128]{1,2,0:T(8,128)S(1)} custom-call(f32[1,128,128]{2,1,0:T(8,128)S(1)} %select_bitcast_fusion), custom_call_target="InvertDiagBlocksLowerTriangular" | custom-call | tf_op jit(solution)/shard_map/triangular_solve/custom-call.0 | solution.py:30
  87.4 2.3 all-to-all-done.2
  89.8 22.2 %all_to_all.55.u_ref = bf16[16,48,128]{2,1,0:T(8,128)(2,1)S(1)} all-to-all(bf16[16,48,128]{2,1,0:T(8,128)(2,1)S(1)} %broadcast_in_dim.16), channel_id=1, replica_groups=mesh['z'=16,'core'=2,'ctr'=16] {'z'}, dimensions={0} | all-to-all | bytes 393216 | tf_op jit(solution)/shard_map/all_to_all | solution.py:34
  112.0 2.2 copy-done.6
  114.2 2.3 back_tile.5
  116.5 7.4 %collective-permute-start.1 = (f32[16,72,128]{2,1,0:T(8,128)S(1)}, f32[16,72,128]{2,1,0:T(8,128)S(1)}, u32[]{:S(2)}, u32[]{:S(2)}) collective-permute-start(f32[16,72,128]{2,1,0:T(8,128)S(1)} %back_tile.5), channel_id=1, source_target_pairs={{0,16},{16,0},{1,17},{17,1},{2,18},{18,2},{3,19},{19,3},{4,20},{20... | collective-permute-start | bytes 1769480 | tf_op jit(solution)/shard_map/ppermute | solution.py:43
  123.9 2.4 back_tile.4
  126.4 18.1 %all_to_all.56 = f32[16,72,128]{2,1,0:T(8,128)S(1)} all-to-all(f32[16,72,128]{2,1,0:T(8,128)S(1)} %add.43), channel_id=1, replica_groups=mesh['z'=16,'core'=2,'ctr'=16] {'ctr'}, dimensions={0} | all-to-all | bytes 1179648 | tf_op jit(solution)/shard_map/all_to_all | solution.py:34
  147.8 16.0 %all_to_all.57 = f32[16,8,128]{2,1,0:T(8,128)S(1)} all-to-all(f32[16,8,128]{2,1,0:T(8,128)S(1)} %broadcast_in_dim.17), channel_id=1, replica_groups=mesh['z'=16,'core'=2,'ctr'=16] {'z'}, dimensions={0} | all-to-all | bytes 131072 | tf_op jit(solution)/shard_map/all_to_all | solution.py:34
  163.8 13.4 %all_to_all.58 = f32[32,8,128]{2,1,0:T(8,128)S(1)} all-to-all(f32[32,8,128]{2,1,0:T(8,128)S(1)} %broadcast_in_dim.18), channel_id=1, replica_groups=mesh['z'=16,'core'=2,'ctr'=16] {'core','ctr'}, dimensions={0} | all-to-all | bytes 262144 | tf_op jit(solution)/shard_map/all_to_all | solution.py:34
  179.1 11.1 %all_to_all.59.blk_ref = bf16[16,64,128]{2,1,0:T(8,128)(2,1)S(1)} all-to-all(bf16[16,64,128]{2,1,0:T(8,128)(2,1)S(1)} %broadcast_in_dim.19), channel_id=1, replica_groups=mesh['z'=16,'core'=2,'ctr'=16] {'ctr'}, dimensions={0} | all-to-all | bytes 524288 | tf_op jit(solution)/shard_map/all_to_all | solution.py:34
  190.2 3.4 %collective-permute-start.2 = (bf16[16,64,128]{2,1,0:T(8,128)(2,1)S(1)}, bf16[16,64,128]{2,1,0:T(8,128)(2,1)S(1)}, u32[]{:S(2)}, u32[]{:S(2)}) collective-permute-start(bf16[16,64,128]{2,1,0:T(8,128)(2,1)S(1)} %all_to_all.59.blk_ref), channel_id=1, source_target_pairs={{0,16},{16,0},{1,17},{17,1},{2,18},{18,2},{3,19},{19,3},{4,20},{20... | collective-permute-start | bytes 786440 | tf_op jit(solution)/shard_map/ppermute | solution.py:43
  193.6 2.2 copy-done.3
  195.8 1.9 apply_tile.2.rest_0_
  198.0 1.9 apply_tile.3
  199.9 17.1 %all_to_all.60 = f32[16,32,128]{2,1,0:T(8,128)S(1)} all-to-all(f32[16,32,128]{2,1,0:T(8,128)S(1)} %apply_tile.3), channel_id=1, replica_groups=mesh['z'=16,'core'=2,'ctr'=16] {'z'}, dimensions={0} | all-to-all | bytes 524288 | tf_op jit(solution)/shard_map/all_to_all | solution.py:34
  217.2 21.8 %all_to_all.61.u_ref = bf16[16,32,128]{2,1,0:T(8,128)(2,1)S(1)} all-to-all(bf16[16,32,128]{2,1,0:T(8,128)(2,1)S(1)} %broadcast_in_dim.20), channel_id=1, replica_groups=mesh['z'=16,'core'=2,'ctr'=16] {'z'}, dimensions={0} | all-to-all | bytes 262144 | tf_op jit(solution)/shard_map/all_to_all | solution.py:34
  239.0 2.2 copy-done.8
  241.2 2.3 back_tile.7
  243.5 5.5 %collective-permute-start.3 = (f32[16,72,128]{2,1,0:T(8,128)S(1)}, f32[16,72,128]{2,1,0:T(8,128)S(1)}, u32[]{:S(2)}, u32[]{:S(2)}) collective-permute-start(f32[16,72,128]{2,1,0:T(8,128)S(1)} %back_tile.7), channel_id=1, source_target_pairs={{0,16},{16,0},{1,17},{17,1},{2,18},{18,2},{3,19},{19,3},{4,20},{20... | collective-permute-start | bytes 1769480 | tf_op jit(solution)/shard_map/ppermute | solution.py:43
  249.0 2.3 back_tile.6
  252.3 3.6 %all-to-all-start.10 = ((f32[16,72,128]{2,1,0:T(8,128)}), f32[16,72,128]{2,1,0:T(8,128)S(1)}, u32[]{:S(2)}, u32[]{:S(2)}) async-start(f32[16,72,128]{2,1,0:T(8,128)} %add.47), calls=%async_computation.10 | async-start | bytes 1179648 | tf_op jit(solution)/shard_map/all_to_all | solution.py:34
  257.8 10.1 %all-to-all-done.10 = f32[16,72,128]{2,1,0:T(8,128)S(1)} async-done(((f32[16,72,128]{2,1,0:T(8,128)}), f32[16,72,128]{2,1,0:T(8,128)S(1)}, u32[]{:S(2)}, u32[]{:S(2)}) %all-to-all-start.10) | async-done | bytes 589856 | tf_op jit(solution)/shard_map/all_to_all | solution.py:34
  (69 shorter events, 11.6 us)
Async XLA Ops:
  0.6 10.2 %copy-start = (bf16[1024,128]{1,0:T(8,128)(2,1)S(1)}, bf16[1024,128]{1,0:T(8,128)(2,1)}, u32[]{:S(2)}) copy-start(bf16[1024,128]{1,0:T(8,128)(2,1)} %param.10) | copy-start | bytes 786436
  3.2 19.4 %all-to-all-start.1 = ((bf16[16,192,128]{2,1,0:T(8,128)(2,1)}), bf16[16,192,128]{2,1,0:T(8,128)(2,1)S(1)}, u32[]{:S(2)}, u32[]{:S(2)}) async-start(bf16[16,192,128]{2,1,0:T(8,128)(2,1)} %broadcast_in_dim.15), calls=%async_computation.1 | async-start | bytes 1572864 | tf_op jit(solution)/shard_map/all_to_all | solution.py:34
  23.4 29.1 %all-to-all-start = ((bf16[16,64,128]{2,1,0:T(8,128)(2,1)}), bf16[16,64,128]{2,1,0:T(8,128)(2,1)S(1)}, u32[]{:S(2)}, u32[]{:S(2)}) async-start(bf16[16,64,128]{2,1,0:T(8,128)(2,1)} %broadcast_in_dim.14), calls=%async_computation | async-start | bytes 524288 | tf_op jit(solution)/shard_map/all_to_all | solution.py:34
  39.7 19.8 %collective-permute-start = (bf16[16,192,128]{2,1,0:T(8,128)(2,1)S(1)}, bf16[16,192,128]{2,1,0:T(8,128)(2,1)S(1)}, u32[]{:S(2)}, u32[]{:S(2)}) collective-permute-start(bf16[16,192,128]{2,1,0:T(8,128)(2,1)S(1)} %all-to-all-done.1.blk_ref), channel_id=1, source_target_pairs={{0,16},{16,0},{1,17},{17,1},{2,18},{18,2},{3,19},{19,3},{4,20},{20... | collective-permute-start | bytes 2359304 | tf_op jit(solution)/shard_map/ppermute | solution.py:43
  52.8 24.1 %copy-start.11 = (f32[128,128]{1,0:T(8,128)S(1)}, f32[128,128]{1,0:T(8,128)}, u32[]{:S(2)}) copy-start(f32[128,128]{1,0:T(8,128)} %param.12) | copy-start | bytes 196612
  52.8 34.0 %copy-start.9 = (f32[128,64]{0,1:T(8,128)S(1)}, f32[128,64]{0,1:T(8,128)}, u32[]{:S(2)}) copy-start(f32[128,64]{0,1:T(8,128)} %param.15) | copy-start | bytes 98308
  52.8 34.0 %copy-start.10 = (f32[128,64]{0,1:T(8,128)S(1)}, f32[128,64]{0,1:T(8,128)}, u32[]{:S(2)}) copy-start(f32[128,64]{0,1:T(8,128)} %param.14) | copy-start | bytes 98308
  57.5 1.9 copy-start.1
  64.9 2.0 copy-start.5
  66.9 22.8 %all-to-all-start.2 = ((f32[16,32,128]{2,1,0:T(8,128)}), f32[16,32,128]{2,1,0:T(8,128)S(1)}, u32[]{:S(2)}, u32[]{:S(2)}) async-start(f32[16,32,128]{2,1,0:T(8,128)} %get-tuple-element.9), calls=%async_computation.2 | async-start | bytes 524288 | tf_op jit(solution)/shard_map/all_to_all | solution.py:34
  89.8 34.1 %copy-start.2 = (bf16[2048,1024]{1,0:T(8,128)(2,1)S(1)}, bf16[2048,1024]{1,0:T(8,128)(2,1)}, u32[]{:S(2)}) copy-start(bf16[2048,1024]{1,0:T(8,128)(2,1)} %copy-done.1) | copy-start | bytes 12582916
  112.0 2.2 copy-start.6
  116.5 9.7 %collective-permute-start.1 = (f32[16,72,128]{2,1,0:T(8,128)S(1)}, f32[16,72,128]{2,1,0:T(8,128)S(1)}, u32[]{:S(2)}, u32[]{:S(2)}) collective-permute-start(f32[16,72,128]{2,1,0:T(8,128)S(1)} %back_tile.5), channel_id=1, source_target_pairs={{0,16},{16,0},{1,17},{17,1},{2,18},{18,2},{3,19},{19,3},{4,20},{20... | collective-permute-start | bytes 1769480 | tf_op jit(solution)/shard_map/ppermute | solution.py:43
  190.2 7.6 %collective-permute-start.2 = (bf16[16,64,128]{2,1,0:T(8,128)(2,1)S(1)}, bf16[16,64,128]{2,1,0:T(8,128)(2,1)S(1)}, u32[]{:S(2)}, u32[]{:S(2)}) collective-permute-start(bf16[16,64,128]{2,1,0:T(8,128)(2,1)S(1)} %all_to_all.59.blk_ref), channel_id=1, source_target_pairs={{0,16},{16,0},{1,17},{17,1},{2,18},{18,2},{3,19},{19,3},{4,20},{20... | collective-permute-start | bytes 786440 | tf_op jit(solution)/shard_map/ppermute | solution.py:43
  193.6 2.2 copy-start.3
  195.8 2.2 copy-start.7
  217.1 31.9 %copy-start.4 = (bf16[2048,1024]{1,0:T(8,128)(2,1)S(1)}, bf16[2048,1024]{1,0:T(8,128)(2,1)}, u32[]{:S(2)}) copy-start(bf16[2048,1024]{1,0:T(8,128)(2,1)} %copy-done.1) | copy-start | bytes 12582916
  239.0 2.2 copy-start.8
  243.5 26.9 %copy-start.12 = (f32[128,64]{0,1:T(8,128)S(1)}, f32[128,64]{0,1:T(8,128)}, u32[]{:S(2)}) copy-start(f32[128,64]{0,1:T(8,128)} %param.13) | copy-start | bytes 98308
  243.5 7.9 %collective-permute-start.3 = (f32[16,72,128]{2,1,0:T(8,128)S(1)}, f32[16,72,128]{2,1,0:T(8,128)S(1)}, u32[]{:S(2)}, u32[]{:S(2)}) collective-permute-start(f32[16,72,128]{2,1,0:T(8,128)S(1)} %back_tile.7), channel_id=1, source_target_pairs={{0,16},{16,0},{1,17},{17,1},{2,18},{18,2},{3,19},{19,3},{4,20},{20... | collective-permute-start | bytes 1769480 | tf_op jit(solution)/shard_map/ppermute | solution.py:43
  252.3 15.7 %all-to-all-start.10 = ((f32[16,72,128]{2,1,0:T(8,128)}), f32[16,72,128]{2,1,0:T(8,128)S(1)}, u32[]{:S(2)}, u32[]{:S(2)}) async-start(f32[16,72,128]{2,1,0:T(8,128)} %add.47), calls=%async_computation.10 | async-start | bytes 1179648 | tf_op jit(solution)/shard_map/all_to_all | solution.py:34

commit v5 on v4

--- a/solution.py
+++ b/solution.py
@@ -17,7 +17,7 @@
 RIDE = 8
 BF = jnp.bfloat16
 F32 = jnp.float32
-PARAMS = pltpu.CompilerParams(vmem_limit_bytes=16 * 1024 * 1024)
+PARAMS = pltpu.CompilerParams(vmem_limit_bytes=24 * 1024 * 1024)
 
 
 def row_gaps(rows):
@@ -78,9 +78,30 @@
             u_ref[at] = piece if before_ref is None else piece + before_ref[at]
 
 
+def rows_at(step):
+    rows = GROUP * LANES
+    return pl.ds(pl.multiple_of(step * rows, rows), rows)
+
+
+def tile_copy(source, target, sems, step):
+    rows = rows_at(step)
+    return pltpu.make_async_copy(source.at[rows], target.at[rows], sems.at[step])
+
+
+def fetch(step, tile_ref, buf, sems):
+    @pl.when(step == 0)
+    def _():
+        for at in range(sems.shape[0]):
+            tile_copy(tile_ref, buf, sems, at).start()
+
+    tile_copy(tile_ref, buf, sems, step).wait()
+    return buf[rows_at(step)]
+
+
 def build_kernel(gamma, first, pts_ref, gap_ref, blk_ref, *rest):
     before_ref = None if first else rest[0]
-    tile_ref, u_ref, acc = rest[-3:]
+    tile_ref, u_ref, acc, buf, sems = rest[-5:]
+    step = pl.program_id(0)
     dim = pts_ref.shape[1]
     blk = blk_ref[...]
     cen = jnp.concatenate([blk[g, :LANES] for g in range(GROUP)], axis=0)
@@ -89,25 +110,35 @@
     gap_c = dim - jnp.sum(wide * wide, axis=1, keepdims=True)
     cross = lax.dot_general(cen, pts_ref[...], (((1,), (1,)), ((), ())), preferred_element_type=F32)
     tile = jnp.exp(gamma * (2.0 * cross + gap_c + gap_ref[...])).astype(BF)
-    tile_ref[...] = tile
+    buf[rows_at(step)] = tile
+    tile_copy(buf, tile_ref, sems, step).start()
     part = jnp.dot(vec, tile, preferred_element_type=F32)
-    add_up(pl.program_id(0), part, before_ref, u_ref, acc)
+    add_up(step, part, before_ref, u_ref, acc)
+
+    @pl.when(step == pl.num_programs(0) - 1)
+    def _():
+        for at in range(sems.shape[0]):
+            tile_copy(buf, tile_ref, sems, at).wait()
 
 
 def apply_kernel(first, blk_ref, tile_ref, *rest):
     before_ref = None if first else rest[0]
-    u_ref, acc = rest[-2:]
+    u_ref, acc, buf, sems = rest[-4:]
+    step = pl.program_id(0)
+    tile = fetch(step, tile_ref, buf, sems)
     blk = blk_ref[...]
     vec = jnp.concatenate([blk[g] for g in range(GROUP)], axis=1)
-    part = jnp.dot(vec, tile_ref[...], preferred_element_type=F32)
-    add_up(pl.program_id(0), part, before_ref, u_ref, acc)
-
-
-def back_kernel(count, u_ref, tile_ref, v_ref, ub, ride):
+    part = jnp.dot(vec, tile, preferred_element_type=F32)
+    add_up(step, part, before_ref, u_ref, acc)
+
+
+def back_kernel(count, u_ref, tile_ref, v_ref, ub, ride, buf, sems):
     outs = ub.shape[0]
     half = outs // 2
-
-    @pl.when(pl.program_id(0) == 0)
+    step = pl.program_id(0)
+    tile = fetch(step, tile_ref, buf, sems)
+
+    @pl.when(step == 0)
     def _():
         squares = jnp.zeros((half, LANES), F32)
         for at in range(u_ref.shape[0]):
@@ -121,7 +152,7 @@
         rows.append(jnp.zeros((RIDE - count - 1, LANES), F32))
         ride[...] = jnp.concatenate(rows, axis=0)
 
-    v = lax.dot_general(ub[...], tile_ref[...], (((1,), (1,)), ((), ())), preferred_element_type=F32)
+    v = lax.dot_general(ub[...], tile, (((1,), (1,)), ((), ())), preferred_element_type=F32)
     for g in range(GROUP):
         v_ref[g, :outs] = v[:, g * LANES : (g + 1) * LANES]
         v_ref[g, outs:] = ride[...]
@@ -135,12 +166,12 @@
     total_points = points.shape[0] * n_z * CORES
     n_pts = points.shape[0]
     share = n_pts // n_ctr
-    wide = GROUP * LANES
     grid = (n_ctr // GROUP,)
     u_shape = jax.ShapeDtypeStruct((2 * n_pts // LANES, outs // 2, LANES), F32)
     whole = lambda shape: pl.BlockSpec(shape, lambda i: (0,) * len(shape))
     blocks = lambda rows: pl.BlockSpec((GROUP, rows, LANES), lambda i: (i, 0, 0))
-    tiles = pl.BlockSpec((wide, n_pts), lambda i: (i, 0))
+    tiles = pl.BlockSpec(memory_space=pltpu.HBM)
+    copies = [pltpu.VMEM((n_ctr * LANES, n_pts), BF), pltpu.SemaphoreType.DMA(grid)]
     acc = pltpu.VMEM((outs, n_pts), F32)
     work = n_ctr * LANES * n_pts
 
@@ -156,7 +187,7 @@
             in_specs=[whole(pts.shape), whole(gap.shape), blocks(blk.shape[1])] + [whole(u_shape.shape)] * len(extra),
             out_specs=[tiles, whole(u_shape.shape)],
             out_shape=[jax.ShapeDtypeStruct((n_ctr * LANES, n_pts), BF), u_shape],
-            scratch_shapes=[acc],
+            scratch_shapes=[acc] + copies,
             compiler_params=PARAMS,
             cost_estimate=cost(2 * work * (dim + outs), work, 2 * work),
             name="build_tile",
@@ -171,7 +202,7 @@
             in_specs=[blocks(outs), tiles] + [whole(u_shape.shape)] * len(extra),
             out_specs=whole(u_shape.shape),
             out_shape=u_shape,
-            scratch_shapes=[acc],
+            scratch_shapes=[acc] + copies,
             compiler_params=PARAMS,
             cost_estimate=cost(2 * work * outs, 0, 2 * work),
             name="apply_tile",
@@ -184,7 +215,7 @@
             in_specs=[whole(u.shape), tiles],
             out_specs=blocks(outs + RIDE),
             out_shape=jax.ShapeDtypeStruct((n_ctr, outs + RIDE, LANES), F32),
-            scratch_shapes=[pltpu.VMEM((outs, n_pts), BF), pltpu.VMEM((RIDE, LANES), F32)],
+            scratch_shapes=[pltpu.VMEM((outs, n_pts), BF), pltpu.VMEM((RIDE, LANES), F32)] + copies,
             compiler_params=PARAMS,
             cost_estimate=cost(2 * work * outs, 0, 2 * work),
             name="back_tile",

time: 272 us -> 276 us (1.015)
  Pallas kernels: 23.5 us -> 27.6 us
  transfers between devices with their start and end apart: 8 -> 8, of which waited for: 4 -> 4; matrix products, arithmetic and copies ran while one was open for 4% -> 4% of each run, Pallas kernels for 4% -> 5%
where the time goes in v5:
time: 276 us; the launch traced here: 275 us
  blocking collectives  120 us (43%)
  starting transfers between devices  58.2 us (21%)
  waiting for transfers between devices  32.5 us (12%)
  Pallas kernels  27.6 us (10%)
  other arithmetic  15.4 us (6%)
  local copies, waits for them, and re-layouts  13.1 us (5%)
  between operations  7.26 us (3%)
    all_to_all x7, blocking collectives, exchange(): return lax.all_to_all(blocks, axes, 0, 0, tiled=True)  120 us
    all_to_all x4, starting transfers between devices, exchange(): return lax.all_to_all(blocks, axes, 0, 0, tiled=True)  37.4 us
    all_to_all x4, waiting for transfers between devices, exchange(): return lax.all_to_all(blocks, axes, 0, 0, tiled=True)  32.5 us
    ppermute x4, starting transfers between devices, other_core(): return lax.ppermute(block, 'core', [(0, 1), (1, 0)])  20.7 us
    pallas_call x2, Pallas kernels, build(): pl.pallas_call(functools.partial(build_kernel, gamma, first), grid=grid,...  12 us
    pallas_call x4, Pallas kernels, back(): pl.pallas_call(functools.partial(back_kernel, count), grid=grid, in_specs...  10.9 us
    unnamed x26, local copies, waits for them, and re-layouts  10.5 us
    another operation x2, other arithmetic, precondition(): lax.linalg.triangular_solve(factor, lower, left_side=True, lower=True, tr...  9.82 us
  transfers between devices with their start and end apart: 8, of which 4 were waited for; matrix products, arithmetic and copies ran while one was open for 4% of the time, Pallas kernels for 5%

profile of v5, /device:TPU:1, one launch (start us, length us, event | category | flops | bytes accessed | tf_op | source)
XLA Modules:
  0.0 274.9 jit_solution(14244183027841427756)
XLA Ops:
  3.2 7.6 %all-to-all-start.1 = ((bf16[16,192,128]{2,1,0:T(8,128)(2,1)}), bf16[16,192,128]{2,1,0:T(8,128)(2,1)S(1)}, u32[]{:S(2)}, u32[]{:S(2)}) async-start(bf16[16,192,128]{2,1,0:T(8,128)(2,1)} %broadcast_in_dim.15), calls=%async_computation.1 | async-start | bytes 1572864 | tf_op jit(solution)/shard_map/all_to_all | solution.py:34
  10.9 11.8 %all-to-all-done.1.blk_ref = bf16[16,192,128]{2,1,0:T(8,128)(2,1)S(1)} async-done(((bf16[16,192,128]{2,1,0:T(8,128)(2,1)}), bf16[16,192,128]{2,1,0:T(8,128)(2,1)S(1)}, u32[]{:S(2)}, u32[]{:S(2)}) %all-to-all-start.1) | async-done | bytes 786464 | tf_op jit(solution)/shard_map/all_to_all | solution.py:34
  23.4 16.3 %all-to-all-start = ((bf16[16,64,128]{2,1,0:T(8,128)(2,1)}), bf16[16,64,128]{2,1,0:T(8,128)(2,1)S(1)}, u32[]{:S(2)}, u32[]{:S(2)}) async-start(bf16[16,64,128]{2,1,0:T(8,128)(2,1)} %broadcast_in_dim.14), calls=%async_computation | async-start | bytes 524288 | tf_op jit(solution)/shard_map/all_to_all | solution.py:34
  39.7 4.5 %collective-permute-start = (bf16[16,192,128]{2,1,0:T(8,128)(2,1)S(1)}, bf16[16,192,128]{2,1,0:T(8,128)(2,1)S(1)}, u32[]{:S(2)}, u32[]{:S(2)}) collective-permute-start(bf16[16,192,128]{2,1,0:T(8,128)(2,1)S(1)} %all-to-all-done.1.blk_ref), channel_id=1, source_target_pairs={{0,16},{16,0},{1,17},{17,1},{2,18},{18,2},{3,19},{19,3},{4,20},{20... | collective-permute-start | bytes 2359304 | tf_op jit(solution)/shard_map/ppermute | solution.py:43
  44.1 8.3 %all-to-all-done = bf16[16,64,128]{2,1,0:T(8,128)(2,1)S(1)} async-done(((bf16[16,64,128]{2,1,0:T(8,128)(2,1)}), bf16[16,64,128]{2,1,0:T(8,128)(2,1)S(1)}, u32[]{:S(2)}, u32[]{:S(2)}) %all-to-all-start) | async-done | bytes 262176 | tf_op jit(solution)/shard_map/all_to_all | solution.py:34
  52.8 5.6 %build_tile.2 = (bf16[2048,1024]{1,0:T(8,128)(2,1)S(1)}, f32[16,32,128]{2,1,0:T(8,128)S(1)}) custom-call(bf16[1024,128]{1,0:T(8,128)(2,1)S(1)} %bitcast.88, f32[1,1024]{1,0:T(1,128)S(1)} %sub.72.gap_ref, bf16[16,192,128]{2,1,0:T(8,128)(2,1)S(1)} %all-to-all-done.1.blk_ref), custom_call_target="tpu_custom_call" | custom-call | flops 805306368 | bytes 4194304 | tf_op jit(solution)/shard_map/build_tile/pallas_call | solution.py:184
  60.3 6.4 %build_tile.3 = (bf16[2048,1024]{1,0:T(8,128)(2,1)S(1)}, f32[16,32,128]{2,1,0:T(8,128)}) custom-call(bf16[1024,128]{1,0:T(8,128)(2,1)S(1)} %bitcast.89, f32[1,1024]{1,0:T(1,128)S(1)} %sub.72.gap_ref, bf16[16,192,128]{2,1,0:T(8,128)(2,1)S(1)} %collective-permute-done.blk_ref, f32[16,32,128]{2,1,0:T(8,128)S(1)} %get-tuple-element.8.rest_0_), custom_call_target="tpu_custom_call" | custom-call | flops 805306368 | bytes 4194304 | tf_op jit(solution)/shard_map/build_tile/pallas_call | solution.py:184
  66.7 2.0 copy-done.5
  68.7 10.0 %all-to-all-start.2 = ((f32[16,32,128]{2,1,0:T(8,128)}), f32[16,32,128]{2,1,0:T(8,128)S(1)}, u32[]{:S(2)}, u32[]{:S(2)}) async-start(f32[16,32,128]{2,1,0:T(8,128)} %get-tuple-element.9), calls=%async_computation.2 | async-start | bytes 524288 | tf_op jit(solution)/shard_map/all_to_all | solution.py:34
  78.7 9.8 %custom-call.9 = f32[1,128,128]{1,2,0:T(8,128)S(1)} custom-call(f32[1,128,128]{2,1,0:T(8,128)S(1)} %select_bitcast_fusion), custom_call_target="InvertDiagBlocksLowerTriangular" | custom-call | tf_op jit(solution)/shard_map/triangular_solve/custom-call.0 | solution.py:30
  89.1 2.3 all-to-all-done.2
  91.6 22.2 %all_to_all.55.u_ref = bf16[16,48,128]{2,1,0:T(8,128)(2,1)S(1)} all-to-all(bf16[16,48,128]{2,1,0:T(8,128)(2,1)S(1)} %broadcast_in_dim.16), channel_id=1, replica_groups=mesh['z'=16,'core'=2,'ctr'=16] {'z'}, dimensions={0} | all-to-all | bytes 393216 | tf_op jit(solution)/shard_map/all_to_all | solution.py:34
  113.8 2.2 copy-done.6
  116.0 2.7 back_tile.5
  118.7 7.4 %collective-permute-start.1 = (f32[16,72,128]{2,1,0:T(8,128)S(1)}, f32[16,72,128]{2,1,0:T(8,128)S(1)}, u32[]{:S(2)}, u32[]{:S(2)}) collective-permute-start(f32[16,72,128]{2,1,0:T(8,128)S(1)} %back_tile.5), channel_id=1, source_target_pairs={{0,16},{16,0},{1,17},{17,1},{2,18},{18,2},{3,19},{19,3},{4,20},{20... | collective-permute-start | bytes 1769480 | tf_op jit(solution)/shard_map/ppermute | solution.py:43
  126.1 2.7 back_tile.4
  128.9 18.1 %all_to_all.56 = f32[16,72,128]{2,1,0:T(8,128)S(1)} all-to-all(f32[16,72,128]{2,1,0:T(8,128)S(1)} %add.43), channel_id=1, replica_groups=mesh['z'=16,'core'=2,'ctr'=16] {'ctr'}, dimensions={0} | all-to-all | bytes 1179648 | tf_op jit(solution)/shard_map/all_to_all | solution.py:34
  150.3 16.0 %all_to_all.57 = f32[16,8,128]{2,1,0:T(8,128)S(1)} all-to-all(f32[16,8,128]{2,1,0:T(8,128)S(1)} %broadcast_in_dim.17), channel_id=1, replica_groups=mesh['z'=16,'core'=2,'ctr'=16] {'z'}, dimensions={0} | all-to-all | bytes 131072 | tf_op jit(solution)/shard_map/all_to_all | solution.py:34
  166.3 13.4 %all_to_all.58 = f32[32,8,128]{2,1,0:T(8,128)S(1)} all-to-all(f32[32,8,128]{2,1,0:T(8,128)S(1)} %broadcast_in_dim.18), channel_id=1, replica_groups=mesh['z'=16,'core'=2,'ctr'=16] {'core','ctr'}, dimensions={0} | all-to-all | bytes 262144 | tf_op jit(solution)/shard_map/all_to_all | solution.py:34
  181.6 11.1 %all_to_all.59.blk_ref = bf16[16,64,128]{2,1,0:T(8,128)(2,1)S(1)} all-to-all(bf16[16,64,128]{2,1,0:T(8,128)(2,1)S(1)} %broadcast_in_dim.19), channel_id=1, replica_groups=mesh['z'=16,'core'=2,'ctr'=16] {'ctr'}, dimensions={0} | all-to-all | bytes 524288 | tf_op jit(solution)/shard_map/all_to_all | solution.py:34
  192.7 3.4 %collective-permute-start.2 = (bf16[16,64,128]{2,1,0:T(8,128)(2,1)S(1)}, bf16[16,64,128]{2,1,0:T(8,128)(2,1)S(1)}, u32[]{:S(2)}, u32[]{:S(2)}) collective-permute-start(bf16[16,64,128]{2,1,0:T(8,128)(2,1)S(1)} %all_to_all.59.blk_ref), channel_id=1, source_target_pairs={{0,16},{16,0},{1,17},{17,1},{2,18},{18,2},{3,19},{19,3},{4,20},{20... | collective-permute-start | bytes 786440 | tf_op jit(solution)/shard_map/ppermute | solution.py:43
  196.2 2.2 copy-done.3
  198.3 2.3 apply_tile.2.rest_0_
  200.7 2.4 apply_tile.3
  203.1 17.1 %all_to_all.60 = f32[16,32,128]{2,1,0:T(8,128)S(1)} all-to-all(f32[16,32,128]{2,1,0:T(8,128)S(1)} %apply_tile.3), channel_id=1, replica_groups=mesh['z'=16,'core'=2,'ctr'=16] {'z'}, dimensions={0} | all-to-all | bytes 524288 | tf_op jit(solution)/shard_map/all_to_all | solution.py:34
  220.3 21.8 %all_to_all.61.u_ref = bf16[16,32,128]{2,1,0:T(8,128)(2,1)S(1)} all-to-all(bf16[16,32,128]{2,1,0:T(8,128)(2,1)S(1)} %broadcast_in_dim.20), channel_id=1, replica_groups=mesh['z'=16,'core'=2,'ctr'=16] {'z'}, dimensions={0} | all-to-all | bytes 262144 | tf_op jit(solution)/shard_map/all_to_all | solution.py:34
  242.1 2.2 copy-done.8
  244.3 2.7 back_tile.7
  247.0 5.5 %collective-permute-start.3 = (f32[16,72,128]{2,1,0:T(8,128)S(1)}, f32[16,72,128]{2,1,0:T(8,128)S(1)}, u32[]{:S(2)}, u32[]{:S(2)}) collective-permute-start(f32[16,72,128]{2,1,0:T(8,128)S(1)} %back_tile.7), channel_id=1, source_target_pairs={{0,16},{16,0},{1,17},{17,1},{2,18},{18,2},{3,19},{19,3},{4,20},{20... | collective-permute-start | bytes 1769480 | tf_op jit(solution)/shard_map/ppermute | solution.py:43
  252.5 2.7 back_tile.6
  256.1 3.6 %all-to-all-start.10 = ((f32[16,72,128]{2,1,0:T(8,128)}), f32[16,72,128]{2,1,0:T(8,128)S(1)}, u32[]{:S(2)}, u32[]{:S(2)}) async-start(f32[16,72,128]{2,1,0:T(8,128)} %add.47), calls=%async_computation.10 | async-start | bytes 1179648 | tf_op jit(solution)/shard_map/all_to_all | solution.py:34
  261.6 10.1 %all-to-all-done.10 = f32[16,72,128]{2,1,0:T(8,128)S(1)} async-done(((f32[16,72,128]{2,1,0:T(8,128)}), f32[16,72,128]{2,1,0:T(8,128)S(1)}, u32[]{:S(2)}, u32[]{:S(2)}) %all-to-all-start.10) | async-done | bytes 589856 | tf_op jit(solution)/shard_map/all_to_all | solution.py:34
  (69 shorter events, 11.3 us)
Async XLA Ops:
  0.6 10.2 %copy-start = (bf16[1024,128]{1,0:T(8,128)(2,1)S(1)}, bf16[1024,128]{1,0:T(8,128)(2,1)}, u32[]{:S(2)}) copy-start(bf16[1024,128]{1,0:T(8,128)(2,1)} %param.10) | copy-start | bytes 786436
  3.2 19.4 %all-to-all-start.1 = ((bf16[16,192,128]{2,1,0:T(8,128)(2,1)}), bf16[16,192,128]{2,1,0:T(8,128)(2,1)S(1)}, u32[]{:S(2)}, u32[]{:S(2)}) async-start(bf16[16,192,128]{2,1,0:T(8,128)(2,1)} %broadcast_in_dim.15), calls=%async_computation.1 | async-start | bytes 1572864 | tf_op jit(solution)/shard_map/all_to_all | solution.py:34
  23.4 29.1 %all-to-all-start = ((bf16[16,64,128]{2,1,0:T(8,128)(2,1)}), bf16[16,64,128]{2,1,0:T(8,128)(2,1)S(1)}, u32[]{:S(2)}, u32[]{:S(2)}) async-start(bf16[16,64,128]{2,1,0:T(8,128)(2,1)} %broadcast_in_dim.14), calls=%async_computation | async-start | bytes 524288 | tf_op jit(solution)/shard_map/all_to_all | solution.py:34
  39.7 20.6 %collective-permute-start = (bf16[16,192,128]{2,1,0:T(8,128)(2,1)S(1)}, bf16[16,192,128]{2,1,0:T(8,128)(2,1)S(1)}, u32[]{:S(2)}, u32[]{:S(2)}) collective-permute-start(bf16[16,192,128]{2,1,0:T(8,128)(2,1)S(1)} %all-to-all-done.1.blk_ref), channel_id=1, source_target_pairs={{0,16},{16,0},{1,17},{17,1},{2,18},{18,2},{3,19},{19,3},{4,20},{20... | collective-permute-start | bytes 2359304 | tf_op jit(solution)/shard_map/ppermute | solution.py:43
  52.8 25.9 %copy-start.11 = (f32[128,128]{1,0:T(8,128)S(1)}, f32[128,128]{1,0:T(8,128)}, u32[]{:S(2)}) copy-start(f32[128,128]{1,0:T(8,128)} %param.12) | copy-start | bytes 196612
  52.8 35.7 %copy-start.9 = (f32[128,64]{0,1:T(8,128)S(1)}, f32[128,64]{0,1:T(8,128)}, u32[]{:S(2)}) copy-start(f32[128,64]{0,1:T(8,128)} %param.15) | copy-start | bytes 98308
  52.8 35.8 %copy-start.10 = (f32[128,64]{0,1:T(8,128)S(1)}, f32[128,64]{0,1:T(8,128)}, u32[]{:S(2)}) copy-start(f32[128,64]{0,1:T(8,128)} %param.14) | copy-start | bytes 98308
  58.4 1.9 copy-start.1
  66.7 2.0 copy-start.5
  68.7 22.8 %all-to-all-start.2 = ((f32[16,32,128]{2,1,0:T(8,128)}), f32[16,32,128]{2,1,0:T(8,128)S(1)}, u32[]{:S(2)}, u32[]{:S(2)}) async-start(f32[16,32,128]{2,1,0:T(8,128)} %get-tuple-element.9), calls=%async_computation.2 | async-start | bytes 524288 | tf_op jit(solution)/shard_map/all_to_all | solution.py:34
  91.5 34.5 %copy-start.2 = (bf16[2048,1024]{1,0:T(8,128)(2,1)S(1)}, bf16[2048,1024]{1,0:T(8,128)(2,1)}, u32[]{:S(2)}) copy-start(bf16[2048,1024]{1,0:T(8,128)(2,1)} %copy-done.1) | copy-start | bytes 12582916
  113.8 2.2 copy-start.6
  118.7 10.1 %collective-permute-start.1 = (f32[16,72,128]{2,1,0:T(8,128)S(1)}, f32[16,72,128]{2,1,0:T(8,128)S(1)}, u32[]{:S(2)}, u32[]{:S(2)}) collective-permute-start(f32[16,72,128]{2,1,0:T(8,128)S(1)} %back_tile.5), channel_id=1, source_target_pairs={{0,16},{16,0},{1,17},{17,1},{2,18},{18,2},{3,19},{19,3},{4,20},{20... | collective-permute-start | bytes 1769480 | tf_op jit(solution)/shard_map/ppermute | solution.py:43
  192.7 8.0 %collective-permute-start.2 = (bf16[16,64,128]{2,1,0:T(8,128)(2,1)S(1)}, bf16[16,64,128]{2,1,0:T(8,128)(2,1)S(1)}, u32[]{:S(2)}, u32[]{:S(2)}) collective-permute-start(bf16[16,64,128]{2,1,0:T(8,128)(2,1)S(1)} %all_to_all.59.blk_ref), channel_id=1, source_target_pairs={{0,16},{16,0},{1,17},{17,1},{2,18},{18,2},{3,19},{19,3},{4,20},{20... | collective-permute-start | bytes 786440 | tf_op jit(solution)/shard_map/ppermute | solution.py:43
  196.1 2.2 copy-start.3
  198.3 2.3 copy-start.7
  220.2 32.3 %copy-start.4 = (bf16[2048,1024]{1,0:T(8,128)(2,1)S(1)}, bf16[2048,1024]{1,0:T(8,128)(2,1)}, u32[]{:S(2)}) copy-start(bf16[2048,1024]{1,0:T(8,128)(2,1)} %copy-done.1) | copy-start | bytes 12582916
  242.1 2.2 copy-start.8
  247.0 27.3 %copy-start.12 = (f32[128,64]{0,1:T(8,128)S(1)}, f32[128,64]{0,1:T(8,128)}, u32[]{:S(2)}) copy-start(f32[128,64]{0,1:T(8,128)} %param.13) | copy-start | bytes 98308
  247.0 8.2 %collective-permute-start.3 = (f32[16,72,128]{2,1,0:T(8,128)S(1)}, f32[16,72,128]{2,1,0:T(8,128)S(1)}, u32[]{:S(2)}, u32[]{:S(2)}) collective-permute-start(f32[16,72,128]{2,1,0:T(8,128)S(1)} %back_tile.7), channel_id=1, source_target_pairs={{0,16},{16,0},{1,17},{17,1},{2,18},{18,2},{3,19},{19,3},{4,20},{20... | collective-permute-start | bytes 1769480 | tf_op jit(solution)/shard_map/ppermute | solution.py:43
  256.1 15.7 %all-to-all-start.10 = ((f32[16,72,128]{2,1,0:T(8,128)}), f32[16,72,128]{2,1,0:T(8,128)S(1)}, u32[]{:S(2)}, u32[]{:S(2)}) async-start(f32[16,72,128]{2,1,0:T(8,128)} %add.47), calls=%async_computation.10 | async-start | bytes 1179648 | tf_op jit(solution)/shard_map/all_to_all | solution.py:34

commit v6 on v5

--- a/solution.py
+++ b/solution.py
@@ -17,7 +17,7 @@
 RIDE = 8
 BF = jnp.bfloat16
 F32 = jnp.float32
-PARAMS = pltpu.CompilerParams(vmem_limit_bytes=24 * 1024 * 1024)
+PARAMS = pltpu.CompilerParams(vmem_limit_bytes=52 * 1024 * 1024)
 
 
 def row_gaps(rows):
@@ -83,6 +83,11 @@
     return pl.ds(pl.multiple_of(step * rows, rows), rows)
 
 
+def half_of(tile_ref, half):
+    rows = tile_ref.shape[0] // 2
+    return tile_ref.at[pl.ds(half * rows, rows)]
+
+
 def tile_copy(source, target, sems, step):
     rows = rows_at(step)
     return pltpu.make_async_copy(source.at[rows], target.at[rows], sems.at[step])
@@ -98,9 +103,10 @@
     return buf[rows_at(step)]
 
 
-def build_kernel(gamma, first, pts_ref, gap_ref, blk_ref, *rest):
-    before_ref = None if first else rest[0]
+def build_kernel(gamma, half, pts_ref, gap_ref, blk_ref, *rest):
+    before_ref = rest[0] if half else None
     tile_ref, u_ref, acc, buf, sems = rest[-5:]
+    tile_ref = half_of(tile_ref, half)
     step = pl.program_id(0)
     dim = pts_ref.shape[1]
     blk = blk_ref[...]
@@ -121,8 +127,9 @@
             tile_copy(buf, tile_ref, sems, at).wait()
 
 
-def apply_kernel(first, blk_ref, tile_ref, *rest):
-    before_ref = None if first else rest[0]
+def apply_kernel(half, blk_ref, tile_ref, *rest):
+    before_ref = rest[0] if half else None
+    tile_ref = half_of(tile_ref, half)
     u_ref, acc, buf, sems = rest[-4:]
     step = pl.program_id(0)
     tile = fetch(step, tile_ref, buf, sems)
@@ -132,7 +139,8 @@
     add_up(step, part, before_ref, u_ref, acc)
 
 
-def back_kernel(count, u_ref, tile_ref, v_ref, ub, ride, buf, sems):
+def back_kernel(half, count, u_ref, tile_ref, v_ref, ub, ride, buf, sems):
+    tile_ref = half_of(tile_ref, half)
     outs = ub.shape[0]
     half = outs // 2
     step = pl.program_id(0)
@@ -179,14 +187,14 @@
         return pl.CostEstimate(flops=flops, transcendentals=exps, bytes_accessed=size)
 
     def build(pts, gap, blk, before):
-        first = before is None
-        extra = [] if first else [before]
+        extra = [] if before is None else [before[1], before[0]]
         return pl.pallas_call(
-            functools.partial(build_kernel, gamma, first),
+            functools.partial(build_kernel, gamma, len(extra) // 2),
             grid=grid,
-            in_specs=[whole(pts.shape), whole(gap.shape), blocks(blk.shape[1])] + [whole(u_shape.shape)] * len(extra),
+            in_specs=[whole(pts.shape), whole(gap.shape), blocks(blk.shape[1])] + [whole(u_shape.shape), tiles][: len(extra)],
             out_specs=[tiles, whole(u_shape.shape)],
-            out_shape=[jax.ShapeDtypeStruct((n_ctr * LANES, n_pts), BF), u_shape],
+            out_shape=[jax.ShapeDtypeStruct((CORES * n_ctr * LANES, n_pts), BF), u_shape],
+            input_output_aliases={4: 0} if extra else {},
             scratch_shapes=[acc] + copies,
             compiler_params=PARAMS,
             cost_estimate=cost(2 * work * (dim + outs), work, 2 * work),
@@ -194,10 +202,9 @@
         )(pts, gap, blk, *extra)
 
     def apply(blk, tile, before):
-        first = before is None
-        extra = [] if first else [before]
+        extra = [] if before is None else [before]
         return pl.pallas_call(
-            functools.partial(apply_kernel, first),
+            functools.partial(apply_kernel, len(extra)),
             grid=grid,
             in_specs=[blocks(outs), tiles] + [whole(u_shape.shape)] * len(extra),
             out_specs=whole(u_shape.shape),
@@ -208,9 +215,9 @@
             name="apply_tile",
         )(blk, tile, *extra)
 
-    def back(u, tile, count):
+    def back(u, tile, half, count):
         return pl.pallas_call(
-            functools.partial(back_kernel, count),
+            functools.partial(back_kernel, half, count),
             grid=grid,
             in_specs=[whole(u.shape), tiles],
             out_specs=blocks(outs + RIDE),
@@ -225,9 +232,9 @@
         u = jnp.sum(exchange(u, "z"), axis=0).astype(BF)
         return spread(jnp.concatenate([u, pack(rows)], 0) if rows else u, "z")
 
-    def reduce_centres(u, tile, tile_other, count):
-        v = other_core(back(u, tile_other, count))
-        v = back(u, tile, count) + v
+    def reduce_centres(u, tile, count):
+        v = other_core(back(u, tile, 1, count))
+        v = back(u, tile, 0, count) + v
         v = jnp.sum(exchange(v, "ctr"), axis=0)
         return v[:outs] / total_points, jnp.sum(v[outs : outs + count + 1], axis=1)
 
@@ -241,11 +248,10 @@
     own = spread(jnp.concatenate([centres, p0.astype(BF)], 0), "ctr")
     other = other_core(own)
 
-    tile, u0 = build(pts, gap, own, None)
-    tile_other, u0 = build(pts, gap, other, u0)
+    tile, u0 = build(pts, gap, other, build(pts, gap, own, None))
     z0 = precondition(factor, residual)
     u0 = reduce_points(u0, [lanes(residual.T, z0.T), lanes(p0, p0)])
-    v0, s = reduce_centres(u0, tile, tile_other, 2)
+    v0, s = reduce_centres(u0, tile, 2)
     rz0 = s[0]
     q0 = v0 + RIDGE * p0
     alpha0 = rz0 / (s[2] / total_points + RIDGE * s[1])
@@ -262,9 +268,9 @@
     own = spread(p1.astype(BF), "ctr")
     other = other_core(own)
     u1 = apply(own, tile, None)
-    u1 = apply(other, tile_other, u1)
+    u1 = apply(other, tile, u1)
     u1 = reduce_points(u1, [])
-    v1, s = reduce_centres(u1, tile, tile_other, 0)
+    v1, s = reduce_centres(u1, tile, 0)
     q1 = v1 + RIDGE * p1
     alpha1 = rz1 / (s[0] / total_points + RIDGE * pp)
     x2 = solution + (alpha0 * p0 + alpha1 * p1).T

time: 276 us -> 270 us (0.978)
  local copies, waits for them, and re-layouts: 13.1 us -> 2.69 us
  Pallas kernels: 27.6 us -> 32 us
    unnamed x26 -> x10, local copies, waits for them, and re-layouts: 10.5 us -> 0.03 us
    pallas_call x8, Pallas kernels: 27.6 us -> 32 us  [the longest x4 14.1 us: back(): pl.pallas_call(functools.partial(back_kernel, half, count), grid=grid, in...]
  transfers between devices with their start and end apart: 8 -> 8, of which waited for: 4 -> 4; matrix products, arithmetic and copies ran while one was open for 4% -> 4% of each run, Pallas kernels for 5% -> 6%
where the time goes in v6:
time: 270 us; the launch traced here: 268 us
  blocking collectives  119 us (44%)
  starting transfers between devices  58.3 us (22%)
  waiting for transfers between devices  32.5 us (12%)
  Pallas kernels  32 us (12%)
  other arithmetic  15.4 us (6%)
  between operations  7.21 us (3%)
    all_to_all x7, blocking collectives, exchange(): return lax.all_to_all(blocks, axes, 0, 0, tiled=True)  119 us
    all_to_all x4, starting transfers between devices, exchange(): return lax.all_to_all(blocks, axes, 0, 0, tiled=True)  37.6 us
    all_to_all x4, waiting for transfers between devices, exchange(): return lax.all_to_all(blocks, axes, 0, 0, tiled=True)  32.5 us
    ppermute x4, starting transfers between devices, other_core(): return lax.ppermute(block, 'core', [(0, 1), (1, 0)])  20.7 us
    pallas_call x4, Pallas kernels, back(): pl.pallas_call(functools.partial(back_kernel, half, count), grid=grid, in...  14.1 us
    pallas_call x2, Pallas kernels, build(): pl.pallas_call(functools.partial(build_kernel, gamma, len(extra) // 2), g...  11.6 us
    another operation x2, other arithmetic, precondition(): lax.linalg.triangular_solve(factor, lower, left_side=True, lower=True, tr...  9.82 us
    pallas_call x2, Pallas kernels, apply(): pl.pallas_call(functools.partial(apply_kernel, len(extra)), grid=grid, in...  6.31 us
  transfers between devices with their start and end apart: 8, of which 4 were waited for; matrix products, arithmetic and copies ran while one was open for 4% of the time, Pallas kernels for 6%

profile of v6, /device:TPU:1, one launch (start us, length us, event | category | flops | bytes accessed | tf_op | source)
XLA Modules:
  0.0 268.4 jit_solution(9062927706050089149)
XLA Ops:
  0.6 0.8 bitcast_convert_fusion
  1.4 0.8 pad_maximum_fusion
  2.2 1.0 broadcast_in_dim.15
  3.2 7.7 %all-to-all-start.1 = ((bf16[16,192,128]{2,1,0:T(8,128)(2,1)}), bf16[16,192,128]{2,1,0:T(8,128)(2,1)S(1)}, u32[]{:S(2)}, u32[]{:S(2)}) async-start(bf16[16,192,128]{2,1,0:T(8,128)(2,1)} %broadcast_in_dim.15), calls=%async_computation.1 | async-start | bytes 1572864 | tf_op jit(solution)/shard_map/all_to_all | solution.py:34
  11.0 11.8 %all-to-all-done.1.blk_ref = bf16[16,192,128]{2,1,0:T(8,128)(2,1)S(1)} async-done(((bf16[16,192,128]{2,1,0:T(8,128)(2,1)}), bf16[16,192,128]{2,1,0:T(8,128)(2,1)S(1)}, u32[]{:S(2)}, u32[]{:S(2)}) %all-to-all-start.1) | async-done | bytes 786464 | tf_op jit(solution)/shard_map/all_to_all | solution.py:34
  23.5 16.3 %all-to-all-start = ((bf16[16,64,128]{2,1,0:T(8,128)(2,1)}), bf16[16,64,128]{2,1,0:T(8,128)(2,1)S(1)}, u32[]{:S(2)}, u32[]{:S(2)}) async-start(bf16[16,64,128]{2,1,0:T(8,128)(2,1)} %broadcast_in_dim.14), calls=%async_computation | async-start | bytes 524288 | tf_op jit(solution)/shard_map/all_to_all | solution.py:34
  39.8 4.5 %collective-permute-start = (bf16[16,192,128]{2,1,0:T(8,128)(2,1)S(1)}, bf16[16,192,128]{2,1,0:T(8,128)(2,1)S(1)}, u32[]{:S(2)}, u32[]{:S(2)}) collective-permute-start(bf16[16,192,128]{2,1,0:T(8,128)(2,1)S(1)} %all-to-all-done.1.blk_ref), channel_id=1, source_target_pairs={{0,16},{16,0},{1,17},{17,1},{2,18},{18,2},{3,19},{19,3},{4,20},{20... | collective-permute-start | bytes 2359304 | tf_op jit(solution)/shard_map/ppermute | solution.py:43
  44.3 8.3 %all-to-all-done = bf16[16,64,128]{2,1,0:T(8,128)(2,1)S(1)} async-done(((bf16[16,64,128]{2,1,0:T(8,128)(2,1)}), bf16[16,64,128]{2,1,0:T(8,128)(2,1)S(1)}, u32[]{:S(2)}, u32[]{:S(2)}) %all-to-all-start) | async-done | bytes 262176 | tf_op jit(solution)/shard_map/all_to_all | solution.py:34
  52.9 5.4 %build_tile.2 = (bf16[4096,1024]{1,0:T(8,128)(2,1)}, f32[16,32,128]{2,1,0:T(8,128)S(1)}) custom-call(bf16[1024,128]{1,0:T(8,128)(2,1)S(1)} %bitcast.88, f32[1,1024]{1,0:T(1,128)S(1)} %sub.72.gap_ref, bf16[16,192,128]{2,1,0:T(8,128)(2,1)S(1)} %all-to-all-done.1.blk_ref), custom_call_target="tpu_custom_call" | custom-call | flops 805306368 | bytes 4194304 | tf_op jit(solution)/shard_map/build_tile/pallas_call | solution.py:191
  58.3 6.2 %build_tile.3 = (bf16[4096,1024]{1,0:T(8,128)(2,1)}, f32[16,32,128]{2,1,0:T(8,128)}) custom-call(bf16[1024,128]{1,0:T(8,128)(2,1)S(1)} %bitcast.89, f32[1,1024]{1,0:T(1,128)S(1)} %sub.72.gap_ref, bf16[16,192,128]{2,1,0:T(8,128)(2,1)S(1)} %collective-permute-done.blk_ref, ...), custom_call_target="tpu_custom_call", output_to_operand_aliasing={{0}: (4, {})} | custom-call | flops 805306368 | bytes 4194304 | tf_op jit(solution)/shard_map/build_tile/pallas_call | solution.py:191
  64.5 10.0 %all-to-all-start.2 = ((f32[16,32,128]{2,1,0:T(8,128)}), f32[16,32,128]{2,1,0:T(8,128)S(1)}, u32[]{:S(2)}, u32[]{:S(2)}) async-start(f32[16,32,128]{2,1,0:T(8,128)} %get-tuple-element.10), calls=%async_computation.2 | async-start | bytes 524288 | tf_op jit(solution)/shard_map/all_to_all | solution.py:34
  74.5 9.8 %custom-call.9 = f32[1,128,128]{1,2,0:T(8,128)S(1)} custom-call(f32[1,128,128]{2,1,0:T(8,128)S(1)} %select_bitcast_fusion), custom_call_target="InvertDiagBlocksLowerTriangular" | custom-call | tf_op jit(solution)/shard_map/triangular_solve/custom-call.0 | solution.py:30
  85.0 2.3 all-to-all-done.2
  87.4 21.9 %all_to_all.55.u_ref = bf16[16,48,128]{2,1,0:T(8,128)(2,1)S(1)} all-to-all(bf16[16,48,128]{2,1,0:T(8,128)(2,1)S(1)} %broadcast_in_dim.16), channel_id=1, replica_groups=mesh['z'=16,'core'=2,'ctr'=16] {'z'}, dimensions={0} | all-to-all | bytes 393216 | tf_op jit(solution)/shard_map/all_to_all | solution.py:34
  109.3 3.5 %back_tile.5 = f32[16,72,128]{2,1,0:T(8,128)S(1)} custom-call(bf16[16,48,128]{2,1,0:T(8,128)(2,1)S(1)} %all_to_all.55.u_ref, bf16[4096,1024]{1,0:T(8,128)(2,1)} %get-tuple-element.11.tile_ref), custom_call_target="tpu_custom_call" | custom-call | flops 268435456 | bytes 4194304 | tf_op jit(solution)/shard_map/back_tile/pallas_call | solution.py:219
  112.9 7.4 %collective-permute-start.1 = (f32[16,72,128]{2,1,0:T(8,128)S(1)}, f32[16,72,128]{2,1,0:T(8,128)S(1)}, u32[]{:S(2)}, u32[]{:S(2)}) collective-permute-start(f32[16,72,128]{2,1,0:T(8,128)S(1)} %back_tile.5), channel_id=1, source_target_pairs={{0,16},{16,0},{1,17},{17,1},{2,18},{18,2},{3,19},{19,3},{4,20},{20... | collective-permute-start | bytes 1769480 | tf_op jit(solution)/shard_map/ppermute | solution.py:43
  120.2 3.5 %back_tile.4 = f32[16,72,128]{2,1,0:T(8,128)S(1)} custom-call(bf16[16,48,128]{2,1,0:T(8,128)(2,1)S(1)} %all_to_all.55.u_ref, bf16[4096,1024]{1,0:T(8,128)(2,1)} %get-tuple-element.11.tile_ref), custom_call_target="tpu_custom_call" | custom-call | flops 268435456 | bytes 4194304 | tf_op jit(solution)/shard_map/back_tile/pallas_call | solution.py:219
  123.9 18.1 %all_to_all.56 = f32[16,72,128]{2,1,0:T(8,128)S(1)} all-to-all(f32[16,72,128]{2,1,0:T(8,128)S(1)} %add.43), channel_id=1, replica_groups=mesh['z'=16,'core'=2,'ctr'=16] {'ctr'}, dimensions={0} | all-to-all | bytes 1179648 | tf_op jit(solution)/shard_map/all_to_all | solution.py:34
  145.3 16.0 %all_to_all.57 = f32[16,8,128]{2,1,0:T(8,128)S(1)} all-to-all(f32[16,8,128]{2,1,0:T(8,128)S(1)} %broadcast_in_dim.17), channel_id=1, replica_groups=mesh['z'=16,'core'=2,'ctr'=16] {'z'}, dimensions={0} | all-to-all | bytes 131072 | tf_op jit(solution)/shard_map/all_to_all | solution.py:34
  161.3 13.4 %all_to_all.58 = f32[32,8,128]{2,1,0:T(8,128)S(1)} all-to-all(f32[32,8,128]{2,1,0:T(8,128)S(1)} %broadcast_in_dim.18), channel_id=1, replica_groups=mesh['z'=16,'core'=2,'ctr'=16] {'core','ctr'}, dimensions={0} | all-to-all | bytes 262144 | tf_op jit(solution)/shard_map/all_to_all | solution.py:34
  176.6 11.1 %all_to_all.59.blk_ref = bf16[16,64,128]{2,1,0:T(8,128)(2,1)S(1)} all-to-all(bf16[16,64,128]{2,1,0:T(8,128)(2,1)S(1)} %broadcast_in_dim.19), channel_id=1, replica_groups=mesh['z'=16,'core'=2,'ctr'=16] {'ctr'}, dimensions={0} | all-to-all | bytes 524288 | tf_op jit(solution)/shard_map/all_to_all | solution.py:34
  187.7 3.4 %collective-permute-start.2 = (bf16[16,64,128]{2,1,0:T(8,128)(2,1)S(1)}, bf16[16,64,128]{2,1,0:T(8,128)(2,1)S(1)}, u32[]{:S(2)}, u32[]{:S(2)}) collective-permute-start(bf16[16,64,128]{2,1,0:T(8,128)(2,1)S(1)} %all_to_all.59.blk_ref), channel_id=1, source_target_pairs={{0,16},{16,0},{1,17},{17,1},{2,18},{18,2},{3,19},{19,3},{4,20},{20... | collective-permute-start | bytes 786440 | tf_op jit(solution)/shard_map/ppermute | solution.py:43
  191.1 3.1 %apply_tile.2.rest_0_ = f32[16,32,128]{2,1,0:T(8,128)S(1)} custom-call(bf16[16,64,128]{2,1,0:T(8,128)(2,1)S(1)} %all_to_all.59.blk_ref, bf16[4096,1024]{1,0:T(8,128)(2,1)} %get-tuple-element.11.tile_ref), custom_call_target="tpu_custom_call" | custom-call | flops 268435456 | bytes 4194304 | tf_op jit(solution)/shard_map/apply_tile/pallas_call | solution.py:206
  194.3 3.2 %apply_tile.3 = f32[16,32,128]{2,1,0:T(8,128)S(1)} custom-call(bf16[16,64,128]{2,1,0:T(8,128)(2,1)S(1)} %collective-permute-done.2.blk_ref, bf16[4096,1024]{1,0:T(8,128)(2,1)} %get-tuple-element.11.tile_ref, f32[16,32,128]{2,1,0:T(8,128)S(1)} %apply_tile.2.rest_0_), custom_call_target="tpu_custom_call" | custom-call | flops 268435456 | bytes 4194304 | tf_op jit(solution)/shard_map/apply_tile/pallas_call | solution.py:206
  197.5 17.1 %all_to_all.60 = f32[16,32,128]{2,1,0:T(8,128)S(1)} all-to-all(f32[16,32,128]{2,1,0:T(8,128)S(1)} %apply_tile.3), channel_id=1, replica_groups=mesh['z'=16,'core'=2,'ctr'=16] {'z'}, dimensions={0} | all-to-all | bytes 524288 | tf_op jit(solution)/shard_map/all_to_all | solution.py:34
  214.7 21.6 %all_to_all.61.u_ref = bf16[16,32,128]{2,1,0:T(8,128)(2,1)S(1)} all-to-all(bf16[16,32,128]{2,1,0:T(8,128)(2,1)S(1)} %broadcast_in_dim.20), channel_id=1, replica_groups=mesh['z'=16,'core'=2,'ctr'=16] {'z'}, dimensions={0} | all-to-all | bytes 262144 | tf_op jit(solution)/shard_map/all_to_all | solution.py:34
  236.2 3.5 %back_tile.7 = f32[16,72,128]{2,1,0:T(8,128)S(1)} custom-call(bf16[16,32,128]{2,1,0:T(8,128)(2,1)S(1)} %all_to_all.61.u_ref, bf16[4096,1024]{1,0:T(8,128)(2,1)} %get-tuple-element.11.tile_ref), custom_call_target="tpu_custom_call" | custom-call | flops 268435456 | bytes 4194304 | tf_op jit(solution)/shard_map/back_tile/pallas_call | solution.py:219
  239.8 5.5 %collective-permute-start.3 = (f32[16,72,128]{2,1,0:T(8,128)S(1)}, f32[16,72,128]{2,1,0:T(8,128)S(1)}, u32[]{:S(2)}, u32[]{:S(2)}) collective-permute-start(f32[16,72,128]{2,1,0:T(8,128)S(1)} %back_tile.7), channel_id=1, source_target_pairs={{0,16},{16,0},{1,17},{17,1},{2,18},{18,2},{3,19},{19,3},{4,20},{20... | collective-permute-start | bytes 1769480 | tf_op jit(solution)/shard_map/ppermute | solution.py:43
  245.2 3.5 %back_tile.6 = f32[16,72,128]{2,1,0:T(8,128)S(1)} custom-call(bf16[16,32,128]{2,1,0:T(8,128)(2,1)S(1)} %all_to_all.61.u_ref, bf16[4096,1024]{1,0:T(8,128)(2,1)} %get-tuple-element.11.tile_ref), custom_call_target="tpu_custom_call" | custom-call | flops 268435456 | bytes 4194304 | tf_op jit(solution)/shard_map/back_tile/pallas_call | solution.py:219
  248.8 0.9 add.47
  249.7 3.6 %all-to-all-start.10 = ((f32[16,72,128]{2,1,0:T(8,128)}), f32[16,72,128]{2,1,0:T(8,128)S(1)}, u32[]{:S(2)}, u32[]{:S(2)}) async-start(f32[16,72,128]{2,1,0:T(8,128)} %add.47), calls=%async_computation.10 | async-start | bytes 1179648 | tf_op jit(solution)/shard_map/all_to_all | solution.py:34
  255.2 10.1 %all-to-all-done.10 = f32[16,72,128]{2,1,0:T(8,128)S(1)} async-done(((f32[16,72,128]{2,1,0:T(8,128)}), f32[16,72,128]{2,1,0:T(8,128)S(1)}, u32[]{:S(2)}, u32[]{:S(2)}) %all-to-all-start.10) | async-done | bytes 589856 | tf_op jit(solution)/shard_map/all_to_all | solution.py:34
  (53 shorter events, 5.9 us)
Async XLA Ops:
  0.6 10.3 %copy-start = (bf16[1024,128]{1,0:T(8,128)(2,1)S(1)}, bf16[1024,128]{1,0:T(8,128)(2,1)}, u32[]{:S(2)}) copy-start(bf16[1024,128]{1,0:T(8,128)(2,1)} %param.10) | copy-start | bytes 786436
  3.2 71.2 %copy-start.3 = (f32[128,128]{1,0:T(8,128)S(1)}, f32[128,128]{1,0:T(8,128)}, u32[]{:S(2)}) copy-start(f32[128,128]{1,0:T(8,128)} %param.12) | copy-start | bytes 196612
  3.2 81.1 %copy-start.1 = (f32[128,64]{0,1:T(8,128)S(1)}, f32[128,64]{0,1:T(8,128)}, u32[]{:S(2)}) copy-start(f32[128,64]{0,1:T(8,128)} %param.15) | copy-start | bytes 98308
  3.2 81.1 %copy-start.2 = (f32[128,64]{0,1:T(8,128)S(1)}, f32[128,64]{0,1:T(8,128)}, u32[]{:S(2)}) copy-start(f32[128,64]{0,1:T(8,128)} %param.14) | copy-start | bytes 98308
  3.2 19.5 %all-to-all-start.1 = ((bf16[16,192,128]{2,1,0:T(8,128)(2,1)}), bf16[16,192,128]{2,1,0:T(8,128)(2,1)S(1)}, u32[]{:S(2)}, u32[]{:S(2)}) async-start(bf16[16,192,128]{2,1,0:T(8,128)(2,1)} %broadcast_in_dim.15), calls=%async_computation.1 | async-start | bytes 1572864 | tf_op jit(solution)/shard_map/all_to_all | solution.py:34
  23.5 29.1 %all-to-all-start = ((bf16[16,64,128]{2,1,0:T(8,128)(2,1)}), bf16[16,64,128]{2,1,0:T(8,128)(2,1)S(1)}, u32[]{:S(2)}, u32[]{:S(2)}) async-start(bf16[16,64,128]{2,1,0:T(8,128)(2,1)} %broadcast_in_dim.14), calls=%async_computation | async-start | bytes 524288 | tf_op jit(solution)/shard_map/all_to_all | solution.py:34
  39.8 18.5 %collective-permute-start = (bf16[16,192,128]{2,1,0:T(8,128)(2,1)S(1)}, bf16[16,192,128]{2,1,0:T(8,128)(2,1)S(1)}, u32[]{:S(2)}, u32[]{:S(2)}) collective-permute-start(bf16[16,192,128]{2,1,0:T(8,128)(2,1)S(1)} %all-to-all-done.1.blk_ref), channel_id=1, source_target_pairs={{0,16},{16,0},{1,17},{17,1},{2,18},{18,2},{3,19},{19,3},{4,20},{20... | collective-permute-start | bytes 2359304 | tf_op jit(solution)/shard_map/ppermute | solution.py:43
  64.5 22.8 %all-to-all-start.2 = ((f32[16,32,128]{2,1,0:T(8,128)}), f32[16,32,128]{2,1,0:T(8,128)S(1)}, u32[]{:S(2)}, u32[]{:S(2)}) async-start(f32[16,32,128]{2,1,0:T(8,128)} %get-tuple-element.10), calls=%async_computation.2 | async-start | bytes 524288 | tf_op jit(solution)/shard_map/all_to_all | solution.py:34
  112.9 10.9 %collective-permute-start.1 = (f32[16,72,128]{2,1,0:T(8,128)S(1)}, f32[16,72,128]{2,1,0:T(8,128)S(1)}, u32[]{:S(2)}, u32[]{:S(2)}) collective-permute-start(f32[16,72,128]{2,1,0:T(8,128)S(1)} %back_tile.5), channel_id=1, source_target_pairs={{0,16},{16,0},{1,17},{17,1},{2,18},{18,2},{3,19},{19,3},{4,20},{20... | collective-permute-start | bytes 1769480 | tf_op jit(solution)/shard_map/ppermute | solution.py:43
  187.7 6.6 %collective-permute-start.2 = (bf16[16,64,128]{2,1,0:T(8,128)(2,1)S(1)}, bf16[16,64,128]{2,1,0:T(8,128)(2,1)S(1)}, u32[]{:S(2)}, u32[]{:S(2)}) collective-permute-start(bf16[16,64,128]{2,1,0:T(8,128)(2,1)S(1)} %all_to_all.59.blk_ref), channel_id=1, source_target_pairs={{0,16},{16,0},{1,17},{17,1},{2,18},{18,2},{3,19},{19,3},{4,20},{20... | collective-permute-start | bytes 786440 | tf_op jit(solution)/shard_map/ppermute | solution.py:43
  239.7 28.1 %copy-start.4 = (f32[128,64]{0,1:T(8,128)S(1)}, f32[128,64]{0,1:T(8,128)}, u32[]{:S(2)}) copy-start(f32[128,64]{0,1:T(8,128)} %param.13) | copy-start | bytes 98308
  239.8 9.0 %collective-permute-start.3 = (f32[16,72,128]{2,1,0:T(8,128)S(1)}, f32[16,72,128]{2,1,0:T(8,128)S(1)}, u32[]{:S(2)}, u32[]{:S(2)}) collective-permute-start(f32[16,72,128]{2,1,0:T(8,128)S(1)} %back_tile.7), channel_id=1, source_target_pairs={{0,16},{16,0},{1,17},{17,1},{2,18},{18,2},{3,19},{19,3},{4,20},{20... | collective-permute-start | bytes 1769480 | tf_op jit(solution)/shard_map/ppermute | solution.py:43
  249.7 15.7 %all-to-all-start.10 = ((f32[16,72,128]{2,1,0:T(8,128)}), f32[16,72,128]{2,1,0:T(8,128)S(1)}, u32[]{:S(2)}, u32[]{:S(2)}) async-start(f32[16,72,128]{2,1,0:T(8,128)} %add.47), calls=%async_computation.10 | async-start | bytes 1179648 | tf_op jit(solution)/shard_map/all_to_all | solution.py:34

commit v7 on v6

--- a/solution.py
+++ b/solution.py
@@ -109,9 +109,10 @@
     tile_ref = half_of(tile_ref, half)
     step = pl.program_id(0)
     dim = pts_ref.shape[1]
+    outs = acc.shape[0]
     blk = blk_ref[...]
     cen = jnp.concatenate([blk[g, :LANES] for g in range(GROUP)], axis=0)
-    vec = jnp.concatenate([blk[g, LANES:] for g in range(GROUP)], axis=1)
+    vec = jnp.concatenate([blk[g, LANES : LANES + outs] for g in range(GROUP)], axis=1)
     wide = cen.astype(F32)
     gap_c = dim - jnp.sum(wide * wide, axis=1, keepdims=True)
     cross = lax.dot_general(cen, pts_ref[...], (((1,), (1,)), ((), ())), preferred_element_type=F32)
@@ -127,15 +128,19 @@
             tile_copy(buf, tile_ref, sems, at).wait()
 
 
-def apply_kernel(half, blk_ref, tile_ref, *rest):
+def apply_kernel(half, beta_ref, z_ref, p_ref, tile_ref, *rest):
     before_ref = rest[0] if half else None
     tile_ref = half_of(tile_ref, half)
     u_ref, acc, buf, sems = rest[-4:]
     step = pl.program_id(0)
     tile = fetch(step, tile_ref, buf, sems)
-    blk = blk_ref[...]
-    vec = jnp.concatenate([blk[g] for g in range(GROUP)], axis=1)
-    part = jnp.dot(vec, tile, preferred_element_type=F32)
+    outs = acc.shape[0]
+    vec = []
+    for g in range(GROUP):
+        high = p_ref[g, LANES : LANES + outs].astype(F32)
+        low = p_ref[g, LANES + outs :].astype(F32)
+        vec.append((z_ref[g, :outs] + beta_ref[...] * (high + low)).astype(BF))
+    part = jnp.dot(jnp.concatenate(vec, axis=1), tile, preferred_element_type=F32)
     add_up(step, part, before_ref, u_ref, acc)
 
 
@@ -201,19 +206,19 @@
             name="build_tile",
         )(pts, gap, blk, *extra)
 
-    def apply(blk, tile, before):
+    def apply(beta, z, p, tile, before):
         extra = [] if before is None else [before]
         return pl.pallas_call(
             functools.partial(apply_kernel, len(extra)),
             grid=grid,
-            in_specs=[blocks(outs), tiles] + [whole(u_shape.shape)] * len(extra),
+            in_specs=[whole(beta.shape), blocks(z.shape[1]), blocks(p.shape[1]), tiles] + [whole(u_shape.shape)] * len(extra),
             out_specs=whole(u_shape.shape),
             out_shape=u_shape,
             scratch_shapes=[acc] + copies,
             compiler_params=PARAMS,
             cost_estimate=cost(2 * work * outs, 0, 2 * work),
             name="apply_tile",
-        )(blk, tile, *extra)
+        )(beta, z, p, tile, *extra)
 
     def back(u, tile, half, count):
         return pl.pallas_call(
@@ -245,7 +250,9 @@
     pts = spread(mine, "z").reshape(n_pts, dim)
     gap = row_gaps(pts)[None]
     p0 = direction.T
-    own = spread(jnp.concatenate([centres, p0.astype(BF)], 0), "ctr")
+    p0_high = lax.reduce_precision(p0, 8, 7)
+    parts = [centres, p0_high.astype(BF), (p0 - p0_high).astype(BF)]
+    own = spread(jnp.concatenate(parts, 0), "ctr")
     other = other_core(own)
 
     tile, u0 = build(pts, gap, other, build(pts, gap, own, None))
@@ -257,18 +264,19 @@
     alpha0 = rz0 / (s[2] / total_points + RIDGE * s[1])
     r1 = residual.T - alpha0 * q0
     z1 = precondition(factor, r1.T).T
-    block = jnp.stack([lanes(r1, z1), lanes(z1, z1), lanes(z1, p0)] + [jnp.zeros((LANES,), F32)] * (RIDE - 3))
-    for axes in ("z", ("core", "ctr")):
-        block = jnp.sum(spread(block, axes), axis=0)
+    zeros = [jnp.zeros((LANES,), F32)] * (RIDE - 3)
+    block = jnp.stack([lanes(r1, z1), lanes(z1, z1), lanes(z1, p0)] + zeros)
+    own_z = spread(jnp.concatenate([z1, block], 0), "ctr")
+    other_z = other_core(own_z)
+    block = jnp.sum(spread(jnp.sum(own_z[:, outs:], axis=0), ("z", "core")), axis=0)
     rz1, zz, zp = [jnp.sum(block[k]) for k in range(3)]
     beta = rz1 / rz0
     p1 = z1 + beta * p0
     pp = zz + beta * (2.0 * zp + beta * s[1])
 
-    own = spread(p1.astype(BF), "ctr")
-    other = other_core(own)
-    u1 = apply(own, tile, None)
-    u1 = apply(other, tile, u1)
+    rate = jnp.broadcast_to(beta, (1, LANES))
+    u1 = apply(rate, own_z, own, tile, None)
+    u1 = apply(rate, other_z, other, tile, u1)
     u1 = reduce_points(u1, [])
     v1, s = reduce_centres(u1, tile, 0)
     q1 = v1 + RIDGE * p1

time: 270 us -> 270 us (level)
  blocking collectives: 119 us -> 92.4 us
  waiting for transfers between devices: 32.5 us -> 48.5 us
  starting transfers between devices: 58.3 us -> 64.6 us
  Pallas kernels: 32 us -> 35.1 us
    all_to_all x7 -> x5, blocking collectives: 119 us -> 92.4 us  [exchange(): return lax.all_to_all(blocks, axes, 0, 0, tiled=True)]
    all_to_all x4 -> x5, waiting for transfers between devices: 32.5 us -> 48.5 us  [exchange(): return lax.all_to_all(blocks, axes, 0, 0, tiled=True)]
    all_to_all x4 -> x5, starting transfers between devices: 37.6 us -> 44.7 us  [exchange(): return lax.all_to_all(blocks, axes, 0, 0, tiled=True)]
    pallas_call x2, Pallas kernels: 6.31 us -> 9.42 us  [apply(): pl.pallas_call(functools.partial(apply_kernel, len(extra)), grid=grid, in...]
  transfers between devices with their start and end apart: 8 -> 9, of which waited for: 4 -> 5; matrix products, arithmetic and copies ran while one was open for 4% -> 4% of each run, Pallas kernels for 6% -> 6%
where the time goes in v7:
time: 270 us; the launch traced here: 268 us
  blocking collectives  92.4 us (34%)
  starting transfers between devices  64.6 us (24%)
  waiting for transfers between devices  48.5 us (18%)
  Pallas kernels  35.1 us (13%)
  other arithmetic  15.4 us (6%)
  between operations  7.64 us (3%)
  local copies, waits for them, and re-layouts  3.58 us (1%)
    all_to_all x5, blocking collectives, exchange(): return lax.all_to_all(blocks, axes, 0, 0, tiled=True)  92.4 us
    all_to_all x5, waiting for transfers between devices, exchange(): return lax.all_to_all(blocks, axes, 0, 0, tiled=True)  48.5 us
    all_to_all x5, starting transfers between devices, exchange(): return lax.all_to_all(blocks, axes, 0, 0, tiled=True)  44.7 us
    ppermute x4, starting transfers between devices, other_core(): return lax.ppermute(block, 'core', [(0, 1), (1, 0)])  19.9 us
    pallas_call x4, Pallas kernels, back(): pl.pallas_call(functools.partial(back_kernel, half, count), grid=grid, in...  14.1 us
    pallas_call x2, Pallas kernels, build(): pl.pallas_call(functools.partial(build_kernel, gamma, len(extra) // 2), g...  11.6 us
    another operation x2, other arithmetic, precondition(): lax.linalg.triangular_solve(factor, lower, left_side=True, lower=True, tr...  9.82 us
    pallas_call x2, Pallas kernels, apply(): pl.pallas_call(functools.partial(apply_kernel, len(extra)), grid=grid, in...  9.42 us
  transfers between devices with their start and end apart: 9, of which 5 were waited for; matrix products, arithmetic and copies ran while one was open for 4% of the time, Pallas kernels for 6%

profile of v7, /device:TPU:1, one launch (start us, length us, event | category | flops | bytes accessed | tf_op | source)
XLA Modules:
  0.0 268.4 jit_solution(17646674083882849493)
XLA Ops:
  0.6 0.8 fusion.18
  1.5 0.8 pad_maximum_fusion
  2.2 1.2 broadcast_in_dim.15
  3.4 7.7 %all-to-all-start.1 = ((bf16[16,256,128]{2,1,0:T(8,128)(2,1)}), bf16[16,256,128]{2,1,0:T(8,128)(2,1)S(1)}, u32[]{:S(2)}, u32[]{:S(2)}) async-start(bf16[16,256,128]{2,1,0:T(8,128)(2,1)} %broadcast_in_dim.15), calls=%async_computation.1 | async-start | bytes 2097152 | tf_op jit(solution)/shard_map/all_to_all | solution.py:34
  11.2 14.4 %all-to-all-done.1.blk_ref.p_ref = bf16[16,256,128]{2,1,0:T(8,128)(2,1)S(1)} async-done(((bf16[16,256,128]{2,1,0:T(8,128)(2,1)}), bf16[16,256,128]{2,1,0:T(8,128)(2,1)S(1)}, u32[]{:S(2)}, u32[]{:S(2)}) %all-to-all-start.1) | async-done | bytes 1048608 | tf_op jit(solution)/shard_map/all_to_all | solution.py:34
  26.4 16.4 %all-to-all-start = ((bf16[16,64,128]{2,1,0:T(8,128)(2,1)}), bf16[16,64,128]{2,1,0:T(8,128)(2,1)S(1)}, u32[]{:S(2)}, u32[]{:S(2)}) async-start(bf16[16,64,128]{2,1,0:T(8,128)(2,1)} %broadcast_in_dim.14), calls=%async_computation | async-start | bytes 524288 | tf_op jit(solution)/shard_map/all_to_all | solution.py:34
  42.8 4.8 %collective-permute-start = (bf16[16,256,128]{2,1,0:T(8,128)(2,1)S(1)}, bf16[16,256,128]{2,1,0:T(8,128)(2,1)S(1)}, u32[]{:S(2)}, u32[]{:S(2)}) collective-permute-start(bf16[16,256,128]{2,1,0:T(8,128)(2,1)S(1)} %all-to-all-done.1.blk_ref.p_ref), channel_id=1, source_target_pairs={{0,16},{16,0},{1,17},{17,1},{2,18},{18,2},{3,19},{19,3},{4,20},{20... | collective-permute-start | bytes 3145736 | tf_op jit(solution)/shard_map/ppermute | solution.py:43
  47.6 8.0 %all-to-all-done = bf16[16,64,128]{2,1,0:T(8,128)(2,1)S(1)} async-done(((bf16[16,64,128]{2,1,0:T(8,128)(2,1)}), bf16[16,64,128]{2,1,0:T(8,128)(2,1)S(1)}, u32[]{:S(2)}, u32[]{:S(2)}) %all-to-all-start) | async-done | bytes 262176 | tf_op jit(solution)/shard_map/all_to_all | solution.py:34
  55.9 5.4 %build_tile.2 = (bf16[4096,1024]{1,0:T(8,128)(2,1)}, f32[16,32,128]{2,1,0:T(8,128)S(1)}) custom-call(bf16[1024,128]{1,0:T(8,128)(2,1)S(1)} %bitcast.81, f32[1,1024]{1,0:T(1,128)S(1)} %sub.75.gap_ref, bf16[16,256,128]{2,1,0:T(8,128)(2,1)S(1)} %all-to-all-done.1.blk_ref.p_ref), custom_call_target="tpu_custom_call" | custom-call | flops 805306368 | bytes 4194304 | tf_op jit(solution)/shard_map/build_tile/pallas_call | solution.py:196
  61.3 6.2 %build_tile.3 = (bf16[4096,1024]{1,0:T(8,128)(2,1)}, f32[16,32,128]{2,1,0:T(8,128)}) custom-call(bf16[1024,128]{1,0:T(8,128)(2,1)S(1)} %bitcast.82, f32[1,1024]{1,0:T(1,128)S(1)} %sub.75.gap_ref, bf16[16,256,128]{2,1,0:T(8,128)(2,1)S(1)} %collective-permute-done.blk_ref.p_ref, ...), custom_call_target="tpu_custom_call", output_to_operand_aliasing={{0}: (4, {})} | custom-call | flops 805306368 | bytes 4194304 | tf_op jit(solution)/shard_map/build_tile/pallas_call | solution.py:196
  67.5 10.0 %all-to-all-start.2 = ((f32[16,32,128]{2,1,0:T(8,128)}), f32[16,32,128]{2,1,0:T(8,128)S(1)}, u32[]{:S(2)}, u32[]{:S(2)}) async-start(f32[16,32,128]{2,1,0:T(8,128)} %get-tuple-element.10), calls=%async_computation.2 | async-start | bytes 524288 | tf_op jit(solution)/shard_map/all_to_all | solution.py:34
  77.6 9.8 %custom-call.9 = f32[1,128,128]{1,2,0:T(8,128)S(1)} custom-call(f32[1,128,128]{2,1,0:T(8,128)S(1)} %select_bitcast_fusion), custom_call_target="InvertDiagBlocksLowerTriangular" | custom-call | tf_op jit(solution)/shard_map/triangular_solve/custom-call.0 | solution.py:30
  88.0 2.3 all-to-all-done.2
  90.4 21.4 %all_to_all.50.u_ref = bf16[16,48,128]{2,1,0:T(8,128)(2,1)S(1)} all-to-all(bf16[16,48,128]{2,1,0:T(8,128)(2,1)S(1)} %broadcast_in_dim.16), channel_id=1, replica_groups=mesh['z'=16,'core'=2,'ctr'=16] {'z'}, dimensions={0} | all-to-all | bytes 393216 | tf_op jit(solution)/shard_map/all_to_all | solution.py:34
  111.8 3.5 %back_tile.5 = f32[16,72,128]{2,1,0:T(8,128)S(1)} custom-call(bf16[16,48,128]{2,1,0:T(8,128)(2,1)S(1)} %all_to_all.50.u_ref, bf16[4096,1024]{1,0:T(8,128)(2,1)} %get-tuple-element.11.tile_ref), custom_call_target="tpu_custom_call" | custom-call | flops 268435456 | bytes 4194304 | tf_op jit(solution)/shard_map/back_tile/pallas_call | solution.py:224
  115.4 7.4 %collective-permute-start.1 = (f32[16,72,128]{2,1,0:T(8,128)S(1)}, f32[16,72,128]{2,1,0:T(8,128)S(1)}, u32[]{:S(2)}, u32[]{:S(2)}) collective-permute-start(f32[16,72,128]{2,1,0:T(8,128)S(1)} %back_tile.5), channel_id=1, source_target_pairs={{0,16},{16,0},{1,17},{17,1},{2,18},{18,2},{3,19},{19,3},{4,20},{20... | collective-permute-start | bytes 1769480 | tf_op jit(solution)/shard_map/ppermute | solution.py:43
  122.8 3.5 %back_tile.4 = f32[16,72,128]{2,1,0:T(8,128)S(1)} custom-call(bf16[16,48,128]{2,1,0:T(8,128)(2,1)S(1)} %all_to_all.50.u_ref, bf16[4096,1024]{1,0:T(8,128)(2,1)} %get-tuple-element.11.tile_ref), custom_call_target="tpu_custom_call" | custom-call | flops 268435456 | bytes 4194304 | tf_op jit(solution)/shard_map/back_tile/pallas_call | solution.py:224
  126.4 19.0 %all_to_all.51 = f32[16,72,128]{2,1,0:T(8,128)S(1)} all-to-all(f32[16,72,128]{2,1,0:T(8,128)S(1)} %add.43), channel_id=1, replica_groups=mesh['z'=16,'core'=2,'ctr'=16] {'ctr'}, dimensions={0} | all-to-all | bytes 1179648 | tf_op jit(solution)/shard_map/all_to_all | solution.py:34
  148.9 14.1 %all_to_all.52.z_ref = f32[16,72,128]{2,1,0:T(8,128)S(1)} all-to-all(f32[16,72,128]{2,1,0:T(8,128)S(1)} %broadcast_in_dim.17), channel_id=1, replica_groups=mesh['z'=16,'core'=2,'ctr'=16] {'ctr'}, dimensions={0} | all-to-all | bytes 1179648 | tf_op jit(solution)/shard_map/all_to_all | solution.py:34
  163.7 7.0 %all-to-all-start.6 = ((f32[32,8,128]{2,1,0:T(8,128)}), f32[32,8,128]{2,1,0:T(8,128)S(1)}, u32[]{:S(2)}, u32[]{:S(2)}) async-start(f32[32,8,128]{2,1,0:T(8,128)} %broadcast_in_dim.18), calls=%async_computation.6 | async-start | bytes 262144 | tf_op jit(solution)/shard_map/all_to_all | solution.py:34
  170.7 2.1 collective-permute-start.2
  172.9 13.7 %all-to-all-done.6 = f32[32,8,128]{2,1,0:T(8,128)S(1)} async-done(((f32[32,8,128]{2,1,0:T(8,128)}), f32[32,8,128]{2,1,0:T(8,128)S(1)}, u32[]{:S(2)}, u32[]{:S(2)}) %all-to-all-start.6) | async-done | bytes 131104 | tf_op jit(solution)/shard_map/all_to_all | solution.py:34
  188.7 3.2 %apply_tile.2.rest_0_ = f32[16,32,128]{2,1,0:T(8,128)S(1)} custom-call(f32[1,128]{1,0:T(1,128)S(1)} %broadcast_in_dim.19.beta_ref, f32[16,72,128]{2,1,0:T(8,128)S(1)} %all_to_all.52.z_ref, bf16[16,256,128]{2,1,0:T(8,128)(2,1)S(1)} %all-to-all-done.1.blk_ref.p_ref, bf16[4096,1024]{1,0:T(8,128)(2,1)} %get-tuple-element.11.tile_ref), custom_call_target="tpu_custom_call" | custom-call | flops 268435456 | bytes 4194304 | tf_op jit(solution)/shard_map/apply_tile/pallas_call | solution.py:211
  191.8 6.3 %apply_tile.3 = f32[16,32,128]{2,1,0:T(8,128)S(1)} custom-call(f32[1,128]{1,0:T(1,128)S(1)} %broadcast_in_dim.19.beta_ref, f32[16,72,128]{2,1,0:T(8,128)S(1)} %collective-permute-done.2.z_ref, bf16[16,256,128]{2,1,0:T(8,128)(2,1)} %copy-done.1, bf16[4096,1024]{1,0:T(8,128)(2,1)} %get-tuple-element.11.tile_ref, f32[16,32,128]{2,1,0:T(8,128)S(1)} %apply_tile.2.rest_0_), custom_call_target="tpu_custom_call" | custom-call | flops 268435456 | bytes 4194304 | tf_op jit(solution)/shard_map/apply_tile/pallas_call | solution.py:211
  198.1 15.4 %all_to_all.53 = f32[16,32,128]{2,1,0:T(8,128)S(1)} all-to-all(f32[16,32,128]{2,1,0:T(8,128)S(1)} %apply_tile.3), channel_id=1, replica_groups=mesh['z'=16,'core'=2,'ctr'=16] {'z'}, dimensions={0} | all-to-all | bytes 524288 | tf_op jit(solution)/shard_map/all_to_all | solution.py:34
  213.6 22.5 %all_to_all.54.u_ref = bf16[16,32,128]{2,1,0:T(8,128)(2,1)S(1)} all-to-all(bf16[16,32,128]{2,1,0:T(8,128)(2,1)S(1)} %broadcast_in_dim.20), channel_id=1, replica_groups=mesh['z'=16,'core'=2,'ctr'=16] {'z'}, dimensions={0} | all-to-all | bytes 262144 | tf_op jit(solution)/shard_map/all_to_all | solution.py:34
  236.1 3.5 %back_tile.7 = f32[16,72,128]{2,1,0:T(8,128)S(1)} custom-call(bf16[16,32,128]{2,1,0:T(8,128)(2,1)S(1)} %all_to_all.54.u_ref, bf16[4096,1024]{1,0:T(8,128)(2,1)} %get-tuple-element.11.tile_ref), custom_call_target="tpu_custom_call" | custom-call | flops 268435456 | bytes 4194304 | tf_op jit(solution)/shard_map/back_tile/pallas_call | solution.py:224
  239.6 5.5 %collective-permute-start.3 = (f32[16,72,128]{2,1,0:T(8,128)S(1)}, f32[16,72,128]{2,1,0:T(8,128)S(1)}, u32[]{:S(2)}, u32[]{:S(2)}) collective-permute-start(f32[16,72,128]{2,1,0:T(8,128)S(1)} %back_tile.7), channel_id=1, source_target_pairs={{0,16},{16,0},{1,17},{17,1},{2,18},{18,2},{3,19},{19,3},{4,20},{20... | collective-permute-start | bytes 1769480 | tf_op jit(solution)/shard_map/ppermute | solution.py:43
  245.1 3.5 %back_tile.6 = f32[16,72,128]{2,1,0:T(8,128)S(1)} custom-call(bf16[16,32,128]{2,1,0:T(8,128)(2,1)S(1)} %all_to_all.54.u_ref, bf16[4096,1024]{1,0:T(8,128)(2,1)} %get-tuple-element.11.tile_ref), custom_call_target="tpu_custom_call" | custom-call | flops 268435456 | bytes 4194304 | tf_op jit(solution)/shard_map/back_tile/pallas_call | solution.py:224
  248.6 0.9 add.46
  249.5 3.6 %all-to-all-start.9 = ((f32[16,72,128]{2,1,0:T(8,128)}), f32[16,72,128]{2,1,0:T(8,128)S(1)}, u32[]{:S(2)}, u32[]{:S(2)}) async-start(f32[16,72,128]{2,1,0:T(8,128)} %add.46), calls=%async_computation.9 | async-start | bytes 1179648 | tf_op jit(solution)/shard_map/all_to_all | solution.py:34
  255.1 10.1 %all-to-all-done.9 = f32[16,72,128]{2,1,0:T(8,128)S(1)} async-done(((f32[16,72,128]{2,1,0:T(8,128)}), f32[16,72,128]{2,1,0:T(8,128)S(1)}, u32[]{:S(2)}, u32[]{:S(2)}) %all-to-all-start.9) | async-done | bytes 589856 | tf_op jit(solution)/shard_map/all_to_all | solution.py:34
  (53 shorter events, 6.7 us)
Async XLA Ops:
  0.6 10.5 %copy-start = (bf16[1024,128]{1,0:T(8,128)(2,1)S(1)}, bf16[1024,128]{1,0:T(8,128)(2,1)}, u32[]{:S(2)}) copy-start(bf16[1024,128]{1,0:T(8,128)(2,1)} %param.10) | copy-start | bytes 786436
  3.4 74.1 %copy-start.4 = (f32[128,128]{1,0:T(8,128)S(1)}, f32[128,128]{1,0:T(8,128)}, u32[]{:S(2)}) copy-start(f32[128,128]{1,0:T(8,128)} %param.12) | copy-start | bytes 196612
  3.4 22.2 %all-to-all-start.1 = ((bf16[16,256,128]{2,1,0:T(8,128)(2,1)}), bf16[16,256,128]{2,1,0:T(8,128)(2,1)S(1)}, u32[]{:S(2)}, u32[]{:S(2)}) async-start(bf16[16,256,128]{2,1,0:T(8,128)(2,1)} %broadcast_in_dim.15), calls=%async_computation.1 | async-start | bytes 2097152 | tf_op jit(solution)/shard_map/all_to_all | solution.py:34
  11.2 76.2 %copy-start.3 = (f32[128,64]{0,1:T(8,128)S(1)}, f32[128,64]{0,1:T(8,128)}, u32[]{:S(2)}) copy-start(f32[128,64]{0,1:T(8,128)} %param.14) | copy-start | bytes 98308
  26.4 29.2 %all-to-all-start = ((bf16[16,64,128]{2,1,0:T(8,128)(2,1)}), bf16[16,64,128]{2,1,0:T(8,128)(2,1)S(1)}, u32[]{:S(2)}, u32[]{:S(2)}) async-start(bf16[16,64,128]{2,1,0:T(8,128)(2,1)} %broadcast_in_dim.14), calls=%async_computation | async-start | bytes 524288 | tf_op jit(solution)/shard_map/all_to_all | solution.py:34
  42.8 18.5 %collective-permute-start = (bf16[16,256,128]{2,1,0:T(8,128)(2,1)S(1)}, bf16[16,256,128]{2,1,0:T(8,128)(2,1)S(1)}, u32[]{:S(2)}, u32[]{:S(2)}) collective-permute-start(bf16[16,256,128]{2,1,0:T(8,128)(2,1)S(1)} %all-to-all-done.1.blk_ref.p_ref), channel_id=1, source_target_pairs={{0,16},{16,0},{1,17},{17,1},{2,18},{18,2},{3,19},{19,3},{4,20},{20... | collective-permute-start | bytes 3145736 | tf_op jit(solution)/shard_map/ppermute | solution.py:43
  61.3 54.0 %copy-start.1 = (bf16[16,256,128]{2,1,0:T(8,128)(2,1)}, bf16[16,256,128]{2,1,0:T(8,128)(2,1)S(1)}, u32[]{:S(2)}) copy-start(bf16[16,256,128]{2,1,0:T(8,128)(2,1)S(1)} %collective-permute-done.blk_ref.p_ref) | copy-start | bytes 3145732
  67.5 22.8 %all-to-all-start.2 = ((f32[16,32,128]{2,1,0:T(8,128)}), f32[16,32,128]{2,1,0:T(8,128)S(1)}, u32[]{:S(2)}, u32[]{:S(2)}) async-start(f32[16,32,128]{2,1,0:T(8,128)} %get-tuple-element.10), calls=%async_computation.2 | async-start | bytes 524288 | tf_op jit(solution)/shard_map/all_to_all | solution.py:34
  115.4 32.9 %copy-start.2 = (f32[128,64]{0,1:T(8,128)S(1)}, f32[128,64]{0,1:T(8,128)}, u32[]{:S(2)}) copy-start(f32[128,64]{0,1:T(8,128)} %param.15) | copy-start | bytes 98308
  115.4 11.0 %collective-permute-start.1 = (f32[16,72,128]{2,1,0:T(8,128)S(1)}, f32[16,72,128]{2,1,0:T(8,128)S(1)}, u32[]{:S(2)}, u32[]{:S(2)}) collective-permute-start(f32[16,72,128]{2,1,0:T(8,128)S(1)} %back_tile.5), channel_id=1, source_target_pairs={{0,16},{16,0},{1,17},{17,1},{2,18},{18,2},{3,19},{19,3},{4,20},{20... | collective-permute-start | bytes 1769480 | tf_op jit(solution)/shard_map/ppermute | solution.py:43
  163.7 22.9 %all-to-all-start.6 = ((f32[32,8,128]{2,1,0:T(8,128)}), f32[32,8,128]{2,1,0:T(8,128)S(1)}, u32[]{:S(2)}, u32[]{:S(2)}) async-start(f32[32,8,128]{2,1,0:T(8,128)} %broadcast_in_dim.18), calls=%async_computation.6 | async-start | bytes 262144 | tf_op jit(solution)/shard_map/all_to_all | solution.py:34
  170.7 21.1 %collective-permute-start.2 = (f32[16,72,128]{2,1,0:T(8,128)S(1)}, f32[16,72,128]{2,1,0:T(8,128)S(1)}, u32[]{:S(2)}, u32[]{:S(2)}) collective-permute-start(f32[16,72,128]{2,1,0:T(8,128)S(1)} %all_to_all.52.z_ref), channel_id=1, source_target_pairs={{0,16},{16,0},{1,17},{17,1},{2,18},{18,2},{3,19},{19,3},{4,20},{20... | collective-permute-start | bytes 1769480 | tf_op jit(solution)/shard_map/ppermute | solution.py:43
  239.6 28.1 %copy-start.5 = (f32[128,64]{0,1:T(8,128)S(1)}, f32[128,64]{0,1:T(8,128)}, u32[]{:S(2)}) copy-start(f32[128,64]{0,1:T(8,128)} %param.13) | copy-start | bytes 98308
  239.6 9.0 %collective-permute-start.3 = (f32[16,72,128]{2,1,0:T(8,128)S(1)}, f32[16,72,128]{2,1,0:T(8,128)S(1)}, u32[]{:S(2)}, u32[]{:S(2)}) collective-permute-start(f32[16,72,128]{2,1,0:T(8,128)S(1)} %back_tile.7), channel_id=1, source_target_pairs={{0,16},{16,0},{1,17},{17,1},{2,18},{18,2},{3,19},{19,3},{4,20},{20... | collective-permute-start | bytes 1769480 | tf_op jit(solution)/shard_map/ppermute | solution.py:43
  249.5 15.7 %all-to-all-start.9 = ((f32[16,72,128]{2,1,0:T(8,128)}), f32[16,72,128]{2,1,0:T(8,128)S(1)}, u32[]{:S(2)}, u32[]{:S(2)}) async-start(f32[16,72,128]{2,1,0:T(8,128)} %add.46), calls=%async_computation.9 | async-start | bytes 1179648 | tf_op jit(solution)/shard_map/all_to_all | solution.py:34

commit v8 on v7

v8 whole, which is shorter than its diff:
```python
import functools
import math

import jax
import jax.numpy as jnp
from jax import lax
from jax.experimental import pallas as pl
from jax.experimental.pallas import tpu as pltpu
from jax.sharding import Mesh, PartitionSpec as P

GAMMA_SCALE = 0.8
RIDGE = 64.0
CORES = 2
LANES = 128
GROUP = 2
ROWS = 16
RIDE = 8
BF = jnp.bfloat16
F32 = jnp.float32
PARAMS = pltpu.CompilerParams(vmem_limit_bytes=52 * 1024 * 1024)


def precondition(factor, resid):
    lower = lax.linalg.triangular_solve(factor, resid, left_side=True, lower=True)
    return lax.linalg.triangular_solve(factor, lower, left_side=True, lower=True, transpose_a=True)


def exchange(blocks, axes):
    return lax.all_to_all(blocks, axes, 0, 0, tiled=True)


def spread(block, axes):
    count = lax.axis_size(axes)
    return exchange(jnp.broadcast_to(block[None], (count,) + block.shape), axes)


def other_core(block):
    return lax.ppermute(block, "core", [(0, 1), (1, 0)])


def pack(rows):
    pieces = []
    for row in rows:
        for _ in range(3):
            piece = lax.reduce_precision(row, 8, 7)
            pieces.append(piece)
            row = row - piece
    pieces += [jnp.zeros_like(pieces[0])] * (ROWS - len(pieces))
    return jnp.stack(pieces).astype(BF)


def chunks_of(total):
    half = total.shape[0] // 2
    return [
        total[part * half : (part + 1) * half, at : at + LANES]
        for at in range(0, total.shape[1], LANES)
        for part in range(2)
    ]


def add_up(step, part, u_ref, acc):
    @pl.when(step == 0)
    def _():
        acc[...] = part

    @pl.when(step > 0)
    def _():
        acc[...] += part

    @pl.when(step == pl.num_programs(0) - 1)
    def _():
        for at, piece in enumerate(chunks_of(acc[...])):
            u_ref[at] = piece


def rows_at(step):
    rows = GROUP * LANES
    return pl.ds(pl.multiple_of(step * rows, rows), rows)


def tile_copy(source, target, sems, step):
    rows = rows_at(step)
    return pltpu.make_async_copy(source.at[rows], target.at[rows], sems.at[step])


def fetch(steps, tile_ref, buf, sems):
    @pl.when(pl.program_id(0) == 0)
    def _():
        for at in range(sems.shape[0]):
            tile_copy(tile_ref, buf, sems, at).start()

    for step in steps:
        tile_copy(tile_ref, buf, sems, step).wait()
    return [buf[rows_at(step)] for step in steps]


def gap_columns(rows, place):
    wide = rows.astype(F32)
    left = 0.5 * (rows.shape[1] - jnp.sum(wide * wide, axis=1, keepdims=True))
    lane = lax.broadcasted_iota(jnp.int32, (rows.shape[0], LANES), 1)
    columns = jnp.where(lane < 6, 1.0, 0.0)
    for k in range(3):
        piece = left.astype(BF).astype(F32)
        columns = jnp.where(lane == place + k, piece, columns)
        left = left - piece
    return columns.astype(BF)


def build_kernel(gamma, pts_ref, own_ref, other_ref, tile_ref, u_ref, acc, buf, sems, side):
    step = pl.program_id(0)
    steps = pl.num_programs(0)
    outs = acc.shape[0]

    @pl.when(step == 0)
    def _():
        side[...] = gap_columns(pts_ref[...], 3)

    pts = jnp.concatenate([pts_ref[...], side[...]], axis=1)
    part = None
    for blk_ref, place in ((own_ref, step), (other_ref, step + steps)):
        cen = jnp.concatenate([blk_ref[g, :LANES] for g in range(GROUP)], axis=0)
        vec = jnp.concatenate([blk_ref[g, LANES : LANES + outs] for g in range(GROUP)], axis=1)
        cen = jnp.concatenate([cen, gap_columns(cen, 0)], axis=1)
        cross = lax.dot_general(cen, pts, (((1,), (1,)), ((), ())), preferred_element_type=F32)
        tile = jnp.exp2((2.0 * gamma * math.log2(math.e)) * cross).astype(BF)
        buf[rows_at(place)] = tile
        tile_copy(buf, tile_ref, sems, place).start()
        term = jnp.dot(vec, tile, preferred_element_type=F32)
        part = term if part is None else part + term
    add_up(step, part, u_ref, acc)

    @pl.when(step == steps - 1)
    def _():
        for at in range(sems.shape[0]):
            tile_copy(buf, tile_ref, sems, at).wait()


def apply_kernel(beta_ref, z_ref, p_ref, z_other_ref, p_other_ref, tile_ref, u_ref, acc, buf, sems):
    step = pl.program_id(0)
    outs = acc.shape[0]
    tiles = fetch([step, step + pl.num_programs(0)], tile_ref, buf, sems)
    part = None
    for tile, z, p in zip(tiles, (z_ref, z_other_ref), (p_ref, p_other_ref)):
        vec = []
        for g in range(GROUP):
            high = p[g, LANES : LANES + outs].astype(F32)
            low = p[g, LANES + outs :].astype(F32)
            vec.append((z[g, :outs] + beta_ref[...] * (high + low)).astype(BF))
        term = jnp.dot(jnp.concatenate(vec, axis=1), tile, preferred_element_type=F32)
        part = term if part is None else part + term
    add_up(step, part, u_ref, acc)


def back_kernel(half, count, u_ref, tile_ref, v_ref, ub, ride, buf, sems):
    rows = buf.shape[0]
    outs = ub.shape[0]
    step = pl.program_id(0)
    tile = fetch([step], tile_ref.at[pl.ds(half * rows, rows)], buf, sems)[0]
    half = outs // 2

    @pl.when(step == 0)
    def _():
        squares = jnp.zeros((half, LANES), F32)
        for at in range(u_ref.shape[0]):
            piece = u_ref[at, :half]
            low = (at % 2) * half
            ub[low : low + half, (at // 2) * LANES : (at // 2 + 1) * LANES] = piece
            squares += piece.astype(F32) * piece.astype(F32)
        packed = jnp.sum(u_ref[:, half:].astype(F32), axis=0) if count else None
        rows = [packed[3 * k : 3 * k + 1] + packed[3 * k + 1 : 3 * k + 2] + packed[3 * k + 2 : 3 * k + 3] for k in range(count)]
        rows.append(jnp.sum(squares, axis=0, keepdims=True))
        rows.append(jnp.zeros((RIDE - count - 1, LANES), F32))
        ride[...] = jnp.concatenate(rows, axis=0)

    v = lax.dot_general(ub[...], tile, (((1,), (1,)), ((), ())), preferred_element_type=F32)
    for g in range(GROUP):
        v_ref[g, :outs] = v[:, g * LANES : (g + 1) * LANES]
        v_ref[g, outs:] = ride[...]


def body(points, centres, factor, solution, residual, direction):
    dim = points.shape[1]
    gamma = GAMMA_SCALE / math.sqrt(dim)
    outs = direction.shape[1]
    n_z, n_ctr = lax.axis_size("z"), lax.axis_size("ctr")
    total_points = points.shape[0] * n_z * CORES
    n_pts = points.shape[0]
    share = n_pts // n_ctr
    grid = (n_ctr // GROUP,)
    u_shape = jax.ShapeDtypeStruct((2 * n_pts // LANES, outs // 2, LANES), F32)
    whole = lambda shape: pl.BlockSpec(shape, lambda i: (0,) * len(shape))
    blocks = lambda rows: pl.BlockSpec((GROUP, rows, LANES), lambda i: (i, 0, 0))
    tiles = pl.BlockSpec(memory_space=pltpu.HBM)

    def copies(halves):
        return [pltpu.VMEM((halves * n_ctr * LANES, n_pts), BF), pltpu.SemaphoreType.DMA((halves * grid[0],))]
    acc = pltpu.VMEM((outs, n_pts), F32)
    work = n_ctr * LANES * n_pts

    def cost(flops, exps, size):
        return pl.CostEstimate(flops=flops, transcendentals=exps, bytes_accessed=size)

    def build(pts, own, other):
        return pl.pallas_call(
            functools.partial(build_kernel, gamma),
            grid=grid,
            in_specs=[whole(pts.shape), blocks(own.shape[1]), blocks(own.shape[1])],
            out_specs=[tiles, whole(u_shape.shape)],
            out_shape=[jax.ShapeDtypeStruct((CORES * n_ctr * LANES, n_pts), BF), u_shape],
            scratch_shapes=[acc] + copies(CORES) + [pltpu.VMEM((n_pts, LANES), BF)],
            compiler_params=PARAMS,
            cost_estimate=cost(4 * work * (dim + outs), 2 * work, 4 * work),
            name="build_tile",
        )(pts, own, other)

    def apply(beta, z, p, z_other, p_other, tile):
        return pl.pallas_call(
            apply_kernel,
            grid=grid,
            in_specs=[whole(beta.shape)] + [blocks(z.shape[1]), blocks(p.shape[1])] * 2 + [tiles],
            out_specs=whole(u_shape.shape),
            out_shape=u_shape,
            scratch_shapes=[acc] + copies(CORES),
            compiler_params=PARAMS,
            cost_estimate=cost(4 * work * outs, 0, 4 * work),
            name="apply_tile",
        )(beta, z, p, z_other, p_other, tile)

    def back(u, tile, half, count):
        return pl.pallas_call(
            functools.partial(back_kernel, half, count),
            grid=grid,
            in_specs=[whole(u.shape), tiles],
            out_specs=blocks(outs + RIDE),
            out_shape=jax.ShapeDtypeStruct((n_ctr, outs + RIDE, LANES), F32),
            scratch_shapes=[pltpu.VMEM((outs, n_pts), BF), pltpu.VMEM((RIDE, LANES), F32)] + copies(1),
            compiler_params=PARAMS,
            cost_estimate=cost(2 * work * outs, 0, 2 * work),
            name="back_tile",
        )(u, tile)

    def reduce_points(u, rows):
        u = jnp.sum(exchange(u, "z"), axis=0).astype(BF)
        return spread(jnp.concatenate([u, pack(rows)], 0) if rows else u, "z")

    def reduce_centres(u, tile, count):
        v = other_core(back(u, tile, 1, count))
        v = back(u, tile, 0, count) + v
        v = jnp.sum(exchange(v, "ctr"), axis=0)
        return v[:outs] / total_points, jnp.sum(v[outs : outs + count + 1], axis=1)

    def lanes(left, right):
        return jnp.sum(left * right, axis=0)

    mine = lax.dynamic_slice_in_dim(points, lax.axis_index("ctr") * share, share, 0)
    pts = spread(mine, "z").reshape(n_pts, dim)
    p0 = direction.T
    p0_high = lax.reduce_precision(p0, 8, 7)
    parts = [centres, p0_high.astype(BF), (p0 - p0_high).astype(BF)]
    own = spread(jnp.concatenate(parts, 0), "ctr")
    other = other_core(own)

    tile, u0 = build(pts, own, other)
    z0 = precondition(factor, residual)
    u0 = reduce_points(u0, [lanes(residual.T, z0.T), lanes(p0, p0)])
    v0, s = reduce_centres(u0, tile, 2)
    rz0 = s[0]
    q0 = v0 + RIDGE * p0
    alpha0 = rz0 / (s[2] / total_points + RIDGE * s[1])
    r1 = residual.T - alpha0 * q0
    z1 = precondition(factor, r1.T).T
    zeros = [jnp.zeros((LANES,), F32)] * (RIDE - 3)
    block = jnp.stack([lanes(r1, z1), lanes(z1, z1), lanes(z1, p0)] + zeros)
    block = block + other_core(block)
    own_z = spread(jnp.concatenate([z1, block], 0), "ctr")
    other_z = other_core(own_z)
    block = jnp.sum(spread(jnp.sum(own_z[:, outs:], axis=0), "z"), axis=0)
    rz1, zz, zp = [jnp.sum(block[k]) for k in range(3)]
    beta = rz1 / rz0
    p1 = z1 + beta * p0
    pp = zz + beta * (2.0 * zp + beta * s[1])

    rate = jnp.broadcast_to(beta, (1, LANES))
    u1 = apply(rate, own_z, own, other_z, other, tile)
    u1 = reduce_points(u1, [])
    v1, s = reduce_centres(u1, tile, 0)
    q1 = v1 + RIDGE * p1
    alpha1 = rz1 / (s[0] / total_points + RIDGE * pp)
    x2 = solution + (alpha0 * p0 + alpha1 * p1).T
    r2 = (r1 - alpha1 * q1).T
    return x2, r2


def solution(mesh):
    shape = (mesh.shape["pt"] // CORES, CORES, mesh.shape["ctr"])
    fine = Mesh(mesh.devices.reshape(shape), ("z", "core", "ctr"))
    rows = P(("z", "core", "ctr"), None)
    return jax.shard_map(
        body,
        mesh=fine,
        in_specs=(P(("z", "core"), None),) + (rows,) * 5,
        out_specs=(rows, rows),
        check_vma=False,
    )
```

time: 270 us -> 272 us (level)
  blocking collectives: 92.4 us -> 137 us
  waiting for transfers between devices: 48.5 us -> 28.8 us
  starting transfers between devices: 64.6 us -> 46 us
  Pallas kernels: 35.1 us -> 31.8 us
    all_to_all x5 -> x7, blocking collectives: 92.4 us -> 137 us  [exchange(): return lax.all_to_all(blocks, axes, 0, 0, tiled=True)]
    all_to_all x5 -> x3, starting transfers between devices: 44.7 us -> 21.1 us  [exchange(): return lax.all_to_all(blocks, axes, 0, 0, tiled=True)]
    all_to_all x5 -> x3, waiting for transfers between devices: 48.5 us -> 27.9 us  [exchange(): return lax.all_to_all(blocks, axes, 0, 0, tiled=True)]
    ppermute x4 -> x5, starting transfers between devices: 19.9 us -> 24.9 us  [other_core(): return lax.ppermute(block, 'core', [(0, 1), (1, 0)])]
    pallas_call x4 -> x2, Pallas kernels: 21 us -> 17.7 us  [the longest x1 9.35 us: build(): pl.pallas_call(functools.partial(build_kernel, gamma), grid=grid, in_spec...]
  transfers between devices with their start and end apart: 9 -> 8, of which waited for: 5 -> 4; matrix products, arithmetic and copies ran while one was open for 4% -> 4% of each run, Pallas kernels for 6% -> 3%
where the time goes in v8:
time: 272 us; the launch traced here: 270 us
  blocking collectives  137 us (50%)
  starting transfers between devices  46 us (17%)
  Pallas kernels  31.8 us (12%)
  waiting for transfers between devices  28.8 us (11%)
  other arithmetic  15.2 us (6%)
  between operations  7.54 us (3%)
  local copies, waits for them, and re-layouts  3.2 us (1%)
    all_to_all x7, blocking collectives, exchange(): return lax.all_to_all(blocks, axes, 0, 0, tiled=True)  137 us
    all_to_all x3, waiting for transfers between devices, exchange(): return lax.all_to_all(blocks, axes, 0, 0, tiled=True)  27.9 us
    ppermute x5, starting transfers between devices, other_core(): return lax.ppermute(block, 'core', [(0, 1), (1, 0)])  24.9 us
    all_to_all x3, starting transfers between devices, exchange(): return lax.all_to_all(blocks, axes, 0, 0, tiled=True)  21.1 us
    pallas_call x4, Pallas kernels, back(): pl.pallas_call(functools.partial(back_kernel, half, count), grid=grid, in...  14.1 us
    another operation x2, other arithmetic, precondition(): lax.linalg.triangular_solve(factor, lower, left_side=True, lower=True, tr...  9.82 us
    pallas_call x1, Pallas kernels, build(): pl.pallas_call(functools.partial(build_kernel, gamma), grid=grid, in_spec...  9.35 us
    pallas_call x1, Pallas kernels, apply(): pl.pallas_call(apply_kernel, grid=grid, in_specs=[whole(beta.shape)] + [b...  8.3 us
  transfers between devices with their start and end apart: 8, of which 4 were waited for; matrix products, arithmetic and copies ran while one was open for 4% of the time, Pallas kernels for 3%

profile of v8, /device:TPU:1, one launch (start us, length us, event | category | flops | bytes accessed | tf_op | source)
XLA Modules:
  0.0 270.3 jit_solution(12069805299823290444)
XLA Ops:
  0.7 0.8 fusion.18
  1.5 0.8 pad_maximum_fusion
  2.3 1.2 broadcast_in_dim.15
  3.4 7.6 %all-to-all-start.1 = ((bf16[16,256,128]{2,1,0:T(8,128)(2,1)}), bf16[16,256,128]{2,1,0:T(8,128)(2,1)S(1)}, u32[]{:S(2)}, u32[]{:S(2)}) async-start(bf16[16,256,128]{2,1,0:T(8,128)(2,1)} %broadcast_in_dim.15), calls=%async_computation.1 | async-start | bytes 2097152 | tf_op jit(solution)/shard_map/all_to_all | solution.py:29
  11.0 14.5 %all-to-all-done.1.own_ref.p_ref = bf16[16,256,128]{2,1,0:T(8,128)(2,1)S(1)} async-done(((bf16[16,256,128]{2,1,0:T(8,128)(2,1)}), bf16[16,256,128]{2,1,0:T(8,128)(2,1)S(1)}, u32[]{:S(2)}, u32[]{:S(2)}) %all-to-all-start.1) | async-done | bytes 1048608 | tf_op jit(solution)/shard_map/all_to_all | solution.py:29
  25.5 6.0 %collective-permute-start = (bf16[16,256,128]{2,1,0:T(8,128)(2,1)S(1)}, bf16[16,256,128]{2,1,0:T(8,128)(2,1)S(1)}, u32[]{:S(2)}, u32[]{:S(2)}) collective-permute-start(bf16[16,256,128]{2,1,0:T(8,128)(2,1)S(1)} %all-to-all-done.1.own_ref.p_ref), channel_id=1, source_target_pairs={{0,16},{16,0},{1,17},{17,1},{2,18},{18,2},{3,19},{19,3},{4,20},{20... | collective-permute-start | bytes 3145736 | tf_op jit(solution)/shard_map/ppermute | solution.py:38
  31.6 29.2 %all_to_all.50 = bf16[16,64,128]{2,1,0:T(8,128)(2,1)S(1)} all-to-all(bf16[16,64,128]{2,1,0:T(8,128)(2,1)S(1)} %broadcast_in_dim.14), channel_id=1, replica_groups=mesh['z'=16,'core'=2,'ctr'=16] {'z'}, dimensions={0} | all-to-all | bytes 524288 | tf_op jit(solution)/shard_map/all_to_all | solution.py:29
  60.8 1.1 copy-done.2
  61.8 9.4 %build_tile.1 = (bf16[4096,1024]{1,0:T(8,128)(2,1)}, f32[16,32,128]{2,1,0:T(8,128)}) custom-call(bf16[1024,128]{1,0:T(8,128)(2,1)S(1)} %bitcast.81, bf16[16,256,128]{2,1,0:T(8,128)(2,1)S(1)} %all-to-all-done.1.own_ref.p_ref, bf16[16,256,128]{2,1,0:T(8,128)(2,1)} %copy-done.2), custom_call_target="tpu_custom_call" | custom-call | flops 1610612736 | bytes 8388608 | tf_op jit(solution)/shard_map/build_tile/pallas_call | solution.py:204
  71.2 9.9 %all-to-all-start.2 = ((f32[16,32,128]{2,1,0:T(8,128)}), f32[16,32,128]{2,1,0:T(8,128)S(1)}, u32[]{:S(2)}, u32[]{:S(2)}) async-start(f32[16,32,128]{2,1,0:T(8,128)} %get-tuple-element.6), calls=%async_computation.2 | async-start | bytes 524288 | tf_op jit(solution)/shard_map/all_to_all | solution.py:29
  81.1 9.8 %custom-call.9 = f32[1,128,128]{1,2,0:T(8,128)S(1)} custom-call(f32[1,128,128]{2,1,0:T(8,128)S(1)} %select_bitcast_fusion), custom_call_target="InvertDiagBlocksLowerTriangular" | custom-call | tf_op jit(solution)/shard_map/triangular_solve/custom-call.0 | solution.py:25
  91.6 3.3 %all-to-all-done.2 = f32[16,32,128]{2,1,0:T(8,128)S(1)} async-done(((f32[16,32,128]{2,1,0:T(8,128)}), f32[16,32,128]{2,1,0:T(8,128)S(1)}, u32[]{:S(2)}, u32[]{:S(2)}) %all-to-all-start.2) | async-done | bytes 262176 | tf_op jit(solution)/shard_map/all_to_all | solution.py:29
  95.0 22.6 %all_to_all.51.u_ref = bf16[16,48,128]{2,1,0:T(8,128)(2,1)S(1)} all-to-all(bf16[16,48,128]{2,1,0:T(8,128)(2,1)S(1)} %broadcast_in_dim.16), channel_id=1, replica_groups=mesh['z'=16,'core'=2,'ctr'=16] {'z'}, dimensions={0} | all-to-all | bytes 393216 | tf_op jit(solution)/shard_map/all_to_all | solution.py:29
  117.5 3.5 %back_tile.5 = f32[16,72,128]{2,1,0:T(8,128)S(1)} custom-call(bf16[16,48,128]{2,1,0:T(8,128)(2,1)S(1)} %all_to_all.51.u_ref, bf16[4096,1024]{1,0:T(8,128)(2,1)} %get-tuple-element.7.tile_ref), custom_call_target="tpu_custom_call" | custom-call | flops 268435456 | bytes 4194304 | tf_op jit(solution)/shard_map/back_tile/pallas_call | solution.py:230
  121.1 6.9 %collective-permute-start.1 = (f32[16,72,128]{2,1,0:T(8,128)S(1)}, f32[16,72,128]{2,1,0:T(8,128)S(1)}, u32[]{:S(2)}, u32[]{:S(2)}) collective-permute-start(f32[16,72,128]{2,1,0:T(8,128)S(1)} %back_tile.5), channel_id=1, source_target_pairs={{0,16},{16,0},{1,17},{17,1},{2,18},{18,2},{3,19},{19,3},{4,20},{20... | collective-permute-start | bytes 1769480 | tf_op jit(solution)/shard_map/ppermute | solution.py:38
  128.0 3.5 %back_tile.4 = f32[16,72,128]{2,1,0:T(8,128)S(1)} custom-call(bf16[16,48,128]{2,1,0:T(8,128)(2,1)S(1)} %all_to_all.51.u_ref, bf16[4096,1024]{1,0:T(8,128)(2,1)} %get-tuple-element.7.tile_ref), custom_call_target="tpu_custom_call" | custom-call | flops 268435456 | bytes 4194304 | tf_op jit(solution)/shard_map/back_tile/pallas_call | solution.py:230
  131.6 15.0 %all_to_all.52 = f32[16,72,128]{2,1,0:T(8,128)S(1)} all-to-all(f32[16,72,128]{2,1,0:T(8,128)S(1)} %add.46), channel_id=1, replica_groups=mesh['z'=16,'core'=2,'ctr'=16] {'ctr'}, dimensions={0} | all-to-all | bytes 1179648 | tf_op jit(solution)/shard_map/all_to_all | solution.py:29
  150.0 2.7 collective-permute-start.2
  152.8 0.8 collective-permute-done.2
  153.6 14.3 %all_to_all.53.z_ref = f32[16,72,128]{2,1,0:T(8,128)S(1)} all-to-all(f32[16,72,128]{2,1,0:T(8,128)S(1)} %broadcast_in_dim.17), channel_id=1, replica_groups=mesh['z'=16,'core'=2,'ctr'=16] {'ctr'}, dimensions={0} | all-to-all | bytes 1179648 | tf_op jit(solution)/shard_map/all_to_all | solution.py:29
  167.9 3.7 %collective-permute-start.3 = (f32[16,72,128]{2,1,0:T(8,128)S(1)}, f32[16,72,128]{2,1,0:T(8,128)S(1)}, u32[]{:S(2)}, u32[]{:S(2)}) collective-permute-start(f32[16,72,128]{2,1,0:T(8,128)S(1)} %all_to_all.53.z_ref), channel_id=1, source_target_pairs={{0,16},{16,0},{1,17},{17,1},{2,18},{18,2},{3,19},{19,3},{4,20},{20... | collective-permute-start | bytes 1769480 | tf_op jit(solution)/shard_map/ppermute | solution.py:38
  171.7 16.1 %all_to_all.54 = f32[16,8,128]{2,1,0:T(8,128)S(1)} all-to-all(f32[16,8,128]{2,1,0:T(8,128)S(1)} %broadcast_in_dim.18), channel_id=1, replica_groups=mesh['z'=16,'core'=2,'ctr'=16] {'z'}, dimensions={0} | all-to-all | bytes 131072 | tf_op jit(solution)/shard_map/all_to_all | solution.py:29
  187.7 0.7 slice_reduce_fusion.3
  189.8 8.3 %apply_tile.1 = f32[16,32,128]{2,1,0:T(8,128)S(1)} custom-call(f32[1,128]{1,0:T(1,128)S(1)} %broadcast_in_dim.19.beta_ref, f32[16,72,128]{2,1,0:T(8,128)S(1)} %all_to_all.53.z_ref, bf16[16,256,128]{2,1,0:T(8,128)(2,1)} %copy-done.1, f32[16,72,128]{2,1,0:T(8,128)S(1)} %collective-permute-done.3.z_other_ref, bf16[16,256,128]{2,1,0:T(8,128)(2,1)} %copy-done.2, ...), custom_call_target="tpu_custom_call" | custom-call | flops 536870912 | bytes 8388608 | tf_op jit(solution)/shard_map/apply_tile/pallas_call | solution.py:217
  198.1 16.8 %all_to_all.55 = f32[16,32,128]{2,1,0:T(8,128)S(1)} all-to-all(f32[16,32,128]{2,1,0:T(8,128)S(1)} %apply_tile.1), channel_id=1, replica_groups=mesh['z'=16,'core'=2,'ctr'=16] {'z'}, dimensions={0} | all-to-all | bytes 524288 | tf_op jit(solution)/shard_map/all_to_all | solution.py:29
  215.0 22.8 %all_to_all.56.u_ref = bf16[16,32,128]{2,1,0:T(8,128)(2,1)S(1)} all-to-all(bf16[16,32,128]{2,1,0:T(8,128)(2,1)S(1)} %broadcast_in_dim.20), channel_id=1, replica_groups=mesh['z'=16,'core'=2,'ctr'=16] {'z'}, dimensions={0} | all-to-all | bytes 262144 | tf_op jit(solution)/shard_map/all_to_all | solution.py:29
  237.8 3.5 %back_tile.7 = f32[16,72,128]{2,1,0:T(8,128)S(1)} custom-call(bf16[16,32,128]{2,1,0:T(8,128)(2,1)S(1)} %all_to_all.56.u_ref, bf16[4096,1024]{1,0:T(8,128)(2,1)} %get-tuple-element.7.tile_ref), custom_call_target="tpu_custom_call" | custom-call | flops 268435456 | bytes 4194304 | tf_op jit(solution)/shard_map/back_tile/pallas_call | solution.py:230
  241.4 5.7 %collective-permute-start.4 = (f32[16,72,128]{2,1,0:T(8,128)S(1)}, f32[16,72,128]{2,1,0:T(8,128)S(1)}, u32[]{:S(2)}, u32[]{:S(2)}) collective-permute-start(f32[16,72,128]{2,1,0:T(8,128)S(1)} %back_tile.7), channel_id=1, source_target_pairs={{0,16},{16,0},{1,17},{17,1},{2,18},{18,2},{3,19},{19,3},{4,20},{20... | collective-permute-start | bytes 1769480 | tf_op jit(solution)/shard_map/ppermute | solution.py:38
  247.0 3.5 %back_tile.6 = f32[16,72,128]{2,1,0:T(8,128)S(1)} custom-call(bf16[16,32,128]{2,1,0:T(8,128)(2,1)S(1)} %all_to_all.56.u_ref, bf16[4096,1024]{1,0:T(8,128)(2,1)} %get-tuple-element.7.tile_ref), custom_call_target="tpu_custom_call" | custom-call | flops 268435456 | bytes 4194304 | tf_op jit(solution)/shard_map/back_tile/pallas_call | solution.py:230
  250.6 0.9 add.50
  251.5 3.6 %all-to-all-start.9 = ((f32[16,72,128]{2,1,0:T(8,128)}), f32[16,72,128]{2,1,0:T(8,128)S(1)}, u32[]{:S(2)}, u32[]{:S(2)}) async-start(f32[16,72,128]{2,1,0:T(8,128)} %add.50), calls=%async_computation.9 | async-start | bytes 1179648 | tf_op jit(solution)/shard_map/all_to_all | solution.py:29
  256.9 10.2 %all-to-all-done.9 = f32[16,72,128]{2,1,0:T(8,128)S(1)} async-done(((f32[16,72,128]{2,1,0:T(8,128)}), f32[16,72,128]{2,1,0:T(8,128)S(1)}, u32[]{:S(2)}, u32[]{:S(2)}) %all-to-all-start.9) | async-done | bytes 589856 | tf_op jit(solution)/shard_map/all_to_all | solution.py:29
  (52 shorter events, 4.3 us)
Async XLA Ops:
  0.6 30.9 %copy-start = (bf16[1024,128]{1,0:T(8,128)(2,1)S(1)}, bf16[1024,128]{1,0:T(8,128)(2,1)}, u32[]{:S(2)}) copy-start(bf16[1024,128]{1,0:T(8,128)(2,1)} %param.10) | copy-start | bytes 786436
  0.6 80.5 %copy-start.5 = (f32[128,128]{1,0:T(8,128)S(1)}, f32[128,128]{1,0:T(8,128)}, u32[]{:S(2)}) copy-start(f32[128,128]{1,0:T(8,128)} %param.12) | copy-start | bytes 196612
  0.7 90.3 %copy-start.4 = (f32[128,64]{0,1:T(8,128)S(1)}, f32[128,64]{0,1:T(8,128)}, u32[]{:S(2)}) copy-start(f32[128,64]{0,1:T(8,128)} %param.14) | copy-start | bytes 98308
  3.4 22.1 %all-to-all-start.1 = ((bf16[16,256,128]{2,1,0:T(8,128)(2,1)}), bf16[16,256,128]{2,1,0:T(8,128)(2,1)S(1)}, u32[]{:S(2)}, u32[]{:S(2)}) async-start(bf16[16,256,128]{2,1,0:T(8,128)(2,1)} %broadcast_in_dim.15), calls=%async_computation.1 | async-start | bytes 2097152 | tf_op jit(solution)/shard_map/all_to_all | solution.py:29
  25.5 95.5 %copy-start.1 = (bf16[16,256,128]{2,1,0:T(8,128)(2,1)}, bf16[16,256,128]{2,1,0:T(8,128)(2,1)S(1)}, u32[]{:S(2)}) copy-start(bf16[16,256,128]{2,1,0:T(8,128)(2,1)S(1)} %all-to-all-done.1.own_ref.p_ref) | copy-start | bytes 3145732
  25.5 35.3 %collective-permute-start = (bf16[16,256,128]{2,1,0:T(8,128)(2,1)S(1)}, bf16[16,256,128]{2,1,0:T(8,128)(2,1)S(1)}, u32[]{:S(2)}, u32[]{:S(2)}) collective-permute-start(bf16[16,256,128]{2,1,0:T(8,128)(2,1)S(1)} %all-to-all-done.1.own_ref.p_ref), channel_id=1, source_target_pairs={{0,16},{16,0},{1,17},{17,1},{2,18},{18,2},{3,19},{19,3},{4,20},{20... | collective-permute-start | bytes 3145736 | tf_op jit(solution)/shard_map/ppermute | solution.py:38
  60.8 1.1 copy-start.2
  71.2 23.6 %all-to-all-start.2 = ((f32[16,32,128]{2,1,0:T(8,128)}), f32[16,32,128]{2,1,0:T(8,128)S(1)}, u32[]{:S(2)}, u32[]{:S(2)}) async-start(f32[16,32,128]{2,1,0:T(8,128)} %get-tuple-element.6), calls=%async_computation.2 | async-start | bytes 524288 | tf_op jit(solution)/shard_map/all_to_all | solution.py:29
  121.1 28.3 %copy-start.3 = (f32[128,64]{0,1:T(8,128)S(1)}, f32[128,64]{0,1:T(8,128)}, u32[]{:S(2)}) copy-start(f32[128,64]{0,1:T(8,128)} %param.15) | copy-start | bytes 98308
  121.1 10.5 %collective-permute-start.1 = (f32[16,72,128]{2,1,0:T(8,128)S(1)}, f32[16,72,128]{2,1,0:T(8,128)S(1)}, u32[]{:S(2)}, u32[]{:S(2)}) collective-permute-start(f32[16,72,128]{2,1,0:T(8,128)S(1)} %back_tile.5), channel_id=1, source_target_pairs={{0,16},{16,0},{1,17},{17,1},{2,18},{18,2},{3,19},{19,3},{4,20},{20... | collective-permute-start | bytes 1769480 | tf_op jit(solution)/shard_map/ppermute | solution.py:38
  150.0 3.5 %collective-permute-start.2 = (f32[8,128]{1,0:T(8,128)S(1)}, f32[8,128]{1,0:T(8,128)S(1)}, u32[]{:S(2)}, u32[]{:S(2)}) collective-permute-start(f32[8,128]{1,0:T(8,128)S(1)} %stack.35), channel_id=1, source_target_pairs={{0,16},{16,0},{1,17},{17,1},{2,18},{18,2},{3,19},{19,3},{4,20},{20... | collective-permute-start | bytes 12296 | tf_op jit(solution)/shard_map/ppermute | solution.py:38
  167.9 21.9 %collective-permute-start.3 = (f32[16,72,128]{2,1,0:T(8,128)S(1)}, f32[16,72,128]{2,1,0:T(8,128)S(1)}, u32[]{:S(2)}, u32[]{:S(2)}) collective-permute-start(f32[16,72,128]{2,1,0:T(8,128)S(1)} %all_to_all.53.z_ref), channel_id=1, source_target_pairs={{0,16},{16,0},{1,17},{17,1},{2,18},{18,2},{3,19},{19,3},{4,20},{20... | collective-permute-start | bytes 1769480 | tf_op jit(solution)/shard_map/ppermute | solution.py:38
  241.4 28.4 %copy-start.6 = (f32[128,64]{0,1:T(8,128)S(1)}, f32[128,64]{0,1:T(8,128)}, u32[]{:S(2)}) copy-start(f32[128,64]{0,1:T(8,128)} %param.13) | copy-start | bytes 98308
  241.4 9.2 %collective-permute-start.4 = (f32[16,72,128]{2,1,0:T(8,128)S(1)}, f32[16,72,128]{2,1,0:T(8,128)S(1)}, u32[]{:S(2)}, u32[]{:S(2)}) collective-permute-start(f32[16,72,128]{2,1,0:T(8,128)S(1)} %back_tile.7), channel_id=1, source_target_pairs={{0,16},{16,0},{1,17},{17,1},{2,18},{18,2},{3,19},{19,3},{4,20},{20... | collective-permute-start | bytes 1769480 | tf_op jit(solution)/shard_map/ppermute | solution.py:38
  251.5 15.7 %all-to-all-start.9 = ((f32[16,72,128]{2,1,0:T(8,128)}), f32[16,72,128]{2,1,0:T(8,128)S(1)}, u32[]{:S(2)}, u32[]{:S(2)}) async-start(f32[16,72,128]{2,1,0:T(8,128)} %add.50), calls=%async_computation.9 | async-start | bytes 1179648 | tf_op jit(solution)/shard_map/all_to_all | solution.py:29

commit v9 on v8

--- a/solution.py
+++ b/solution.py
@@ -17,6 +17,7 @@
 RIDE = 8
 BF = jnp.bfloat16
 F32 = jnp.float32
+SMALL = pltpu.CompilerParams(vmem_limit_bytes=8 * 1024 * 1024)
 PARAMS = pltpu.CompilerParams(vmem_limit_bytes=52 * 1024 * 1024)
 
 
@@ -135,17 +136,23 @@
             tile_copy(buf, tile_ref, sems, at).wait()
 
 
-def apply_kernel(beta_ref, z_ref, p_ref, z_other_ref, p_other_ref, tile_ref, u_ref, acc, buf, sems):
+def apply_kernel(sums_ref, scalars_ref, z_ref, p_ref, z_other_ref, p_other_ref, tile_ref, u_ref, acc, buf, sems, beta):
     step = pl.program_id(0)
     outs = acc.shape[0]
     tiles = fetch([step, step + pl.num_programs(0)], tile_ref, buf, sems)
+
+    @pl.when(step == 0)
+    def _():
+        rate = totals(sums_ref)[0:1] / scalars_ref[0:1, 0:1]
+        beta[...] = jnp.broadcast_to(rate, beta.shape)
+
     part = None
     for tile, z, p in zip(tiles, (z_ref, z_other_ref), (p_ref, p_other_ref)):
         vec = []
         for g in range(GROUP):
             high = p[g, LANES : LANES + outs].astype(F32)
             low = p[g, LANES + outs :].astype(F32)
-            vec.append((z[g, :outs] + beta_ref[...] * (high + low)).astype(BF))
+            vec.append((z[g, :outs] + beta[...] * (high + low)).astype(BF))
         term = jnp.dot(jnp.concatenate(vec, axis=1), tile, preferred_element_type=F32)
         part = term if part is None else part + term
     add_up(step, part, u_ref, acc)
@@ -176,6 +183,34 @@
     for g in range(GROUP):
         v_ref[g, :outs] = v[:, g * LANES : (g + 1) * LANES]
         v_ref[g, outs:] = ride[...]
+
+
+def totals(sums_ref):
+    return jnp.sum(jnp.sum(sums_ref[...], axis=0), axis=1, keepdims=True)
+
+
+def first_kernel(points, v_ref, p_ref, r_ref, r1_ref, scalars_ref):
+    outs = p_ref.shape[0]
+    v = jnp.sum(v_ref[...], axis=0)
+    s = jnp.sum(v[outs:], axis=1, keepdims=True)
+    alpha = s[0:1] / (s[2:3] / points + RIDGE * s[1:2])
+    r1_ref[...] = r_ref[...] - alpha * (v[:outs] / points + RIDGE * p_ref[...])
+    rows = [jnp.broadcast_to(value, (1, LANES)) for value in (s[0:1], s[1:2], alpha)]
+    scalars_ref[...] = jnp.concatenate(rows + [jnp.zeros((RIDE - 3, LANES), F32)], axis=0)
+
+
+def last_kernel(points, v_ref, sums_ref, scalars_ref, z_ref, p_ref, r_ref, x_ref, x_out, r_out):
+    outs = p_ref.shape[0]
+    v = jnp.sum(v_ref[...], axis=0)
+    uu = jnp.sum(v[outs : outs + 1], axis=1, keepdims=True)
+    t = totals(sums_ref)
+    rz0, pp0, alpha0 = [scalars_ref[k : k + 1, 0:1] for k in range(3)]
+    beta = t[0:1] / rz0
+    p1 = z_ref[...] + beta * p_ref[...]
+    pp = t[1:2] + beta * (2.0 * t[2:3] + beta * pp0)
+    alpha1 = t[0:1] / (uu / points + RIDGE * pp)
+    x_out[...] = x_ref[...] + alpha0 * p_ref[...] + alpha1 * p1
+    r_out[...] = r_ref[...] - alpha1 * (v[:outs] / points + RIDGE * p1)
 
 
 def body(points, centres, factor, solution, residual, direction):
@@ -213,18 +248,18 @@
             name="build_tile",
         )(pts, own, other)
 
-    def apply(beta, z, p, z_other, p_other, tile):
+    def apply(sums, scalars, z, p, z_other, p_other, tile):
         return pl.pallas_call(
             apply_kernel,
             grid=grid,
-            in_specs=[whole(beta.shape)] + [blocks(z.shape[1]), blocks(p.shape[1])] * 2 + [tiles],
+            in_specs=[whole(sums.shape), whole(scalars.shape)] + [blocks(z.shape[1]), blocks(p.shape[1])] * 2 + [tiles],
             out_specs=whole(u_shape.shape),
             out_shape=u_shape,
-            scratch_shapes=[acc] + copies(CORES),
+            scratch_shapes=[acc] + copies(CORES) + [pltpu.VMEM((1, LANES), F32)],
             compiler_params=PARAMS,
             cost_estimate=cost(4 * work * outs, 0, 4 * work),
             name="apply_tile",
-        )(beta, z, p, z_other, p_other, tile)
+        )(sums, scalars, z, p, z_other, p_other, tile)
 
     def back(u, tile, half, count):
         return pl.pallas_call(
@@ -246,8 +281,16 @@
     def reduce_centres(u, tile, count):
         v = other_core(back(u, tile, 1, count))
         v = back(u, tile, 0, count) + v
-        v = jnp.sum(exchange(v, "ctr"), axis=0)
-        return v[:outs] / total_points, jnp.sum(v[outs : outs + count + 1], axis=1)
+        return exchange(v, "ctr")
+
+    def local(kernel, shapes, *operands):
+        return pl.pallas_call(
+            functools.partial(kernel, float(total_points)),
+            out_shape=[jax.ShapeDtypeStruct(shape, F32) for shape in shapes],
+            compiler_params=SMALL,
+            cost_estimate=cost(2 * n_ctr * outs * LANES, 0, 4 * n_ctr * outs * LANES),
+            name=kernel.__name__,
+        )(*operands)
 
     def lanes(left, right):
         return jnp.sum(left * right, axis=0)
@@ -263,32 +306,20 @@
     tile, u0 = build(pts, own, other)
     z0 = precondition(factor, residual)
     u0 = reduce_points(u0, [lanes(residual.T, z0.T), lanes(p0, p0)])
-    v0, s = reduce_centres(u0, tile, 2)
-    rz0 = s[0]
-    q0 = v0 + RIDGE * p0
-    alpha0 = rz0 / (s[2] / total_points + RIDGE * s[1])
-    r1 = residual.T - alpha0 * q0
+    v0 = reduce_centres(u0, tile, 2)
+    r1, scalars = local(first_kernel, [p0.shape, (RIDE, LANES)], v0, p0, residual.T)
     z1 = precondition(factor, r1.T).T
     zeros = [jnp.zeros((LANES,), F32)] * (RIDE - 3)
     block = jnp.stack([lanes(r1, z1), lanes(z1, z1), lanes(z1, p0)] + zeros)
     block = block + other_core(block)
     own_z = spread(jnp.concatenate([z1, block], 0), "ctr")
     other_z = other_core(own_z)
-    block = jnp.sum(spread(jnp.sum(own_z[:, outs:], axis=0), "z"), axis=0)
-    rz1, zz, zp = [jnp.sum(block[k]) for k in range(3)]
-    beta = rz1 / rz0
-    p1 = z1 + beta * p0
-    pp = zz + beta * (2.0 * zp + beta * s[1])
-
-    rate = jnp.broadcast_to(beta, (1, LANES))
-    u1 = apply(rate, own_z, own, other_z, other, tile)
+    sums = spread(jnp.sum(own_z[:, outs:], axis=0), "z")
+    u1 = apply(sums, scalars, own_z, own, other_z, other, tile)
     u1 = reduce_points(u1, [])
-    v1, s = reduce_centres(u1, tile, 0)
-    q1 = v1 + RIDGE * p1
-    alpha1 = rz1 / (s[0] / total_points + RIDGE * pp)
-    x2 = solution + (alpha0 * p0 + alpha1 * p1).T
-    r2 = (r1 - alpha1 * q1).T
-    return x2, r2
+    v1 = reduce_centres(u1, tile, 0)
+    x2, r2 = local(last_kernel, [p0.shape, p0.shape], v1, sums, scalars, z1, p0, r1, solution.T)
+    return x2.T, r2.T
 
 
 def solution(mesh):

time: 272 us -> 263 us (0.967)
  blocking collectives: 137 us -> 152 us
  waiting for transfers between devices: 28.8 us -> 18.5 us
  between operations: 7.54 us -> 0.95 us
  starting transfers between devices: 46 us -> 42.4 us
  other arithmetic: 15.2 us -> 11.6 us
    all_to_all x7 -> x8, blocking collectives: 137 us -> 152 us  [exchange(): return lax.all_to_all(blocks, axes, 0, 0, tiled=True)]
    all_to_all x3 -> x2, waiting for transfers between devices: 27.9 us -> 17.7 us  [exchange(): return lax.all_to_all(blocks, axes, 0, 0, tiled=True)]
    all_to_all x3 -> x2, starting transfers between devices: 21.1 us -> 17.5 us  [exchange(): return lax.all_to_all(blocks, axes, 0, 0, tiled=True)]
    pallas_call x1 -> x3, Pallas kernels: 8.3 us -> 9.44 us  [the longest x1 8.49 us: apply(): pl.pallas_call(apply_kernel, grid=grid, in_specs=[whole(sums.shape), whol...]
  transfers between devices with their start and end apart: 8 -> 7, of which waited for: 4 -> 3; matrix products, arithmetic and copies ran while one was open for 4% -> 4% of each run, Pallas kernels for 3% -> 3%
where the time goes in v9:
time: 263 us; the launch traced here: 262 us
  blocking collectives  152 us (58%)
  starting transfers between devices  42.4 us (16%)
  Pallas kernels  32.9 us (13%)
  waiting for transfers between devices  18.5 us (7%)
  other arithmetic  11.6 us (4%)
    all_to_all x8, blocking collectives, exchange(): return lax.all_to_all(blocks, axes, 0, 0, tiled=True)  152 us
    ppermute x5, starting transfers between devices, other_core(): return lax.ppermute(block, 'core', [(0, 1), (1, 0)])  24.9 us
    all_to_all x2, waiting for transfers between devices, exchange(): return lax.all_to_all(blocks, axes, 0, 0, tiled=True)  17.7 us
    all_to_all x2, starting transfers between devices, exchange(): return lax.all_to_all(blocks, axes, 0, 0, tiled=True)  17.5 us
    pallas_call x4, Pallas kernels, back(): pl.pallas_call(functools.partial(back_kernel, half, count), grid=grid, in...  14.1 us
    another operation x2, other arithmetic, precondition(): lax.linalg.triangular_solve(factor, lower, left_side=True, lower=True, tr...  9.82 us
    pallas_call x1, Pallas kernels, build(): pl.pallas_call(functools.partial(build_kernel, gamma), grid=grid, in_spec...  9.35 us
    pallas_call x1, Pallas kernels, apply(): pl.pallas_call(apply_kernel, grid=grid, in_specs=[whole(sums.shape), whol...  8.49 us
  transfers between devices with their start and end apart: 7, of which 3 were waited for; matrix products, arithmetic and copies ran while one was open for 4% of the time, Pallas kernels for 3%

profile of v9, /device:TPU:1, one launch (start us, length us, event | category | flops | bytes accessed | tf_op | source)
XLA Modules:
  0.0 261.8 jit_solution(14141676009710411442)
XLA Ops:
  0.7 0.8 multiply_reduce_fusion.3
  1.5 0.8 pad_maximum_fusion
  2.3 1.2 broadcast_in_dim.13
  3.4 7.6 %all-to-all-start.1 = ((bf16[16,256,128]{2,1,0:T(8,128)(2,1)}), bf16[16,256,128]{2,1,0:T(8,128)(2,1)S(1)}, u32[]{:S(2)}, u32[]{:S(2)}) async-start(bf16[16,256,128]{2,1,0:T(8,128)(2,1)} %broadcast_in_dim.13), calls=%async_computation.1 | async-start | bytes 2097152 | tf_op jit(solution)/shard_map/all_to_all | solution.py:30
  11.0 14.5 %all-to-all-done.1.own_ref.p_ref = bf16[16,256,128]{2,1,0:T(8,128)(2,1)S(1)} async-done(((bf16[16,256,128]{2,1,0:T(8,128)(2,1)}), bf16[16,256,128]{2,1,0:T(8,128)(2,1)S(1)}, u32[]{:S(2)}, u32[]{:S(2)}) %all-to-all-start.1) | async-done | bytes 1048608 | tf_op jit(solution)/shard_map/all_to_all | solution.py:30
  25.5 6.0 %collective-permute-start = (bf16[16,256,128]{2,1,0:T(8,128)(2,1)S(1)}, bf16[16,256,128]{2,1,0:T(8,128)(2,1)S(1)}, u32[]{:S(2)}, u32[]{:S(2)}) collective-permute-start(bf16[16,256,128]{2,1,0:T(8,128)(2,1)S(1)} %all-to-all-done.1.own_ref.p_ref), channel_id=1, source_target_pairs={{0,16},{16,0},{1,17},{17,1},{2,18},{18,2},{3,19},{19,3},{4,20},{20... | collective-permute-start | bytes 3145736 | tf_op jit(solution)/shard_map/ppermute | solution.py:39
  31.6 29.2 %all_to_all.50 = bf16[16,64,128]{2,1,0:T(8,128)(2,1)S(1)} all-to-all(bf16[16,64,128]{2,1,0:T(8,128)(2,1)S(1)} %broadcast_in_dim.12), channel_id=1, replica_groups=mesh['z'=16,'core'=2,'ctr'=16] {'z'}, dimensions={0} | all-to-all | bytes 524288 | tf_op jit(solution)/shard_map/all_to_all | solution.py:30
  60.8 1.1 copy-done.5
  61.8 9.4 %build_tile.1 = (bf16[4096,1024]{1,0:T(8,128)(2,1)}, f32[16,32,128]{2,1,0:T(8,128)}) custom-call(bf16[1024,128]{1,0:T(8,128)(2,1)S(1)} %bitcast.64, bf16[16,256,128]{2,1,0:T(8,128)(2,1)S(1)} %all-to-all-done.1.own_ref.p_ref, bf16[16,256,128]{2,1,0:T(8,128)(2,1)} %copy-done.5), custom_call_target="tpu_custom_call" | custom-call | flops 1610612736 | bytes 8388608 | tf_op jit(solution)/shard_map/build_tile/pallas_call | solution.py:239
  71.2 9.9 %all-to-all-start.2 = ((f32[16,32,128]{2,1,0:T(8,128)}), f32[16,32,128]{2,1,0:T(8,128)S(1)}, u32[]{:S(2)}, u32[]{:S(2)}) async-start(f32[16,32,128]{2,1,0:T(8,128)} %get-tuple-element.10), calls=%async_computation.2 | async-start | bytes 524288 | tf_op jit(solution)/shard_map/all_to_all | solution.py:30
  81.1 9.8 %custom-call.11 = f32[1,128,128]{1,2,0:T(8,128)S(1)} custom-call(f32[1,128,128]{2,1,0:T(8,128)S(1)} %select_bitcast_fusion), custom_call_target="InvertDiagBlocksLowerTriangular" | custom-call | tf_op jit(solution)/shard_map/triangular_solve/custom-call.0 | solution.py:26
  91.3 0.3 fusion.1
  91.6 3.3 %all-to-all-done.2 = f32[16,32,128]{2,1,0:T(8,128)S(1)} async-done(((f32[16,32,128]{2,1,0:T(8,128)}), f32[16,32,128]{2,1,0:T(8,128)S(1)}, u32[]{:S(2)}, u32[]{:S(2)}) %all-to-all-start.2) | async-done | bytes 262176 | tf_op jit(solution)/shard_map/all_to_all | solution.py:30
  95.0 22.6 %all_to_all.51.u_ref = bf16[16,48,128]{2,1,0:T(8,128)(2,1)S(1)} all-to-all(bf16[16,48,128]{2,1,0:T(8,128)(2,1)S(1)} %broadcast_in_dim.14), channel_id=1, replica_groups=mesh['z'=16,'core'=2,'ctr'=16] {'z'}, dimensions={0} | all-to-all | bytes 393216 | tf_op jit(solution)/shard_map/all_to_all | solution.py:30
  117.5 3.5 %back_tile.5 = f32[16,72,128]{2,1,0:T(8,128)S(1)} custom-call(bf16[16,48,128]{2,1,0:T(8,128)(2,1)S(1)} %all_to_all.51.u_ref, bf16[4096,1024]{1,0:T(8,128)(2,1)} %get-tuple-element.11.tile_ref), custom_call_target="tpu_custom_call" | custom-call | flops 268435456 | bytes 4194304 | tf_op jit(solution)/shard_map/back_tile/pallas_call | solution.py:265
  121.1 6.9 %collective-permute-start.1 = (f32[16,72,128]{2,1,0:T(8,128)S(1)}, f32[16,72,128]{2,1,0:T(8,128)S(1)}, u32[]{:S(2)}, u32[]{:S(2)}) collective-permute-start(f32[16,72,128]{2,1,0:T(8,128)S(1)} %back_tile.5), channel_id=1, source_target_pairs={{0,16},{16,0},{1,17},{17,1},{2,18},{18,2},{3,19},{19,3},{4,20},{20... | collective-permute-start | bytes 1769480 | tf_op jit(solution)/shard_map/ppermute | solution.py:39
  128.0 3.5 %back_tile.4 = f32[16,72,128]{2,1,0:T(8,128)S(1)} custom-call(bf16[16,48,128]{2,1,0:T(8,128)(2,1)S(1)} %all_to_all.51.u_ref, bf16[4096,1024]{1,0:T(8,128)(2,1)} %get-tuple-element.11.tile_ref), custom_call_target="tpu_custom_call" | custom-call | flops 268435456 | bytes 4194304 | tf_op jit(solution)/shard_map/back_tile/pallas_call | solution.py:265
  131.6 15.0 %all_to_all.52.v_ref = f32[16,72,128]{2,1,0:T(8,128)S(1)} all-to-all(f32[16,72,128]{2,1,0:T(8,128)S(1)} %add.15), channel_id=1, replica_groups=mesh['z'=16,'core'=2,'ctr'=16] {'ctr'}, dimensions={0} | all-to-all | bytes 1179648 | tf_op jit(solution)/shard_map/all_to_all | solution.py:30
  147.1 0.3 multiply_reduce_fusion
  147.4 2.7 %collective-permute-start.2 = (f32[8,128]{1,0:T(8,128)S(1)}, f32[8,128]{1,0:T(8,128)S(1)}, u32[]{:S(2)}, u32[]{:S(2)}) collective-permute-start(f32[8,128]{1,0:T(8,128)S(1)} %stack.35), channel_id=1, source_target_pairs={{0,16},{16,0},{1,17},{17,1},{2,18},{18,2},{3,19},{19,3},{4,20},{20... | collective-permute-start | bytes 12296 | tf_op jit(solution)/shard_map/ppermute | solution.py:39
  150.1 0.8 collective-permute-done.2
  151.0 14.3 %all_to_all.53.z_ref = f32[16,72,128]{2,1,0:T(8,128)S(1)} all-to-all(f32[16,72,128]{2,1,0:T(8,128)S(1)} %broadcast_in_dim.15), channel_id=1, replica_groups=mesh['z'=16,'core'=2,'ctr'=16] {'ctr'}, dimensions={0} | all-to-all | bytes 1179648 | tf_op jit(solution)/shard_map/all_to_all | solution.py:30
  165.3 3.7 %collective-permute-start.3 = (f32[16,72,128]{2,1,0:T(8,128)S(1)}, f32[16,72,128]{2,1,0:T(8,128)S(1)}, u32[]{:S(2)}, u32[]{:S(2)}) collective-permute-start(f32[16,72,128]{2,1,0:T(8,128)S(1)} %all_to_all.53.z_ref), channel_id=1, source_target_pairs={{0,16},{16,0},{1,17},{17,1},{2,18},{18,2},{3,19},{19,3},{4,20},{20... | collective-permute-start | bytes 1769480 | tf_op jit(solution)/shard_map/ppermute | solution.py:39
  169.0 16.1 %all_to_all.54.sums_ref = f32[16,8,128]{2,1,0:T(8,128)S(1)} all-to-all(f32[16,8,128]{2,1,0:T(8,128)S(1)} %broadcast_in_dim.16), channel_id=1, replica_groups=mesh['z'=16,'core'=2,'ctr'=16] {'z'}, dimensions={0} | all-to-all | bytes 131072 | tf_op jit(solution)/shard_map/all_to_all | solution.py:30
  185.1 8.5 %apply_tile.1 = f32[16,32,128]{2,1,0:T(8,128)S(1)} custom-call(f32[16,8,128]{2,1,0:T(8,128)S(1)} %all_to_all.54.sums_ref, f32[8,128]{1,0:T(8,128)S(1)} %get-tuple-element.13.scalars_ref, f32[16,72,128]{2,1,0:T(8,128)S(1)} %all_to_all.53.z_ref, bf16[16,256,128]{2,1,0:T(8,128)(2,1)} %copy-done.1, f32[16,72,128]{2,1,0:T(8,128)S(1)} %collective-permute-done.3.z_other_ref, ...), custom_call_target="tpu_custom_call" | custom-call | flops 536870912 | bytes 8388608 | tf_op jit(solution)/shard_map/apply_tile/pallas_call | solution.py:252
  193.6 16.8 %all_to_all.55 = f32[16,32,128]{2,1,0:T(8,128)S(1)} all-to-all(f32[16,32,128]{2,1,0:T(8,128)S(1)} %apply_tile.1), channel_id=1, replica_groups=mesh['z'=16,'core'=2,'ctr'=16] {'z'}, dimensions={0} | all-to-all | bytes 524288 | tf_op jit(solution)/shard_map/all_to_all | solution.py:30
  210.5 22.8 %all_to_all.56.u_ref = bf16[16,32,128]{2,1,0:T(8,128)(2,1)S(1)} all-to-all(bf16[16,32,128]{2,1,0:T(8,128)(2,1)S(1)} %broadcast_in_dim.17), channel_id=1, replica_groups=mesh['z'=16,'core'=2,'ctr'=16] {'z'}, dimensions={0} | all-to-all | bytes 262144 | tf_op jit(solution)/shard_map/all_to_all | solution.py:30
  233.3 3.5 %back_tile.7 = f32[16,72,128]{2,1,0:T(8,128)S(1)} custom-call(bf16[16,32,128]{2,1,0:T(8,128)(2,1)S(1)} %all_to_all.56.u_ref, bf16[4096,1024]{1,0:T(8,128)(2,1)} %get-tuple-element.11.tile_ref), custom_call_target="tpu_custom_call" | custom-call | flops 268435456 | bytes 4194304 | tf_op jit(solution)/shard_map/back_tile/pallas_call | solution.py:265
  236.8 5.7 %collective-permute-start.4 = (f32[16,72,128]{2,1,0:T(8,128)S(1)}, f32[16,72,128]{2,1,0:T(8,128)S(1)}, u32[]{:S(2)}, u32[]{:S(2)}) collective-permute-start(f32[16,72,128]{2,1,0:T(8,128)S(1)} %back_tile.7), channel_id=1, source_target_pairs={{0,16},{16,0},{1,17},{17,1},{2,18},{18,2},{3,19},{19,3},{4,20},{20... | collective-permute-start | bytes 1769480 | tf_op jit(solution)/shard_map/ppermute | solution.py:39
  242.5 3.5 %back_tile.6 = f32[16,72,128]{2,1,0:T(8,128)S(1)} custom-call(bf16[16,32,128]{2,1,0:T(8,128)(2,1)S(1)} %all_to_all.56.u_ref, bf16[4096,1024]{1,0:T(8,128)(2,1)} %get-tuple-element.11.tile_ref), custom_call_target="tpu_custom_call" | custom-call | flops 268435456 | bytes 4194304 | tf_op jit(solution)/shard_map/back_tile/pallas_call | solution.py:265
  246.1 14.9 %all_to_all.57.v_ref = f32[16,72,128]{2,1,0:T(8,128)S(1)} all-to-all(f32[16,72,128]{2,1,0:T(8,128)S(1)} %add.17), channel_id=1, replica_groups=mesh['z'=16,'core'=2,'ctr'=16] {'ctr'}, dimensions={0} | all-to-all | bytes 1179648 | tf_op jit(solution)/shard_map/all_to_all | solution.py:30
  261.0 0.8 last_kernel.1
  (42 shorter events, 1.3 us)
Async XLA Ops:
  0.6 30.9 %copy-start = (bf16[1024,128]{1,0:T(8,128)(2,1)S(1)}, bf16[1024,128]{1,0:T(8,128)(2,1)}, u32[]{:S(2)}) copy-start(bf16[1024,128]{1,0:T(8,128)(2,1)} %param.10) | copy-start | bytes 786436
  0.6 80.5 %copy-start.6 = (f32[128,128]{1,0:T(8,128)S(1)}, f32[128,128]{1,0:T(8,128)}, u32[]{:S(2)}) copy-start(f32[128,128]{1,0:T(8,128)} %param.12) | copy-start | bytes 196612
  0.7 90.3 %copy-start.3 = (f32[128,64]{0,1:T(8,128)S(1)}, f32[128,64]{0,1:T(8,128)}, u32[]{:S(2)}) copy-start(f32[128,64]{0,1:T(8,128)} %param.14) | copy-start | bytes 98308
  3.4 22.1 %all-to-all-start.1 = ((bf16[16,256,128]{2,1,0:T(8,128)(2,1)}), bf16[16,256,128]{2,1,0:T(8,128)(2,1)S(1)}, u32[]{:S(2)}, u32[]{:S(2)}) async-start(bf16[16,256,128]{2,1,0:T(8,128)(2,1)} %broadcast_in_dim.13), calls=%async_computation.1 | async-start | bytes 2097152 | tf_op jit(solution)/shard_map/all_to_all | solution.py:30
  25.5 95.6 %copy-start.1 = (bf16[16,256,128]{2,1,0:T(8,128)(2,1)}, bf16[16,256,128]{2,1,0:T(8,128)(2,1)S(1)}, u32[]{:S(2)}) copy-start(bf16[16,256,128]{2,1,0:T(8,128)(2,1)S(1)} %all-to-all-done.1.own_ref.p_ref) | copy-start | bytes 3145732
  25.5 35.3 %collective-permute-start = (bf16[16,256,128]{2,1,0:T(8,128)(2,1)S(1)}, bf16[16,256,128]{2,1,0:T(8,128)(2,1)S(1)}, u32[]{:S(2)}, u32[]{:S(2)}) collective-permute-start(bf16[16,256,128]{2,1,0:T(8,128)(2,1)S(1)} %all-to-all-done.1.own_ref.p_ref), channel_id=1, source_target_pairs={{0,16},{16,0},{1,17},{17,1},{2,18},{18,2},{3,19},{19,3},{4,20},{20... | collective-permute-start | bytes 3145736 | tf_op jit(solution)/shard_map/ppermute | solution.py:39
  60.8 1.1 copy-start.5
  71.2 23.6 %all-to-all-start.2 = ((f32[16,32,128]{2,1,0:T(8,128)}), f32[16,32,128]{2,1,0:T(8,128)S(1)}, u32[]{:S(2)}, u32[]{:S(2)}) async-start(f32[16,32,128]{2,1,0:T(8,128)} %get-tuple-element.10), calls=%async_computation.2 | async-start | bytes 524288 | tf_op jit(solution)/shard_map/all_to_all | solution.py:30
  117.5 29.1 %copy-start.2 = (f32[128,64]{0,1:T(8,128)S(1)}, f32[128,64]{0,1:T(8,128)}, u32[]{:S(2)}) copy-start(f32[128,64]{0,1:T(8,128)} %param.15) | copy-start | bytes 98308
  121.1 10.5 %collective-permute-start.1 = (f32[16,72,128]{2,1,0:T(8,128)S(1)}, f32[16,72,128]{2,1,0:T(8,128)S(1)}, u32[]{:S(2)}, u32[]{:S(2)}) collective-permute-start(f32[16,72,128]{2,1,0:T(8,128)S(1)} %back_tile.5), channel_id=1, source_target_pairs={{0,16},{16,0},{1,17},{17,1},{2,18},{18,2},{3,19},{19,3},{4,20},{20... | collective-permute-start | bytes 1769480 | tf_op jit(solution)/shard_map/ppermute | solution.py:39
  147.4 3.5 %collective-permute-start.2 = (f32[8,128]{1,0:T(8,128)S(1)}, f32[8,128]{1,0:T(8,128)S(1)}, u32[]{:S(2)}, u32[]{:S(2)}) collective-permute-start(f32[8,128]{1,0:T(8,128)S(1)} %stack.35), channel_id=1, source_target_pairs={{0,16},{16,0},{1,17},{17,1},{2,18},{18,2},{3,19},{19,3},{4,20},{20... | collective-permute-start | bytes 12296 | tf_op jit(solution)/shard_map/ppermute | solution.py:39
  165.3 19.8 %collective-permute-start.3 = (f32[16,72,128]{2,1,0:T(8,128)S(1)}, f32[16,72,128]{2,1,0:T(8,128)S(1)}, u32[]{:S(2)}, u32[]{:S(2)}) collective-permute-start(f32[16,72,128]{2,1,0:T(8,128)S(1)} %all_to_all.53.z_ref), channel_id=1, source_target_pairs={{0,16},{16,0},{1,17},{17,1},{2,18},{18,2},{3,19},{19,3},{4,20},{20... | collective-permute-start | bytes 1769480 | tf_op jit(solution)/shard_map/ppermute | solution.py:39
  233.3 27.8 %copy-start.4 = (f32[128,64]{0,1:T(8,128)S(1)}, f32[128,64]{0,1:T(8,128)}, u32[]{:S(2)}) copy-start(f32[128,64]{0,1:T(8,128)} %param.13) | copy-start | bytes 98308
  236.8 9.2 %collective-permute-start.4 = (f32[16,72,128]{2,1,0:T(8,128)S(1)}, f32[16,72,128]{2,1,0:T(8,128)S(1)}, u32[]{:S(2)}, u32[]{:S(2)}) collective-permute-start(f32[16,72,128]{2,1,0:T(8,128)S(1)} %back_tile.7), channel_id=1, source_target_pairs={{0,16},{16,0},{1,17},{17,1},{2,18},{18,2},{3,19},{19,3},{4,20},{20... | collective-permute-start | bytes 1769480 | tf_op jit(solution)/shard_map/ppermute | solution.py:39

commit v10 on v9

--- a/solution.py
+++ b/solution.py
@@ -13,6 +13,7 @@
 CORES = 2
 LANES = 128
 GROUP = 2
+MERGE = 2
 ROWS = 16
 RIDE = 8
 BF = jnp.bfloat16
@@ -84,10 +85,10 @@
     return pltpu.make_async_copy(source.at[rows], target.at[rows], sems.at[step])
 
 
-def fetch(steps, tile_ref, buf, sems):
+def fetch(steps, order, tile_ref, buf, sems):
     @pl.when(pl.program_id(0) == 0)
     def _():
-        for at in range(sems.shape[0]):
+        for at in order:
             tile_copy(tile_ref, buf, sems, at).start()
 
     for step in steps:
@@ -105,6 +106,16 @@
         columns = jnp.where(lane == place + k, piece, columns)
         left = left - piece
     return columns.astype(BF)
+
+
+def start_kernel(cen_ref, p_ref, out_ref):
+    dim, outs = cen_ref.shape[0], p_ref.shape[0]
+    high = p_ref[...].astype(BF)
+    low = (p_ref[...] - high.astype(F32)).astype(BF)
+    for k in range(out_ref.shape[0]):
+        out_ref[k, :dim] = cen_ref[...]
+        out_ref[k, dim : dim + outs] = high
+        out_ref[k, dim + outs :] = low
 
 
 def build_kernel(gamma, pts_ref, own_ref, other_ref, tile_ref, u_ref, acc, buf, sems, side):
@@ -139,7 +150,13 @@
 def apply_kernel(sums_ref, scalars_ref, z_ref, p_ref, z_other_ref, p_other_ref, tile_ref, u_ref, acc, buf, sems, beta):
     step = pl.program_id(0)
     outs = acc.shape[0]
-    tiles = fetch([step, step + pl.num_programs(0)], tile_ref, buf, sems)
+    count = sems.shape[0] // (2 * MERGE)
+
+    def groups(at):
+        return [MERGE * first + m for first in (at, at + count) for m in range(MERGE)]
+
+    order = [group for at in range(count) for group in groups(at)]
+    tiles = fetch(groups(step), order, tile_ref, buf, sems)
 
     @pl.when(step == 0)
     def _():
@@ -147,14 +164,13 @@
         beta[...] = jnp.broadcast_to(rate, beta.shape)
 
     part = None
-    for tile, z, p in zip(tiles, (z_ref, z_other_ref), (p_ref, p_other_ref)):
-        vec = []
-        for g in range(GROUP):
-            high = p[g, LANES : LANES + outs].astype(F32)
-            low = p[g, LANES + outs :].astype(F32)
-            vec.append((z[g, :outs] + beta[...] * (high + low)).astype(BF))
-        term = jnp.dot(jnp.concatenate(vec, axis=1), tile, preferred_element_type=F32)
-        part = term if part is None else part + term
+    for tile, z, p in ((tiles[:MERGE], z_ref, p_ref), (tiles[MERGE:], z_other_ref, p_other_ref)):
+        for m in range(MERGE):
+            vec = []
+            for g in range(m * GROUP, (m + 1) * GROUP):
+                vec.append((z[g, :outs] + beta[...] * (p[g, :outs].astype(F32) + p[g, outs:].astype(F32))).astype(BF))
+            term = jnp.dot(jnp.concatenate(vec, axis=1), tile[m], preferred_element_type=F32)
+            part = term if part is None else part + term
     add_up(step, part, u_ref, acc)
 
 
@@ -162,7 +178,7 @@
     rows = buf.shape[0]
     outs = ub.shape[0]
     step = pl.program_id(0)
-    tile = fetch([step], tile_ref.at[pl.ds(half * rows, rows)], buf, sems)[0]
+    tile = fetch([step], range(sems.shape[0]), tile_ref.at[pl.ds(half * rows, rows)], buf, sems)[0]
     half = outs // 2
 
     @pl.when(step == 0)
@@ -249,10 +265,12 @@
         )(pts, own, other)
 
     def apply(sums, scalars, z, p, z_other, p_other, tile):
+        step_z = pl.BlockSpec((MERGE * GROUP, z.shape[1], LANES), lambda i: (i, 0, 0))
+        step_p = pl.BlockSpec((MERGE * GROUP, 2 * outs, LANES), lambda i: (i, 1, 0))
         return pl.pallas_call(
             apply_kernel,
-            grid=grid,
-            in_specs=[whole(sums.shape), whole(scalars.shape)] + [blocks(z.shape[1]), blocks(p.shape[1])] * 2 + [tiles],
+            grid=(grid[0] // MERGE,),
+            in_specs=[whole(sums.shape), whole(scalars.shape)] + [step_z, step_p] * 2 + [tiles],
             out_specs=whole(u_shape.shape),
             out_shape=u_shape,
             scratch_shapes=[acc] + copies(CORES) + [pltpu.VMEM((1, LANES), F32)],
@@ -298,9 +316,13 @@
     mine = lax.dynamic_slice_in_dim(points, lax.axis_index("ctr") * share, share, 0)
     pts = spread(mine, "z").reshape(n_pts, dim)
     p0 = direction.T
-    p0_high = lax.reduce_precision(p0, 8, 7)
-    parts = [centres, p0_high.astype(BF), (p0 - p0_high).astype(BF)]
-    own = spread(jnp.concatenate(parts, 0), "ctr")
+    parts = pl.pallas_call(
+        start_kernel,
+        out_shape=jax.ShapeDtypeStruct((n_ctr, LANES + 2 * outs, dim), BF),
+        compiler_params=SMALL,
+        name="start_kernel",
+    )(centres, p0)
+    own = exchange(parts, "ctr")
     other = other_core(own)
 
     tile, u0 = build(pts, own, other)

time: 263 us -> 260 us (0.989)
    pallas_call x1 -> x2, Pallas kernels: 8.49 us -> 6.99 us  [the longest x1 5.88 us: apply(): pl.pallas_call(apply_kernel, grid=(grid[0] // MERGE,), in_specs=[whole(su...]
where the time goes in v10:
time: 260 us; the launch traced here: 259 us
  blocking collectives  152 us (58%)
  starting transfers between devices  42.4 us (16%)
  Pallas kernels  31.4 us (12%)
  waiting for transfers between devices  18.5 us (7%)
  other arithmetic  10.1 us (4%)
  local copies, waits for them, and re-layouts  2.89 us (1%)
    all_to_all x8, blocking collectives, exchange(): return lax.all_to_all(blocks, axes, 0, 0, tiled=True)  152 us
    ppermute x5, starting transfers between devices, other_core(): return lax.ppermute(block, 'core', [(0, 1), (1, 0)])  24.9 us
    all_to_all x2, waiting for transfers between devices, exchange(): return lax.all_to_all(blocks, axes, 0, 0, tiled=True)  17.7 us
    all_to_all x2, starting transfers between devices, exchange(): return lax.all_to_all(blocks, axes, 0, 0, tiled=True)  17.5 us
    pallas_call x4, Pallas kernels, back(): pl.pallas_call(functools.partial(back_kernel, half, count), grid=grid, in...  14.1 us
    another operation x2, other arithmetic, precondition(): lax.linalg.triangular_solve(factor, lower, left_side=True, lower=True, tr...  9.82 us
    pallas_call x1, Pallas kernels, build(): pl.pallas_call(functools.partial(build_kernel, gamma), grid=grid, in_spec...  9.38 us
    pallas_call x1, Pallas kernels, apply(): pl.pallas_call(apply_kernel, grid=(grid[0] // MERGE,), in_specs=[whole(su...  5.88 us
  transfers between devices with their start and end apart: 7, of which 3 were waited for; matrix products, arithmetic and copies ran while one was open for 4% of the time, Pallas kernels for 3%

profile of v10, /device:TPU:1, one launch (start us, length us, event | category | flops | bytes accessed | tf_op | source)
XLA Modules:
  0.0 259.1 jit_solution(14056838488021376631)
XLA Ops:
  0.7 0.8 copy-done.2
  1.4 0.8 copy-done.5
  2.2 1.1 start_kernel.1
  3.3 7.6 %all-to-all-start.1 = ((bf16[16,256,128]{2,1,0:T(8,128)(2,1)}), bf16[16,256,128]{2,1,0:T(8,128)(2,1)S(1)}, u32[]{:S(2)}, u32[]{:S(2)}) async-start(bf16[16,256,128]{2,1,0:T(8,128)(2,1)} %start_kernel.1), calls=%async_computation.1 | async-start | bytes 2097152 | tf_op jit(solution)/shard_map/all_to_all | solution.py:31
  10.9 14.5 %all-to-all-done.1.own_ref.p_ref = bf16[16,256,128]{2,1,0:T(8,128)(2,1)S(1)} async-done(((bf16[16,256,128]{2,1,0:T(8,128)(2,1)}), bf16[16,256,128]{2,1,0:T(8,128)(2,1)S(1)}, u32[]{:S(2)}, u32[]{:S(2)}) %all-to-all-start.1) | async-done | bytes 1048608 | tf_op jit(solution)/shard_map/all_to_all | solution.py:31
  25.4 6.0 %collective-permute-start = (bf16[16,256,128]{2,1,0:T(8,128)(2,1)S(1)}, bf16[16,256,128]{2,1,0:T(8,128)(2,1)S(1)}, u32[]{:S(2)}, u32[]{:S(2)}) collective-permute-start(bf16[16,256,128]{2,1,0:T(8,128)(2,1)S(1)} %all-to-all-done.1.own_ref.p_ref), channel_id=1, source_target_pairs={{0,16},{16,0},{1,17},{17,1},{2,18},{18,2},{3,19},{19,3},{4,20},{20... | collective-permute-start | bytes 3145736 | tf_op jit(solution)/shard_map/ppermute | solution.py:40
  31.4 29.2 %all_to_all.50 = bf16[16,64,128]{2,1,0:T(8,128)(2,1)S(1)} all-to-all(bf16[16,64,128]{2,1,0:T(8,128)(2,1)S(1)} %broadcast_in_dim.10), channel_id=1, replica_groups=mesh['z'=16,'core'=2,'ctr'=16] {'z'}, dimensions={0} | all-to-all | bytes 524288 | tf_op jit(solution)/shard_map/all_to_all | solution.py:31
  60.7 1.1 copy-done.7
  61.7 9.4 %build_tile.1 = (bf16[4096,1024]{1,0:T(8,128)(2,1)}, f32[16,32,128]{2,1,0:T(8,128)}) custom-call(bf16[1024,128]{1,0:T(8,128)(2,1)S(1)} %bitcast.63, bf16[16,256,128]{2,1,0:T(8,128)(2,1)S(1)} %all-to-all-done.1.own_ref.p_ref, bf16[16,256,128]{2,1,0:T(8,128)(2,1)} %copy-done.7), custom_call_target="tpu_custom_call" | custom-call | flops 1610612736 | bytes 8388608 | tf_op jit(solution)/shard_map/build_tile/pallas_call | solution.py:255
  71.1 9.9 %all-to-all-start.2 = ((f32[16,32,128]{2,1,0:T(8,128)}), f32[16,32,128]{2,1,0:T(8,128)S(1)}, u32[]{:S(2)}, u32[]{:S(2)}) async-start(f32[16,32,128]{2,1,0:T(8,128)} %get-tuple-element.10), calls=%async_computation.2 | async-start | bytes 524288 | tf_op jit(solution)/shard_map/all_to_all | solution.py:31
  81.1 9.8 %custom-call.11 = f32[1,128,128]{1,2,0:T(8,128)S(1)} custom-call(f32[1,128,128]{2,1,0:T(8,128)S(1)} %select_bitcast_fusion), custom_call_target="InvertDiagBlocksLowerTriangular" | custom-call | tf_op jit(solution)/shard_map/triangular_solve/custom-call.0 | solution.py:27
  91.2 0.3 fusion.1
  91.5 3.2 %all-to-all-done.2 = f32[16,32,128]{2,1,0:T(8,128)S(1)} async-done(((f32[16,32,128]{2,1,0:T(8,128)}), f32[16,32,128]{2,1,0:T(8,128)S(1)}, u32[]{:S(2)}, u32[]{:S(2)}) %all-to-all-start.2) | async-done | bytes 262176 | tf_op jit(solution)/shard_map/all_to_all | solution.py:31
  94.9 22.6 %all_to_all.51.u_ref = bf16[16,48,128]{2,1,0:T(8,128)(2,1)S(1)} all-to-all(bf16[16,48,128]{2,1,0:T(8,128)(2,1)S(1)} %broadcast_in_dim.11), channel_id=1, replica_groups=mesh['z'=16,'core'=2,'ctr'=16] {'z'}, dimensions={0} | all-to-all | bytes 393216 | tf_op jit(solution)/shard_map/all_to_all | solution.py:31
  117.4 3.5 %back_tile.5 = f32[16,72,128]{2,1,0:T(8,128)S(1)} custom-call(bf16[16,48,128]{2,1,0:T(8,128)(2,1)S(1)} %all_to_all.51.u_ref, bf16[4096,1024]{1,0:T(8,128)(2,1)} %get-tuple-element.11.tile_ref), custom_call_target="tpu_custom_call" | custom-call | flops 268435456 | bytes 4194304 | tf_op jit(solution)/shard_map/back_tile/pallas_call | solution.py:283
  121.0 6.9 %collective-permute-start.1 = (f32[16,72,128]{2,1,0:T(8,128)S(1)}, f32[16,72,128]{2,1,0:T(8,128)S(1)}, u32[]{:S(2)}, u32[]{:S(2)}) collective-permute-start(f32[16,72,128]{2,1,0:T(8,128)S(1)} %back_tile.5), channel_id=1, source_target_pairs={{0,16},{16,0},{1,17},{17,1},{2,18},{18,2},{3,19},{19,3},{4,20},{20... | collective-permute-start | bytes 1769480 | tf_op jit(solution)/shard_map/ppermute | solution.py:40
  127.9 3.5 %back_tile.4 = f32[16,72,128]{2,1,0:T(8,128)S(1)} custom-call(bf16[16,48,128]{2,1,0:T(8,128)(2,1)S(1)} %all_to_all.51.u_ref, bf16[4096,1024]{1,0:T(8,128)(2,1)} %get-tuple-element.11.tile_ref), custom_call_target="tpu_custom_call" | custom-call | flops 268435456 | bytes 4194304 | tf_op jit(solution)/shard_map/back_tile/pallas_call | solution.py:283
  131.5 15.0 %all_to_all.52.v_ref = f32[16,72,128]{2,1,0:T(8,128)S(1)} all-to-all(f32[16,72,128]{2,1,0:T(8,128)S(1)} %add.15), channel_id=1, replica_groups=mesh['z'=16,'core'=2,'ctr'=16] {'ctr'}, dimensions={0} | all-to-all | bytes 1179648 | tf_op jit(solution)/shard_map/all_to_all | solution.py:31
  147.0 0.3 multiply_reduce_fusion
  147.3 2.7 %collective-permute-start.2 = (f32[8,128]{1,0:T(8,128)S(1)}, f32[8,128]{1,0:T(8,128)S(1)}, u32[]{:S(2)}, u32[]{:S(2)}) collective-permute-start(f32[8,128]{1,0:T(8,128)S(1)} %stack.35), channel_id=1, source_target_pairs={{0,16},{16,0},{1,17},{17,1},{2,18},{18,2},{3,19},{19,3},{4,20},{20... | collective-permute-start | bytes 12296 | tf_op jit(solution)/shard_map/ppermute | solution.py:40
  150.0 0.8 collective-permute-done.2
  150.9 14.3 %all_to_all.53.z_ref = f32[16,72,128]{2,1,0:T(8,128)S(1)} all-to-all(f32[16,72,128]{2,1,0:T(8,128)S(1)} %broadcast_in_dim.12), channel_id=1, replica_groups=mesh['z'=16,'core'=2,'ctr'=16] {'ctr'}, dimensions={0} | all-to-all | bytes 1179648 | tf_op jit(solution)/shard_map/all_to_all | solution.py:31
  165.2 3.7 %collective-permute-start.3 = (f32[16,72,128]{2,1,0:T(8,128)S(1)}, f32[16,72,128]{2,1,0:T(8,128)S(1)}, u32[]{:S(2)}, u32[]{:S(2)}) collective-permute-start(f32[16,72,128]{2,1,0:T(8,128)S(1)} %all_to_all.53.z_ref), channel_id=1, source_target_pairs={{0,16},{16,0},{1,17},{17,1},{2,18},{18,2},{3,19},{19,3},{4,20},{20... | collective-permute-start | bytes 1769480 | tf_op jit(solution)/shard_map/ppermute | solution.py:40
  168.9 16.1 %all_to_all.54.sums_ref = f32[16,8,128]{2,1,0:T(8,128)S(1)} all-to-all(f32[16,8,128]{2,1,0:T(8,128)S(1)} %broadcast_in_dim.13), channel_id=1, replica_groups=mesh['z'=16,'core'=2,'ctr'=16] {'z'}, dimensions={0} | all-to-all | bytes 131072 | tf_op jit(solution)/shard_map/all_to_all | solution.py:31
  185.0 5.9 %apply_tile.1 = f32[16,32,128]{2,1,0:T(8,128)S(1)} custom-call(f32[16,8,128]{2,1,0:T(8,128)S(1)} %all_to_all.54.sums_ref, f32[8,128]{1,0:T(8,128)S(1)} %get-tuple-element.13.scalars_ref, f32[16,72,128]{2,1,0:T(8,128)S(1)} %all_to_all.53.z_ref, bf16[16,256,128]{2,1,0:T(8,128)(2,1)} %copy-done.1, f32[16,72,128]{2,1,0:T(8,128)S(1)} %collective-permute-done.3.z_other_ref, ...), custom_call_target="tpu_custom_call" | custom-call | flops 536870912 | bytes 8388608 | tf_op jit(solution)/shard_map/apply_tile/pallas_call | solution.py:270
  190.9 16.8 %all_to_all.55 = f32[16,32,128]{2,1,0:T(8,128)S(1)} all-to-all(f32[16,32,128]{2,1,0:T(8,128)S(1)} %apply_tile.1), channel_id=1, replica_groups=mesh['z'=16,'core'=2,'ctr'=16] {'z'}, dimensions={0} | all-to-all | bytes 524288 | tf_op jit(solution)/shard_map/all_to_all | solution.py:31
  207.8 22.8 %all_to_all.56.u_ref = bf16[16,32,128]{2,1,0:T(8,128)(2,1)S(1)} all-to-all(bf16[16,32,128]{2,1,0:T(8,128)(2,1)S(1)} %broadcast_in_dim.14), channel_id=1, replica_groups=mesh['z'=16,'core'=2,'ctr'=16] {'z'}, dimensions={0} | all-to-all | bytes 262144 | tf_op jit(solution)/shard_map/all_to_all | solution.py:31
  230.6 3.5 %back_tile.7 = f32[16,72,128]{2,1,0:T(8,128)S(1)} custom-call(bf16[16,32,128]{2,1,0:T(8,128)(2,1)S(1)} %all_to_all.56.u_ref, bf16[4096,1024]{1,0:T(8,128)(2,1)} %get-tuple-element.11.tile_ref), custom_call_target="tpu_custom_call" | custom-call | flops 268435456 | bytes 4194304 | tf_op jit(solution)/shard_map/back_tile/pallas_call | solution.py:283
  234.1 5.7 %collective-permute-start.4 = (f32[16,72,128]{2,1,0:T(8,128)S(1)}, f32[16,72,128]{2,1,0:T(8,128)S(1)}, u32[]{:S(2)}, u32[]{:S(2)}) collective-permute-start(f32[16,72,128]{2,1,0:T(8,128)S(1)} %back_tile.7), channel_id=1, source_target_pairs={{0,16},{16,0},{1,17},{17,1},{2,18},{18,2},{3,19},{19,3},{4,20},{20... | collective-permute-start | bytes 1769480 | tf_op jit(solution)/shard_map/ppermute | solution.py:40
  239.8 3.5 %back_tile.6 = f32[16,72,128]{2,1,0:T(8,128)S(1)} custom-call(bf16[16,32,128]{2,1,0:T(8,128)(2,1)S(1)} %all_to_all.56.u_ref, bf16[4096,1024]{1,0:T(8,128)(2,1)} %get-tuple-element.11.tile_ref), custom_call_target="tpu_custom_call" | custom-call | flops 268435456 | bytes 4194304 | tf_op jit(solution)/shard_map/back_tile/pallas_call | solution.py:283
  243.4 14.9 %all_to_all.57.v_ref = f32[16,72,128]{2,1,0:T(8,128)S(1)} all-to-all(f32[16,72,128]{2,1,0:T(8,128)S(1)} %add.17), channel_id=1, replica_groups=mesh['z'=16,'core'=2,'ctr'=16] {'ctr'}, dimensions={0} | all-to-all | bytes 1179648 | tf_op jit(solution)/shard_map/all_to_all | solution.py:31
  258.3 0.8 last_kernel.1
  (45 shorter events, 1.3 us)
Async XLA Ops:
  0.6 30.7 %copy-start = (bf16[1024,128]{1,0:T(8,128)(2,1)S(1)}, bf16[1024,128]{1,0:T(8,128)(2,1)}, u32[]{:S(2)}) copy-start(bf16[1024,128]{1,0:T(8,128)(2,1)} %param.10) | copy-start | bytes 786436
  0.6 0.8 copy-start.2
  1.4 0.8 copy-start.5
  2.2 78.8 %copy-start.8 = (f32[128,128]{1,0:T(8,128)S(1)}, f32[128,128]{1,0:T(8,128)}, u32[]{:S(2)}) copy-start(f32[128,128]{1,0:T(8,128)} %param.12) | copy-start | bytes 196612
  2.2 88.7 %copy-start.3 = (f32[128,64]{0,1:T(8,128)S(1)}, f32[128,64]{0,1:T(8,128)}, u32[]{:S(2)}) copy-start(f32[128,64]{0,1:T(8,128)} %param.15) | copy-start | bytes 98308
  2.2 88.7 %copy-start.4 = (f32[128,64]{0,1:T(8,128)S(1)}, f32[128,64]{0,1:T(8,128)}, u32[]{:S(2)}) copy-start(f32[128,64]{0,1:T(8,128)} %param.14) | copy-start | bytes 98308
  3.3 22.1 %all-to-all-start.1 = ((bf16[16,256,128]{2,1,0:T(8,128)(2,1)}), bf16[16,256,128]{2,1,0:T(8,128)(2,1)S(1)}, u32[]{:S(2)}, u32[]{:S(2)}) async-start(bf16[16,256,128]{2,1,0:T(8,128)(2,1)} %start_kernel.1), calls=%async_computation.1 | async-start | bytes 2097152 | tf_op jit(solution)/shard_map/all_to_all | solution.py:31
  25.4 95.6 %copy-start.1 = (bf16[16,256,128]{2,1,0:T(8,128)(2,1)}, bf16[16,256,128]{2,1,0:T(8,128)(2,1)S(1)}, u32[]{:S(2)}) copy-start(bf16[16,256,128]{2,1,0:T(8,128)(2,1)S(1)} %all-to-all-done.1.own_ref.p_ref) | copy-start | bytes 3145732
  25.4 35.3 %collective-permute-start = (bf16[16,256,128]{2,1,0:T(8,128)(2,1)S(1)}, bf16[16,256,128]{2,1,0:T(8,128)(2,1)S(1)}, u32[]{:S(2)}, u32[]{:S(2)}) collective-permute-start(bf16[16,256,128]{2,1,0:T(8,128)(2,1)S(1)} %all-to-all-done.1.own_ref.p_ref), channel_id=1, source_target_pairs={{0,16},{16,0},{1,17},{17,1},{2,18},{18,2},{3,19},{19,3},{4,20},{20... | collective-permute-start | bytes 3145736 | tf_op jit(solution)/shard_map/ppermute | solution.py:40
  60.7 1.1 copy-start.7
  71.1 23.6 %all-to-all-start.2 = ((f32[16,32,128]{2,1,0:T(8,128)}), f32[16,32,128]{2,1,0:T(8,128)S(1)}, u32[]{:S(2)}, u32[]{:S(2)}) async-start(f32[16,32,128]{2,1,0:T(8,128)} %get-tuple-element.10), calls=%async_computation.2 | async-start | bytes 524288 | tf_op jit(solution)/shard_map/all_to_all | solution.py:31
  121.0 10.5 %collective-permute-start.1 = (f32[16,72,128]{2,1,0:T(8,128)S(1)}, f32[16,72,128]{2,1,0:T(8,128)S(1)}, u32[]{:S(2)}, u32[]{:S(2)}) collective-permute-start(f32[16,72,128]{2,1,0:T(8,128)S(1)} %back_tile.5), channel_id=1, source_target_pairs={{0,16},{16,0},{1,17},{17,1},{2,18},{18,2},{3,19},{19,3},{4,20},{20... | collective-permute-start | bytes 1769480 | tf_op jit(solution)/shard_map/ppermute | solution.py:40
  147.3 3.5 %collective-permute-start.2 = (f32[8,128]{1,0:T(8,128)S(1)}, f32[8,128]{1,0:T(8,128)S(1)}, u32[]{:S(2)}, u32[]{:S(2)}) collective-permute-start(f32[8,128]{1,0:T(8,128)S(1)} %stack.35), channel_id=1, source_target_pairs={{0,16},{16,0},{1,17},{17,1},{2,18},{18,2},{3,19},{19,3},{4,20},{20... | collective-permute-start | bytes 12296 | tf_op jit(solution)/shard_map/ppermute | solution.py:40
  165.2 19.8 %collective-permute-start.3 = (f32[16,72,128]{2,1,0:T(8,128)S(1)}, f32[16,72,128]{2,1,0:T(8,128)S(1)}, u32[]{:S(2)}, u32[]{:S(2)}) collective-permute-start(f32[16,72,128]{2,1,0:T(8,128)S(1)} %all_to_all.53.z_ref), channel_id=1, source_target_pairs={{0,16},{16,0},{1,17},{17,1},{2,18},{18,2},{3,19},{19,3},{4,20},{20... | collective-permute-start | bytes 1769480 | tf_op jit(solution)/shard_map/ppermute | solution.py:40
  230.6 27.8 %copy-start.6 = (f32[128,64]{0,1:T(8,128)S(1)}, f32[128,64]{0,1:T(8,128)}, u32[]{:S(2)}) copy-start(f32[128,64]{0,1:T(8,128)} %param.13) | copy-start | bytes 98308
  234.1 9.2 %collective-permute-start.4 = (f32[16,72,128]{2,1,0:T(8,128)S(1)}, f32[16,72,128]{2,1,0:T(8,128)S(1)}, u32[]{:S(2)}, u32[]{:S(2)}) collective-permute-start(f32[16,72,128]{2,1,0:T(8,128)S(1)} %back_tile.7), channel_id=1, source_target_pairs={{0,16},{16,0},{1,17},{17,1},{2,18},{18,2},{3,19},{19,3},{4,20},{20... | collective-permute-start | bytes 1769480 | tf_op jit(solution)/shard_map/ppermute | solution.py:40

commit v11 on v10

--- a/solution.py
+++ b/solution.py
@@ -19,7 +19,7 @@
 BF = jnp.bfloat16
 F32 = jnp.float32
 SMALL = pltpu.CompilerParams(vmem_limit_bytes=8 * 1024 * 1024)
-PARAMS = pltpu.CompilerParams(vmem_limit_bytes=52 * 1024 * 1024)
+PARAMS = pltpu.CompilerParams(vmem_limit_bytes=50 * 1024 * 1024)
 
 
 def precondition(factor, resid):
@@ -178,7 +178,8 @@
     rows = buf.shape[0]
     outs = ub.shape[0]
     step = pl.program_id(0)
-    tile = fetch([step], range(sems.shape[0]), tile_ref.at[pl.ds(half * rows, rows)], buf, sems)[0]
+    mine = [MERGE * step + m for m in range(MERGE)]
+    tiles = fetch(mine, range(sems.shape[0]), tile_ref.at[pl.ds(half * rows, rows)], buf, sems)
     half = outs // 2
 
     @pl.when(step == 0)
@@ -195,10 +196,11 @@
         rows.append(jnp.zeros((RIDE - count - 1, LANES), F32))
         ride[...] = jnp.concatenate(rows, axis=0)
 
-    v = lax.dot_general(ub[...], tile, (((1,), (1,)), ((), ())), preferred_element_type=F32)
-    for g in range(GROUP):
-        v_ref[g, :outs] = v[:, g * LANES : (g + 1) * LANES]
-        v_ref[g, outs:] = ride[...]
+    for m, tile in enumerate(tiles):
+        v = lax.dot_general(ub[...], tile, (((1,), (1,)), ((), ())), preferred_element_type=F32)
+        for g in range(GROUP):
+            v_ref[m * GROUP + g, :outs] = v[:, g * LANES : (g + 1) * LANES]
+            v_ref[m * GROUP + g, outs:] = ride[...]
 
 
 def totals(sums_ref):
@@ -282,9 +284,9 @@
     def back(u, tile, half, count):
         return pl.pallas_call(
             functools.partial(back_kernel, half, count),
-            grid=grid,
+            grid=(grid[0] // MERGE,),
             in_specs=[whole(u.shape), tiles],
-            out_specs=blocks(outs + RIDE),
+            out_specs=pl.BlockSpec((MERGE * GROUP, outs + RIDE, LANES), lambda i: (i, 0, 0)),
             out_shape=jax.ShapeDtypeStruct((n_ctr, outs + RIDE, LANES), F32),
             scratch_shapes=[pltpu.VMEM((outs, n_pts), BF), pltpu.VMEM((RIDE, LANES), F32)] + copies(1),
             compiler_params=PARAMS,

time: 260 us -> 255 us (0.981)
  Pallas kernels: 31.4 us -> 27.9 us
where the time goes in v11:
time: 255 us
  blocking collectives  152 us (60%)
  starting transfers between devices  42.4 us (17%)
  Pallas kernels  27.9 us (11%)
  waiting for transfers between devices  18.5 us (7%)
  other arithmetic  10.1 us (4%)
    all_to_all x8, blocking collectives, exchange(): return lax.all_to_all(blocks, axes, 0, 0, tiled=True)  152 us
    ppermute x5, starting transfers between devices, other_core(): return lax.ppermute(block, 'core', [(0, 1), (1, 0)])  24.9 us
    all_to_all x2, waiting for transfers between devices, exchange(): return lax.all_to_all(blocks, axes, 0, 0, tiled=True)  17.7 us
    all_to_all x2, starting transfers between devices, exchange(): return lax.all_to_all(blocks, axes, 0, 0, tiled=True)  17.5 us
    pallas_call x4, Pallas kernels, back(): pl.pallas_call(functools.partial(back_kernel, half, count), grid=(grid[0]...  13.6 us
    another operation x2, other arithmetic, precondition(): lax.linalg.triangular_solve(factor, lower, left_side=True, lower=True, tr...  9.82 us
    pallas_call x1, Pallas kernels, build(): pl.pallas_call(functools.partial(build_kernel, gamma), grid=grid, in_spec...  8.09 us
  transfers between devices with their start and end apart: 7, of which 3 were waited for; matrix products, arithmetic and copies ran while one was open for 4% of the time, Pallas kernels for 3%

profile of v11, /device:TPU:1, one launch (start us, length us, event | category | flops | bytes accessed | tf_op | source)
XLA Modules:
  0.0 254.5 jit_solution(11798352406545044254)
XLA Ops:
  0.7 0.8 copy-done.1
  1.4 0.8 copy-done.4
  2.2 1.1 start_kernel.1
  3.3 7.6 %all-to-all-start.1 = ((bf16[16,256,128]{2,1,0:T(8,128)(2,1)}), bf16[16,256,128]{2,1,0:T(8,128)(2,1)S(1)}, u32[]{:S(2)}, u32[]{:S(2)}) async-start(bf16[16,256,128]{2,1,0:T(8,128)(2,1)} %start_kernel.1), calls=%async_computation.1 | async-start | bytes 2097152 | tf_op jit(solution)/shard_map/all_to_all | solution.py:31
  10.9 14.5 %all-to-all-done.1.own_ref.p_ref = bf16[16,256,128]{2,1,0:T(8,128)(2,1)S(1)} async-done(((bf16[16,256,128]{2,1,0:T(8,128)(2,1)}), bf16[16,256,128]{2,1,0:T(8,128)(2,1)S(1)}, u32[]{:S(2)}, u32[]{:S(2)}) %all-to-all-start.1) | async-done | bytes 1048608 | tf_op jit(solution)/shard_map/all_to_all | solution.py:31
  25.4 6.0 %collective-permute-start = (bf16[16,256,128]{2,1,0:T(8,128)(2,1)S(1)}, bf16[16,256,128]{2,1,0:T(8,128)(2,1)S(1)}, u32[]{:S(2)}, u32[]{:S(2)}) collective-permute-start(bf16[16,256,128]{2,1,0:T(8,128)(2,1)S(1)} %all-to-all-done.1.own_ref.p_ref), channel_id=1, source_target_pairs={{0,16},{16,0},{1,17},{17,1},{2,18},{18,2},{3,19},{19,3},{4,20},{20... | collective-permute-start | bytes 3145736 | tf_op jit(solution)/shard_map/ppermute | solution.py:40
  31.4 29.2 %all_to_all.50 = bf16[16,64,128]{2,1,0:T(8,128)(2,1)S(1)} all-to-all(bf16[16,64,128]{2,1,0:T(8,128)(2,1)S(1)} %broadcast_in_dim.10), channel_id=1, replica_groups=mesh['z'=16,'core'=2,'ctr'=16] {'z'}, dimensions={0} | all-to-all | bytes 524288 | tf_op jit(solution)/shard_map/all_to_all | solution.py:31
  60.7 8.1 %build_tile.1 = (bf16[4096,1024]{1,0:T(8,128)(2,1)}, f32[16,32,128]{2,1,0:T(8,128)}) custom-call(bf16[1024,128]{1,0:T(8,128)(2,1)S(1)} %bitcast.63, bf16[16,256,128]{2,1,0:T(8,128)(2,1)S(1)} %all-to-all-done.1.own_ref.p_ref, bf16[16,256,128]{2,1,0:T(8,128)(2,1)S(1)} %collective-permute-done.other_ref.p_other_ref), custom_call_target="tpu_custom_call" | custom-call | flops 1610612736 | bytes 8388608 | tf_op jit(solution)/shard_map/build_tile/pallas_call | solution.py:257
  68.8 9.9 %all-to-all-start.2 = ((f32[16,32,128]{2,1,0:T(8,128)}), f32[16,32,128]{2,1,0:T(8,128)S(1)}, u32[]{:S(2)}, u32[]{:S(2)}) async-start(f32[16,32,128]{2,1,0:T(8,128)} %get-tuple-element.10), calls=%async_computation.2 | async-start | bytes 524288 | tf_op jit(solution)/shard_map/all_to_all | solution.py:31
  78.7 9.8 %custom-call.11 = f32[1,128,128]{1,2,0:T(8,128)S(1)} custom-call(f32[1,128,128]{2,1,0:T(8,128)S(1)} %select_bitcast_fusion), custom_call_target="InvertDiagBlocksLowerTriangular" | custom-call | tf_op jit(solution)/shard_map/triangular_solve/custom-call.0 | solution.py:27
  88.5 0.3 fusion.2
  88.8 0.3 fusion.1
  89.1 3.2 %all-to-all-done.2 = f32[16,32,128]{2,1,0:T(8,128)S(1)} async-done(((f32[16,32,128]{2,1,0:T(8,128)}), f32[16,32,128]{2,1,0:T(8,128)S(1)}, u32[]{:S(2)}, u32[]{:S(2)}) %all-to-all-start.2) | async-done | bytes 262176 | tf_op jit(solution)/shard_map/all_to_all | solution.py:31
  92.5 22.6 %all_to_all.51.u_ref = bf16[16,48,128]{2,1,0:T(8,128)(2,1)S(1)} all-to-all(bf16[16,48,128]{2,1,0:T(8,128)(2,1)S(1)} %broadcast_in_dim.11), channel_id=1, replica_groups=mesh['z'=16,'core'=2,'ctr'=16] {'z'}, dimensions={0} | all-to-all | bytes 393216 | tf_op jit(solution)/shard_map/all_to_all | solution.py:31
  115.1 3.4 %back_tile.5 = f32[16,72,128]{2,1,0:T(8,128)S(1)} custom-call(bf16[16,48,128]{2,1,0:T(8,128)(2,1)S(1)} %all_to_all.51.u_ref, bf16[4096,1024]{1,0:T(8,128)(2,1)} %get-tuple-element.11.tile_ref), custom_call_target="tpu_custom_call" | custom-call | flops 268435456 | bytes 4194304 | tf_op jit(solution)/shard_map/back_tile/pallas_call | solution.py:285
  118.5 6.9 %collective-permute-start.1 = (f32[16,72,128]{2,1,0:T(8,128)S(1)}, f32[16,72,128]{2,1,0:T(8,128)S(1)}, u32[]{:S(2)}, u32[]{:S(2)}) collective-permute-start(f32[16,72,128]{2,1,0:T(8,128)S(1)} %back_tile.5), channel_id=1, source_target_pairs={{0,16},{16,0},{1,17},{17,1},{2,18},{18,2},{3,19},{19,3},{4,20},{20... | collective-permute-start | bytes 1769480 | tf_op jit(solution)/shard_map/ppermute | solution.py:40
  125.4 3.4 %back_tile.4 = f32[16,72,128]{2,1,0:T(8,128)S(1)} custom-call(bf16[16,48,128]{2,1,0:T(8,128)(2,1)S(1)} %all_to_all.51.u_ref, bf16[4096,1024]{1,0:T(8,128)(2,1)} %get-tuple-element.11.tile_ref), custom_call_target="tpu_custom_call" | custom-call | flops 268435456 | bytes 4194304 | tf_op jit(solution)/shard_map/back_tile/pallas_call | solution.py:285
  128.9 15.0 %all_to_all.52.v_ref = f32[16,72,128]{2,1,0:T(8,128)S(1)} all-to-all(f32[16,72,128]{2,1,0:T(8,128)S(1)} %add.15), channel_id=1, replica_groups=mesh['z'=16,'core'=2,'ctr'=16] {'ctr'}, dimensions={0} | all-to-all | bytes 1179648 | tf_op jit(solution)/shard_map/all_to_all | solution.py:31
  144.4 0.3 multiply_reduce_fusion
  144.7 2.7 %collective-permute-start.2 = (f32[8,128]{1,0:T(8,128)S(1)}, f32[8,128]{1,0:T(8,128)S(1)}, u32[]{:S(2)}, u32[]{:S(2)}) collective-permute-start(f32[8,128]{1,0:T(8,128)S(1)} %stack.35), channel_id=1, source_target_pairs={{0,16},{16,0},{1,17},{17,1},{2,18},{18,2},{3,19},{19,3},{4,20},{20... | collective-permute-start | bytes 12296 | tf_op jit(solution)/shard_map/ppermute | solution.py:40
  147.4 0.8 collective-permute-done.2
  148.2 14.3 %all_to_all.53.z_ref = f32[16,72,128]{2,1,0:T(8,128)S(1)} all-to-all(f32[16,72,128]{2,1,0:T(8,128)S(1)} %broadcast_in_dim.12), channel_id=1, replica_groups=mesh['z'=16,'core'=2,'ctr'=16] {'ctr'}, dimensions={0} | all-to-all | bytes 1179648 | tf_op jit(solution)/shard_map/all_to_all | solution.py:31
  162.6 3.7 %collective-permute-start.3 = (f32[16,72,128]{2,1,0:T(8,128)S(1)}, f32[16,72,128]{2,1,0:T(8,128)S(1)}, u32[]{:S(2)}, u32[]{:S(2)}) collective-permute-start(f32[16,72,128]{2,1,0:T(8,128)S(1)} %all_to_all.53.z_ref), channel_id=1, source_target_pairs={{0,16},{16,0},{1,17},{17,1},{2,18},{18,2},{3,19},{19,3},{4,20},{20... | collective-permute-start | bytes 1769480 | tf_op jit(solution)/shard_map/ppermute | solution.py:40
  166.3 16.1 %all_to_all.54.sums_ref = f32[16,8,128]{2,1,0:T(8,128)S(1)} all-to-all(f32[16,8,128]{2,1,0:T(8,128)S(1)} %broadcast_in_dim.13), channel_id=1, replica_groups=mesh['z'=16,'core'=2,'ctr'=16] {'z'}, dimensions={0} | all-to-all | bytes 131072 | tf_op jit(solution)/shard_map/all_to_all | solution.py:31
  182.4 4.2 %apply_tile.1 = f32[16,32,128]{2,1,0:T(8,128)S(1)} custom-call(f32[16,8,128]{2,1,0:T(8,128)S(1)} %all_to_all.54.sums_ref, f32[8,128]{1,0:T(8,128)S(1)} %get-tuple-element.13.scalars_ref, f32[16,72,128]{2,1,0:T(8,128)S(1)} %all_to_all.53.z_ref, bf16[16,256,128]{2,1,0:T(8,128)(2,1)S(1)} %all-to-all-done.1.own_ref.p_ref, ...), custom_call_target="tpu_custom_call" | custom-call | flops 536870912 | bytes 8388608 | tf_op jit(solution)/shard_map/apply_tile/pallas_call | solution.py:272
  186.5 16.8 %all_to_all.55 = f32[16,32,128]{2,1,0:T(8,128)S(1)} all-to-all(f32[16,32,128]{2,1,0:T(8,128)S(1)} %apply_tile.1), channel_id=1, replica_groups=mesh['z'=16,'core'=2,'ctr'=16] {'z'}, dimensions={0} | all-to-all | bytes 524288 | tf_op jit(solution)/shard_map/all_to_all | solution.py:31
  203.4 22.8 %all_to_all.56.u_ref = bf16[16,32,128]{2,1,0:T(8,128)(2,1)S(1)} all-to-all(bf16[16,32,128]{2,1,0:T(8,128)(2,1)S(1)} %broadcast_in_dim.14), channel_id=1, replica_groups=mesh['z'=16,'core'=2,'ctr'=16] {'z'}, dimensions={0} | all-to-all | bytes 262144 | tf_op jit(solution)/shard_map/all_to_all | solution.py:31
  226.2 3.4 %back_tile.7 = f32[16,72,128]{2,1,0:T(8,128)S(1)} custom-call(bf16[16,32,128]{2,1,0:T(8,128)(2,1)S(1)} %all_to_all.56.u_ref, bf16[4096,1024]{1,0:T(8,128)(2,1)} %get-tuple-element.11.tile_ref), custom_call_target="tpu_custom_call" | custom-call | flops 268435456 | bytes 4194304 | tf_op jit(solution)/shard_map/back_tile/pallas_call | solution.py:285
  229.6 5.7 %collective-permute-start.4 = (f32[16,72,128]{2,1,0:T(8,128)S(1)}, f32[16,72,128]{2,1,0:T(8,128)S(1)}, u32[]{:S(2)}, u32[]{:S(2)}) collective-permute-start(f32[16,72,128]{2,1,0:T(8,128)S(1)} %back_tile.7), channel_id=1, source_target_pairs={{0,16},{16,0},{1,17},{17,1},{2,18},{18,2},{3,19},{19,3},{4,20},{20... | collective-permute-start | bytes 1769480 | tf_op jit(solution)/shard_map/ppermute | solution.py:40
  235.3 3.4 %back_tile.6 = f32[16,72,128]{2,1,0:T(8,128)S(1)} custom-call(bf16[16,32,128]{2,1,0:T(8,128)(2,1)S(1)} %all_to_all.56.u_ref, bf16[4096,1024]{1,0:T(8,128)(2,1)} %get-tuple-element.11.tile_ref), custom_call_target="tpu_custom_call" | custom-call | flops 268435456 | bytes 4194304 | tf_op jit(solution)/shard_map/back_tile/pallas_call | solution.py:285
  238.8 14.9 %all_to_all.57.v_ref = f32[16,72,128]{2,1,0:T(8,128)S(1)} all-to-all(f32[16,72,128]{2,1,0:T(8,128)S(1)} %add.17), channel_id=1, replica_groups=mesh['z'=16,'core'=2,'ctr'=16] {'ctr'}, dimensions={0} | all-to-all | bytes 1179648 | tf_op jit(solution)/shard_map/all_to_all | solution.py:31
  253.8 0.8 last_kernel.1
  (41 shorter events, 1.0 us)
Async XLA Ops:
  0.6 30.7 %copy-start = (bf16[1024,128]{1,0:T(8,128)(2,1)S(1)}, bf16[1024,128]{1,0:T(8,128)(2,1)}, u32[]{:S(2)}) copy-start(bf16[1024,128]{1,0:T(8,128)(2,1)} %param.10) | copy-start | bytes 786436
  0.6 0.8 copy-start.1
  1.4 0.8 copy-start.4
  2.2 76.5 %copy-start.6 = (f32[128,128]{1,0:T(8,128)S(1)}, f32[128,128]{1,0:T(8,128)}, u32[]{:S(2)}) copy-start(f32[128,128]{1,0:T(8,128)} %param.12) | copy-start | bytes 196612
  2.2 86.3 %copy-start.2 = (f32[128,64]{0,1:T(8,128)S(1)}, f32[128,64]{0,1:T(8,128)}, u32[]{:S(2)}) copy-start(f32[128,64]{0,1:T(8,128)} %param.15) | copy-start | bytes 98308
  2.2 86.3 %copy-start.3 = (f32[128,64]{0,1:T(8,128)S(1)}, f32[128,64]{0,1:T(8,128)}, u32[]{:S(2)}) copy-start(f32[128,64]{0,1:T(8,128)} %param.14) | copy-start | bytes 98308
  3.3 22.1 %all-to-all-start.1 = ((bf16[16,256,128]{2,1,0:T(8,128)(2,1)}), bf16[16,256,128]{2,1,0:T(8,128)(2,1)S(1)}, u32[]{:S(2)}, u32[]{:S(2)}) async-start(bf16[16,256,128]{2,1,0:T(8,128)(2,1)} %start_kernel.1), calls=%async_computation.1 | async-start | bytes 2097152 | tf_op jit(solution)/shard_map/all_to_all | solution.py:31
  25.4 35.3 %collective-permute-start = (bf16[16,256,128]{2,1,0:T(8,128)(2,1)S(1)}, bf16[16,256,128]{2,1,0:T(8,128)(2,1)S(1)}, u32[]{:S(2)}, u32[]{:S(2)}) collective-permute-start(bf16[16,256,128]{2,1,0:T(8,128)(2,1)S(1)} %all-to-all-done.1.own_ref.p_ref), channel_id=1, source_target_pairs={{0,16},{16,0},{1,17},{17,1},{2,18},{18,2},{3,19},{19,3},{4,20},{20... | collective-permute-start | bytes 3145736 | tf_op jit(solution)/shard_map/ppermute | solution.py:40
  68.8 23.6 %all-to-all-start.2 = ((f32[16,32,128]{2,1,0:T(8,128)}), f32[16,32,128]{2,1,0:T(8,128)S(1)}, u32[]{:S(2)}, u32[]{:S(2)}) async-start(f32[16,32,128]{2,1,0:T(8,128)} %get-tuple-element.10), calls=%async_computation.2 | async-start | bytes 524288 | tf_op jit(solution)/shard_map/all_to_all | solution.py:31
  118.5 10.3 %collective-permute-start.1 = (f32[16,72,128]{2,1,0:T(8,128)S(1)}, f32[16,72,128]{2,1,0:T(8,128)S(1)}, u32[]{:S(2)}, u32[]{:S(2)}) collective-permute-start(f32[16,72,128]{2,1,0:T(8,128)S(1)} %back_tile.5), channel_id=1, source_target_pairs={{0,16},{16,0},{1,17},{17,1},{2,18},{18,2},{3,19},{19,3},{4,20},{20... | collective-permute-start | bytes 1769480 | tf_op jit(solution)/shard_map/ppermute | solution.py:40
  144.7 3.5 %collective-permute-start.2 = (f32[8,128]{1,0:T(8,128)S(1)}, f32[8,128]{1,0:T(8,128)S(1)}, u32[]{:S(2)}, u32[]{:S(2)}) collective-permute-start(f32[8,128]{1,0:T(8,128)S(1)} %stack.35), channel_id=1, source_target_pairs={{0,16},{16,0},{1,17},{17,1},{2,18},{18,2},{3,19},{19,3},{4,20},{20... | collective-permute-start | bytes 12296 | tf_op jit(solution)/shard_map/ppermute | solution.py:40
  162.6 19.8 %collective-permute-start.3 = (f32[16,72,128]{2,1,0:T(8,128)S(1)}, f32[16,72,128]{2,1,0:T(8,128)S(1)}, u32[]{:S(2)}, u32[]{:S(2)}) collective-permute-start(f32[16,72,128]{2,1,0:T(8,128)S(1)} %all_to_all.53.z_ref), channel_id=1, source_target_pairs={{0,16},{16,0},{1,17},{17,1},{2,18},{18,2},{3,19},{19,3},{4,20},{20... | collective-permute-start | bytes 1769480 | tf_op jit(solution)/shard_map/ppermute | solution.py:40
  226.2 27.5 %copy-start.5 = (f32[128,64]{0,1:T(8,128)S(1)}, f32[128,64]{0,1:T(8,128)}, u32[]{:S(2)}) copy-start(f32[128,64]{0,1:T(8,128)} %param.13) | copy-start | bytes 98308
  229.6 9.1 %collective-permute-start.4 = (f32[16,72,128]{2,1,0:T(8,128)S(1)}, f32[16,72,128]{2,1,0:T(8,128)S(1)}, u32[]{:S(2)}, u32[]{:S(2)}) collective-permute-start(f32[16,72,128]{2,1,0:T(8,128)S(1)} %back_tile.7), channel_id=1, source_target_pairs={{0,16},{16,0},{1,17},{17,1},{2,18},{18,2},{3,19},{19,3},{4,20},{20... | collective-permute-start | bytes 1769480 | tf_op jit(solution)/shard_map/ppermute | solution.py:40

commit v12 on v11

--- a/solution.py
+++ b/solution.py
@@ -108,8 +108,13 @@
     return columns.astype(BF)
 
 
-def start_kernel(cen_ref, p_ref, out_ref):
+def start_kernel(cen_hbm, p_hbm, out_ref, cen_ref, p_ref, sems):
     dim, outs = cen_ref.shape[0], p_ref.shape[0]
+    reads = [pltpu.make_async_copy(cen_hbm, cen_ref, sems.at[0]), pltpu.make_async_copy(p_hbm, p_ref, sems.at[1])]
+    for read in reads:
+        read.start()
+    for read in reads:
+        read.wait()
     high = p_ref[...].astype(BF)
     low = (p_ref[...] - high.astype(F32)).astype(BF)
     for k in range(out_ref.shape[0]):
@@ -129,16 +134,19 @@
 
     pts = jnp.concatenate([pts_ref[...], side[...]], axis=1)
     part = None
-    for blk_ref, place in ((own_ref, step), (other_ref, step + steps)):
-        cen = jnp.concatenate([blk_ref[g, :LANES] for g in range(GROUP)], axis=0)
-        vec = jnp.concatenate([blk_ref[g, LANES : LANES + outs] for g in range(GROUP)], axis=1)
-        cen = jnp.concatenate([cen, gap_columns(cen, 0)], axis=1)
-        cross = lax.dot_general(cen, pts, (((1,), (1,)), ((), ())), preferred_element_type=F32)
-        tile = jnp.exp2((2.0 * gamma * math.log2(math.e)) * cross).astype(BF)
-        buf[rows_at(place)] = tile
-        tile_copy(buf, tile_ref, sems, place).start()
-        term = jnp.dot(vec, tile, preferred_element_type=F32)
-        part = term if part is None else part + term
+    for blk_ref, first in ((own_ref, step), (other_ref, step + steps)):
+        for m in range(MERGE):
+            blks = [blk_ref[g] for g in range(m * GROUP, (m + 1) * GROUP)]
+            place = MERGE * first + m
+            cen = jnp.concatenate([blk[:LANES] for blk in blks], axis=0)
+            vec = jnp.concatenate([blk[LANES : LANES + outs] for blk in blks], axis=1)
+            cen = jnp.concatenate([cen, gap_columns(cen, 0)], axis=1)
+            cross = lax.dot_general(cen, pts, (((1,), (1,)), ((), ())), preferred_element_type=F32)
+            tile = jnp.exp2((2.0 * gamma * math.log2(math.e)) * cross).astype(BF)
+            buf[rows_at(place)] = tile
+            tile_copy(buf, tile_ref, sems, place).start()
+            term = jnp.dot(vec, tile, preferred_element_type=F32)
+            part = term if part is None else part + term
     add_up(step, part, u_ref, acc)
 
     @pl.when(step == steps - 1)
@@ -242,7 +250,6 @@
     grid = (n_ctr // GROUP,)
     u_shape = jax.ShapeDtypeStruct((2 * n_pts // LANES, outs // 2, LANES), F32)
     whole = lambda shape: pl.BlockSpec(shape, lambda i: (0,) * len(shape))
-    blocks = lambda rows: pl.BlockSpec((GROUP, rows, LANES), lambda i: (i, 0, 0))
     tiles = pl.BlockSpec(memory_space=pltpu.HBM)
 
     def copies(halves):
@@ -256,8 +263,8 @@
     def build(pts, own, other):
         return pl.pallas_call(
             functools.partial(build_kernel, gamma),
-            grid=grid,
-            in_specs=[whole(pts.shape), blocks(own.shape[1]), blocks(own.shape[1])],
+            grid=(grid[0] // MERGE,),
+            in_specs=[whole(pts.shape)] + [pl.BlockSpec((MERGE * GROUP, own.shape[1], LANES), lambda i: (i, 0, 0))] * 2,
             out_specs=[tiles, whole(u_shape.shape)],
             out_shape=[jax.ShapeDtypeStruct((CORES * n_ctr * LANES, n_pts), BF), u_shape],
             scratch_shapes=[acc] + copies(CORES) + [pltpu.VMEM((n_pts, LANES), BF)],
@@ -320,7 +327,9 @@
     p0 = direction.T
     parts = pl.pallas_call(
         start_kernel,
+        in_specs=[pl.BlockSpec(memory_space=pltpu.HBM)] * 2,
         out_shape=jax.ShapeDtypeStruct((n_ctr, LANES + 2 * outs, dim), BF),
+        scratch_shapes=[pltpu.VMEM(centres.shape, BF), pltpu.VMEM(p0.shape, F32), pltpu.SemaphoreType.DMA((2,))],
         compiler_params=SMALL,
         name="start_kernel",
     )(centres, p0)

time: 255 us -> 255 us (level)
  no operation moved by 1% of the time
where the time goes in v12:
time: 255 us; the launch traced here: 254 us
  blocking collectives  152 us (60%)
  starting transfers between devices  42.4 us (17%)
  Pallas kernels  27.9 us (11%)
  waiting for transfers between devices  18.5 us (7%)
  other arithmetic  10.1 us (4%)
    all_to_all x8, blocking collectives, exchange(): return lax.all_to_all(blocks, axes, 0, 0, tiled=True)  152 us
    ppermute x5, starting transfers between devices, other_core(): return lax.ppermute(block, 'core', [(0, 1), (1, 0)])  24.9 us
    all_to_all x2, waiting for transfers between devices, exchange(): return lax.all_to_all(blocks, axes, 0, 0, tiled=True)  17.7 us
    all_to_all x2, starting transfers between devices, exchange(): return lax.all_to_all(blocks, axes, 0, 0, tiled=True)  17.5 us
    pallas_call x4, Pallas kernels, back(): pl.pallas_call(functools.partial(back_kernel, half, count), grid=(grid[0]...  13.6 us
    another operation x2, other arithmetic, precondition(): lax.linalg.triangular_solve(factor, lower, left_side=True, lower=True, tr...  9.82 us
    pallas_call x1, Pallas kernels, build(): pl.pallas_call(functools.partial(build_kernel, gamma), grid=(grid[0] // M...  7.94 us
  transfers between devices with their start and end apart: 7, of which 3 were waited for; matrix products, arithmetic and copies ran while one was open for 4% of the time, Pallas kernels for 3%

profile of v12, /device:TPU:1, one launch (start us, length us, event | category | flops | bytes accessed | tf_op | source)
XLA Modules:
  0.0 254.5 jit_solution(16102592003501758143)
XLA Ops:
  0.7 0.8 copy-done.1
  1.4 0.8 copy-done.4
  2.2 1.2 start_kernel.1
  3.4 7.6 %all-to-all-start.1 = ((bf16[16,256,128]{2,1,0:T(8,128)(2,1)}), bf16[16,256,128]{2,1,0:T(8,128)(2,1)S(1)}, u32[]{:S(2)}, u32[]{:S(2)}) async-start(bf16[16,256,128]{2,1,0:T(8,128)(2,1)} %start_kernel.1), calls=%async_computation.1 | async-start | bytes 2097152 | tf_op jit(solution)/shard_map/all_to_all | solution.py:31
  11.0 14.5 %all-to-all-done.1.own_ref.p_ref = bf16[16,256,128]{2,1,0:T(8,128)(2,1)S(1)} async-done(((bf16[16,256,128]{2,1,0:T(8,128)(2,1)}), bf16[16,256,128]{2,1,0:T(8,128)(2,1)S(1)}, u32[]{:S(2)}, u32[]{:S(2)}) %all-to-all-start.1) | async-done | bytes 1048608 | tf_op jit(solution)/shard_map/all_to_all | solution.py:31
  25.5 6.0 %collective-permute-start = (bf16[16,256,128]{2,1,0:T(8,128)(2,1)S(1)}, bf16[16,256,128]{2,1,0:T(8,128)(2,1)S(1)}, u32[]{:S(2)}, u32[]{:S(2)}) collective-permute-start(bf16[16,256,128]{2,1,0:T(8,128)(2,1)S(1)} %all-to-all-done.1.own_ref.p_ref), channel_id=1, source_target_pairs={{0,16},{16,0},{1,17},{17,1},{2,18},{18,2},{3,19},{19,3},{4,20},{20... | collective-permute-start | bytes 3145736 | tf_op jit(solution)/shard_map/ppermute | solution.py:40
  31.6 29.2 %all_to_all.50 = bf16[16,64,128]{2,1,0:T(8,128)(2,1)S(1)} all-to-all(bf16[16,64,128]{2,1,0:T(8,128)(2,1)S(1)} %broadcast_in_dim.10), channel_id=1, replica_groups=mesh['z'=16,'core'=2,'ctr'=16] {'z'}, dimensions={0} | all-to-all | bytes 524288 | tf_op jit(solution)/shard_map/all_to_all | solution.py:31
  60.8 7.9 %build_tile.1 = (bf16[4096,1024]{1,0:T(8,128)(2,1)}, f32[16,32,128]{2,1,0:T(8,128)}) custom-call(bf16[1024,128]{1,0:T(8,128)(2,1)S(1)} %bitcast.63, bf16[16,256,128]{2,1,0:T(8,128)(2,1)S(1)} %all-to-all-done.1.own_ref.p_ref, bf16[16,256,128]{2,1,0:T(8,128)(2,1)S(1)} %collective-permute-done.other_ref.p_other_ref), custom_call_target="tpu_custom_call" | custom-call | flops 1610612736 | bytes 8388608 | tf_op jit(solution)/shard_map/build_tile/pallas_call | solution.py:264
  68.7 9.9 %all-to-all-start.2 = ((f32[16,32,128]{2,1,0:T(8,128)}), f32[16,32,128]{2,1,0:T(8,128)S(1)}, u32[]{:S(2)}, u32[]{:S(2)}) async-start(f32[16,32,128]{2,1,0:T(8,128)} %get-tuple-element.10), calls=%async_computation.2 | async-start | bytes 524288 | tf_op jit(solution)/shard_map/all_to_all | solution.py:31
  78.7 9.8 %custom-call.11 = f32[1,128,128]{1,2,0:T(8,128)S(1)} custom-call(f32[1,128,128]{2,1,0:T(8,128)S(1)} %select_bitcast_fusion), custom_call_target="InvertDiagBlocksLowerTriangular" | custom-call | tf_op jit(solution)/shard_map/triangular_solve/custom-call.0 | solution.py:27
  88.5 0.3 fusion.2
  88.8 0.3 fusion.1
  89.1 3.2 %all-to-all-done.2 = f32[16,32,128]{2,1,0:T(8,128)S(1)} async-done(((f32[16,32,128]{2,1,0:T(8,128)}), f32[16,32,128]{2,1,0:T(8,128)S(1)}, u32[]{:S(2)}, u32[]{:S(2)}) %all-to-all-start.2) | async-done | bytes 262176 | tf_op jit(solution)/shard_map/all_to_all | solution.py:31
  92.5 22.6 %all_to_all.51.u_ref = bf16[16,48,128]{2,1,0:T(8,128)(2,1)S(1)} all-to-all(bf16[16,48,128]{2,1,0:T(8,128)(2,1)S(1)} %broadcast_in_dim.11), channel_id=1, replica_groups=mesh['z'=16,'core'=2,'ctr'=16] {'z'}, dimensions={0} | all-to-all | bytes 393216 | tf_op jit(solution)/shard_map/all_to_all | solution.py:31
  115.0 3.4 %back_tile.5 = f32[16,72,128]{2,1,0:T(8,128)S(1)} custom-call(bf16[16,48,128]{2,1,0:T(8,128)(2,1)S(1)} %all_to_all.51.u_ref, bf16[4096,1024]{1,0:T(8,128)(2,1)} %get-tuple-element.11.tile_ref), custom_call_target="tpu_custom_call" | custom-call | flops 268435456 | bytes 4194304 | tf_op jit(solution)/shard_map/back_tile/pallas_call | solution.py:292
  118.5 6.9 %collective-permute-start.1 = (f32[16,72,128]{2,1,0:T(8,128)S(1)}, f32[16,72,128]{2,1,0:T(8,128)S(1)}, u32[]{:S(2)}, u32[]{:S(2)}) collective-permute-start(f32[16,72,128]{2,1,0:T(8,128)S(1)} %back_tile.5), channel_id=1, source_target_pairs={{0,16},{16,0},{1,17},{17,1},{2,18},{18,2},{3,19},{19,3},{4,20},{20... | collective-permute-start | bytes 1769480 | tf_op jit(solution)/shard_map/ppermute | solution.py:40
  125.4 3.4 %back_tile.4 = f32[16,72,128]{2,1,0:T(8,128)S(1)} custom-call(bf16[16,48,128]{2,1,0:T(8,128)(2,1)S(1)} %all_to_all.51.u_ref, bf16[4096,1024]{1,0:T(8,128)(2,1)} %get-tuple-element.11.tile_ref), custom_call_target="tpu_custom_call" | custom-call | flops 268435456 | bytes 4194304 | tf_op jit(solution)/shard_map/back_tile/pallas_call | solution.py:292
  128.9 15.0 %all_to_all.52.v_ref = f32[16,72,128]{2,1,0:T(8,128)S(1)} all-to-all(f32[16,72,128]{2,1,0:T(8,128)S(1)} %add.15), channel_id=1, replica_groups=mesh['z'=16,'core'=2,'ctr'=16] {'ctr'}, dimensions={0} | all-to-all | bytes 1179648 | tf_op jit(solution)/shard_map/all_to_all | solution.py:31
  144.3 0.3 multiply_reduce_fusion
  144.6 2.7 %collective-permute-start.2 = (f32[8,128]{1,0:T(8,128)S(1)}, f32[8,128]{1,0:T(8,128)S(1)}, u32[]{:S(2)}, u32[]{:S(2)}) collective-permute-start(f32[8,128]{1,0:T(8,128)S(1)} %stack.35), channel_id=1, source_target_pairs={{0,16},{16,0},{1,17},{17,1},{2,18},{18,2},{3,19},{19,3},{4,20},{20... | collective-permute-start | bytes 12296 | tf_op jit(solution)/shard_map/ppermute | solution.py:40
  147.4 0.8 collective-permute-done.2
  148.2 14.3 %all_to_all.53.z_ref = f32[16,72,128]{2,1,0:T(8,128)S(1)} all-to-all(f32[16,72,128]{2,1,0:T(8,128)S(1)} %broadcast_in_dim.12), channel_id=1, replica_groups=mesh['z'=16,'core'=2,'ctr'=16] {'ctr'}, dimensions={0} | all-to-all | bytes 1179648 | tf_op jit(solution)/shard_map/all_to_all | solution.py:31
  162.5 3.7 %collective-permute-start.3 = (f32[16,72,128]{2,1,0:T(8,128)S(1)}, f32[16,72,128]{2,1,0:T(8,128)S(1)}, u32[]{:S(2)}, u32[]{:S(2)}) collective-permute-start(f32[16,72,128]{2,1,0:T(8,128)S(1)} %all_to_all.53.z_ref), channel_id=1, source_target_pairs={{0,16},{16,0},{1,17},{17,1},{2,18},{18,2},{3,19},{19,3},{4,20},{20... | collective-permute-start | bytes 1769480 | tf_op jit(solution)/shard_map/ppermute | solution.py:40
  166.3 16.1 %all_to_all.54.sums_ref = f32[16,8,128]{2,1,0:T(8,128)S(1)} all-to-all(f32[16,8,128]{2,1,0:T(8,128)S(1)} %broadcast_in_dim.13), channel_id=1, replica_groups=mesh['z'=16,'core'=2,'ctr'=16] {'z'}, dimensions={0} | all-to-all | bytes 131072 | tf_op jit(solution)/shard_map/all_to_all | solution.py:31
  182.3 4.2 %apply_tile.1 = f32[16,32,128]{2,1,0:T(8,128)S(1)} custom-call(f32[16,8,128]{2,1,0:T(8,128)S(1)} %all_to_all.54.sums_ref, f32[8,128]{1,0:T(8,128)S(1)} %get-tuple-element.13.scalars_ref, f32[16,72,128]{2,1,0:T(8,128)S(1)} %all_to_all.53.z_ref, bf16[16,256,128]{2,1,0:T(8,128)(2,1)S(1)} %all-to-all-done.1.own_ref.p_ref, ...), custom_call_target="tpu_custom_call" | custom-call | flops 536870912 | bytes 8388608 | tf_op jit(solution)/shard_map/apply_tile/pallas_call | solution.py:279
  186.5 16.8 %all_to_all.55 = f32[16,32,128]{2,1,0:T(8,128)S(1)} all-to-all(f32[16,32,128]{2,1,0:T(8,128)S(1)} %apply_tile.1), channel_id=1, replica_groups=mesh['z'=16,'core'=2,'ctr'=16] {'z'}, dimensions={0} | all-to-all | bytes 524288 | tf_op jit(solution)/shard_map/all_to_all | solution.py:31
  203.4 22.8 %all_to_all.56.u_ref = bf16[16,32,128]{2,1,0:T(8,128)(2,1)S(1)} all-to-all(bf16[16,32,128]{2,1,0:T(8,128)(2,1)S(1)} %broadcast_in_dim.14), channel_id=1, replica_groups=mesh['z'=16,'core'=2,'ctr'=16] {'z'}, dimensions={0} | all-to-all | bytes 262144 | tf_op jit(solution)/shard_map/all_to_all | solution.py:31
  226.2 3.4 %back_tile.7 = f32[16,72,128]{2,1,0:T(8,128)S(1)} custom-call(bf16[16,32,128]{2,1,0:T(8,128)(2,1)S(1)} %all_to_all.56.u_ref, bf16[4096,1024]{1,0:T(8,128)(2,1)} %get-tuple-element.11.tile_ref), custom_call_target="tpu_custom_call" | custom-call | flops 268435456 | bytes 4194304 | tf_op jit(solution)/shard_map/back_tile/pallas_call | solution.py:292
  229.6 5.7 %collective-permute-start.4 = (f32[16,72,128]{2,1,0:T(8,128)S(1)}, f32[16,72,128]{2,1,0:T(8,128)S(1)}, u32[]{:S(2)}, u32[]{:S(2)}) collective-permute-start(f32[16,72,128]{2,1,0:T(8,128)S(1)} %back_tile.7), channel_id=1, source_target_pairs={{0,16},{16,0},{1,17},{17,1},{2,18},{18,2},{3,19},{19,3},{4,20},{20... | collective-permute-start | bytes 1769480 | tf_op jit(solution)/shard_map/ppermute | solution.py:40
  235.3 3.4 %back_tile.6 = f32[16,72,128]{2,1,0:T(8,128)S(1)} custom-call(bf16[16,32,128]{2,1,0:T(8,128)(2,1)S(1)} %all_to_all.56.u_ref, bf16[4096,1024]{1,0:T(8,128)(2,1)} %get-tuple-element.11.tile_ref), custom_call_target="tpu_custom_call" | custom-call | flops 268435456 | bytes 4194304 | tf_op jit(solution)/shard_map/back_tile/pallas_call | solution.py:292
  238.8 14.9 %all_to_all.57.v_ref = f32[16,72,128]{2,1,0:T(8,128)S(1)} all-to-all(f32[16,72,128]{2,1,0:T(8,128)S(1)} %add.17), channel_id=1, replica_groups=mesh['z'=16,'core'=2,'ctr'=16] {'ctr'}, dimensions={0} | all-to-all | bytes 1179648 | tf_op jit(solution)/shard_map/all_to_all | solution.py:31
  253.7 0.8 last_kernel.1
  (41 shorter events, 1.0 us)
Async XLA Ops:
  0.6 30.9 %copy-start = (bf16[1024,128]{1,0:T(8,128)(2,1)S(1)}, bf16[1024,128]{1,0:T(8,128)(2,1)}, u32[]{:S(2)}) copy-start(bf16[1024,128]{1,0:T(8,128)(2,1)} %param.10) | copy-start | bytes 786436
  0.6 0.8 copy-start.1
  1.4 0.8 copy-start.4
  2.2 76.4 %copy-start.6 = (f32[128,128]{1,0:T(8,128)S(1)}, f32[128,128]{1,0:T(8,128)}, u32[]{:S(2)}) copy-start(f32[128,128]{1,0:T(8,128)} %param.12) | copy-start | bytes 196612
  2.2 86.3 %copy-start.2 = (f32[128,64]{0,1:T(8,128)S(1)}, f32[128,64]{0,1:T(8,128)}, u32[]{:S(2)}) copy-start(f32[128,64]{0,1:T(8,128)} %param.15) | copy-start | bytes 98308
  2.2 86.3 %copy-start.3 = (f32[128,64]{0,1:T(8,128)S(1)}, f32[128,64]{0,1:T(8,128)}, u32[]{:S(2)}) copy-start(f32[128,64]{0,1:T(8,128)} %param.14) | copy-start | bytes 98308
  3.4 22.1 %all-to-all-start.1 = ((bf16[16,256,128]{2,1,0:T(8,128)(2,1)}), bf16[16,256,128]{2,1,0:T(8,128)(2,1)S(1)}, u32[]{:S(2)}, u32[]{:S(2)}) async-start(bf16[16,256,128]{2,1,0:T(8,128)(2,1)} %start_kernel.1), calls=%async_computation.1 | async-start | bytes 2097152 | tf_op jit(solution)/shard_map/all_to_all | solution.py:31
  25.5 35.3 %collective-permute-start = (bf16[16,256,128]{2,1,0:T(8,128)(2,1)S(1)}, bf16[16,256,128]{2,1,0:T(8,128)(2,1)S(1)}, u32[]{:S(2)}, u32[]{:S(2)}) collective-permute-start(bf16[16,256,128]{2,1,0:T(8,128)(2,1)S(1)} %all-to-all-done.1.own_ref.p_ref), channel_id=1, source_target_pairs={{0,16},{16,0},{1,17},{17,1},{2,18},{18,2},{3,19},{19,3},{4,20},{20... | collective-permute-start | bytes 3145736 | tf_op jit(solution)/shard_map/ppermute | solution.py:40
  68.7 23.6 %all-to-all-start.2 = ((f32[16,32,128]{2,1,0:T(8,128)}), f32[16,32,128]{2,1,0:T(8,128)S(1)}, u32[]{:S(2)}, u32[]{:S(2)}) async-start(f32[16,32,128]{2,1,0:T(8,128)} %get-tuple-element.10), calls=%async_computation.2 | async-start | bytes 524288 | tf_op jit(solution)/shard_map/all_to_all | solution.py:31
  118.5 10.3 %collective-permute-start.1 = (f32[16,72,128]{2,1,0:T(8,128)S(1)}, f32[16,72,128]{2,1,0:T(8,128)S(1)}, u32[]{:S(2)}, u32[]{:S(2)}) collective-permute-start(f32[16,72,128]{2,1,0:T(8,128)S(1)} %back_tile.5), channel_id=1, source_target_pairs={{0,16},{16,0},{1,17},{17,1},{2,18},{18,2},{3,19},{19,3},{4,20},{20... | collective-permute-start | bytes 1769480 | tf_op jit(solution)/shard_map/ppermute | solution.py:40
  144.6 3.5 %collective-permute-start.2 = (f32[8,128]{1,0:T(8,128)S(1)}, f32[8,128]{1,0:T(8,128)S(1)}, u32[]{:S(2)}, u32[]{:S(2)}) collective-permute-start(f32[8,128]{1,0:T(8,128)S(1)} %stack.35), channel_id=1, source_target_pairs={{0,16},{16,0},{1,17},{17,1},{2,18},{18,2},{3,19},{19,3},{4,20},{20... | collective-permute-start | bytes 12296 | tf_op jit(solution)/shard_map/ppermute | solution.py:40
  162.5 19.8 %collective-permute-start.3 = (f32[16,72,128]{2,1,0:T(8,128)S(1)}, f32[16,72,128]{2,1,0:T(8,128)S(1)}, u32[]{:S(2)}, u32[]{:S(2)}) collective-permute-start(f32[16,72,128]{2,1,0:T(8,128)S(1)} %all_to_all.53.z_ref), channel_id=1, source_target_pairs={{0,16},{16,0},{1,17},{17,1},{2,18},{18,2},{3,19},{19,3},{4,20},{20... | collective-permute-start | bytes 1769480 | tf_op jit(solution)/shard_map/ppermute | solution.py:40
  226.2 27.5 %copy-start.5 = (f32[128,64]{0,1:T(8,128)S(1)}, f32[128,64]{0,1:T(8,128)}, u32[]{:S(2)}) copy-start(f32[128,64]{0,1:T(8,128)} %param.13) | copy-start | bytes 98308
  229.6 9.1 %collective-permute-start.4 = (f32[16,72,128]{2,1,0:T(8,128)S(1)}, f32[16,72,128]{2,1,0:T(8,128)S(1)}, u32[]{:S(2)}, u32[]{:S(2)}) collective-permute-start(f32[16,72,128]{2,1,0:T(8,128)S(1)} %back_tile.7), channel_id=1, source_target_pairs={{0,16},{16,0},{1,17},{17,1},{2,18},{18,2},{3,19},{19,3},{4,20},{20... | collective-permute-start | bytes 1769480 | tf_op jit(solution)/shard_map/ppermute | solution.py:40

commit v13 on v12

--- a/solution.py
+++ b/solution.py
@@ -330,7 +330,7 @@
         in_specs=[pl.BlockSpec(memory_space=pltpu.HBM)] * 2,
         out_shape=jax.ShapeDtypeStruct((n_ctr, LANES + 2 * outs, dim), BF),
         scratch_shapes=[pltpu.VMEM(centres.shape, BF), pltpu.VMEM(p0.shape, F32), pltpu.SemaphoreType.DMA((2,))],
-        compiler_params=SMALL,
+        compiler_params=pltpu.CompilerParams(vmem_limit_bytes=62 * 1024 * 1024),
         name="start_kernel",
     )(centres, p0)
     own = exchange(parts, "ctr")

time: 255 us -> 254 us (level)
  no operation moved by 1% of the time
where the time goes in v13:
time: 254 us
  blocking collectives  152 us (60%)
  starting transfers between devices  42.4 us (17%)
  Pallas kernels  28.6 us (11%)
  waiting for transfers between devices  18.5 us (7%)
  other arithmetic  10.1 us (4%)
    all_to_all x8, blocking collectives, exchange(): return lax.all_to_all(blocks, axes, 0, 0, tiled=True)  152 us
    ppermute x5, starting transfers between devices, other_core(): return lax.ppermute(block, 'core', [(0, 1), (1, 0)])  24.9 us
    all_to_all x2, waiting for transfers between devices, exchange(): return lax.all_to_all(blocks, axes, 0, 0, tiled=True)  17.7 us
    all_to_all x2, starting transfers between devices, exchange(): return lax.all_to_all(blocks, axes, 0, 0, tiled=True)  17.5 us
    pallas_call x4, Pallas kernels, back(): pl.pallas_call(functools.partial(back_kernel, half, count), grid=(grid[0]...  13.6 us
    another operation x2, other arithmetic, precondition(): lax.linalg.triangular_solve(factor, lower, left_side=True, lower=True, tr...  9.82 us
    pallas_call x1, Pallas kernels, build(): pl.pallas_call(functools.partial(build_kernel, gamma), grid=(grid[0] // M...  7.94 us
  transfers between devices with their start and end apart: 7, of which 3 were waited for; matrix products, arithmetic and copies ran while one was open for 4% of the time, Pallas kernels for 3%

profile of v13, /device:TPU:1, one launch (start us, length us, event | category | flops | bytes accessed | tf_op | source)
XLA Modules:
  0.0 253.7 jit_solution(17504866580985368574)
XLA Ops:
  0.7 2.0 start_kernel.1
  2.6 7.6 %all-to-all-start.1 = ((bf16[16,256,128]{2,1,0:T(8,128)(2,1)}), bf16[16,256,128]{2,1,0:T(8,128)(2,1)S(1)}, u32[]{:S(2)}, u32[]{:S(2)}) async-start(bf16[16,256,128]{2,1,0:T(8,128)(2,1)} %start_kernel.1), calls=%async_computation.1 | async-start | bytes 2097152 | tf_op jit(solution)/shard_map/all_to_all | solution.py:31
  10.2 14.5 %all-to-all-done.1.own_ref.p_ref = bf16[16,256,128]{2,1,0:T(8,128)(2,1)S(1)} async-done(((bf16[16,256,128]{2,1,0:T(8,128)(2,1)}), bf16[16,256,128]{2,1,0:T(8,128)(2,1)S(1)}, u32[]{:S(2)}, u32[]{:S(2)}) %all-to-all-start.1) | async-done | bytes 1048608 | tf_op jit(solution)/shard_map/all_to_all | solution.py:31
  24.7 6.0 %collective-permute-start = (bf16[16,256,128]{2,1,0:T(8,128)(2,1)S(1)}, bf16[16,256,128]{2,1,0:T(8,128)(2,1)S(1)}, u32[]{:S(2)}, u32[]{:S(2)}) collective-permute-start(bf16[16,256,128]{2,1,0:T(8,128)(2,1)S(1)} %all-to-all-done.1.own_ref.p_ref), channel_id=1, source_target_pairs={{0,16},{16,0},{1,17},{17,1},{2,18},{18,2},{3,19},{19,3},{4,20},{20... | collective-permute-start | bytes 3145736 | tf_op jit(solution)/shard_map/ppermute | solution.py:40
  30.8 29.2 %all_to_all.50 = bf16[16,64,128]{2,1,0:T(8,128)(2,1)S(1)} all-to-all(bf16[16,64,128]{2,1,0:T(8,128)(2,1)S(1)} %broadcast_in_dim.10), channel_id=1, replica_groups=mesh['z'=16,'core'=2,'ctr'=16] {'z'}, dimensions={0} | all-to-all | bytes 524288 | tf_op jit(solution)/shard_map/all_to_all | solution.py:31
  60.0 7.9 %build_tile.1 = (bf16[4096,1024]{1,0:T(8,128)(2,1)}, f32[16,32,128]{2,1,0:T(8,128)}) custom-call(bf16[1024,128]{1,0:T(8,128)(2,1)S(1)} %bitcast.63, bf16[16,256,128]{2,1,0:T(8,128)(2,1)S(1)} %all-to-all-done.1.own_ref.p_ref, bf16[16,256,128]{2,1,0:T(8,128)(2,1)S(1)} %collective-permute-done.other_ref.p_other_ref), custom_call_target="tpu_custom_call" | custom-call | flops 1610612736 | bytes 8388608 | tf_op jit(solution)/shard_map/build_tile/pallas_call | solution.py:264
  67.9 9.9 %all-to-all-start.2 = ((f32[16,32,128]{2,1,0:T(8,128)}), f32[16,32,128]{2,1,0:T(8,128)S(1)}, u32[]{:S(2)}, u32[]{:S(2)}) async-start(f32[16,32,128]{2,1,0:T(8,128)} %get-tuple-element.10), calls=%async_computation.2 | async-start | bytes 524288 | tf_op jit(solution)/shard_map/all_to_all | solution.py:31
  77.9 9.8 %custom-call.11 = f32[1,128,128]{1,2,0:T(8,128)S(1)} custom-call(f32[1,128,128]{2,1,0:T(8,128)S(1)} %select_bitcast_fusion), custom_call_target="InvertDiagBlocksLowerTriangular" | custom-call | tf_op jit(solution)/shard_map/triangular_solve/custom-call.0 | solution.py:27
  87.7 0.3 fusion.2
  88.0 0.3 fusion.1
  88.3 3.2 %all-to-all-done.2 = f32[16,32,128]{2,1,0:T(8,128)S(1)} async-done(((f32[16,32,128]{2,1,0:T(8,128)}), f32[16,32,128]{2,1,0:T(8,128)S(1)}, u32[]{:S(2)}, u32[]{:S(2)}) %all-to-all-start.2) | async-done | bytes 262176 | tf_op jit(solution)/shard_map/all_to_all | solution.py:31
  91.7 22.6 %all_to_all.51.u_ref = bf16[16,48,128]{2,1,0:T(8,128)(2,1)S(1)} all-to-all(bf16[16,48,128]{2,1,0:T(8,128)(2,1)S(1)} %broadcast_in_dim.11), channel_id=1, replica_groups=mesh['z'=16,'core'=2,'ctr'=16] {'z'}, dimensions={0} | all-to-all | bytes 393216 | tf_op jit(solution)/shard_map/all_to_all | solution.py:31
  114.3 3.4 %back_tile.5 = f32[16,72,128]{2,1,0:T(8,128)S(1)} custom-call(bf16[16,48,128]{2,1,0:T(8,128)(2,1)S(1)} %all_to_all.51.u_ref, bf16[4096,1024]{1,0:T(8,128)(2,1)} %get-tuple-element.11.tile_ref), custom_call_target="tpu_custom_call" | custom-call | flops 268435456 | bytes 4194304 | tf_op jit(solution)/shard_map/back_tile/pallas_call | solution.py:292
  117.7 6.9 %collective-permute-start.1 = (f32[16,72,128]{2,1,0:T(8,128)S(1)}, f32[16,72,128]{2,1,0:T(8,128)S(1)}, u32[]{:S(2)}, u32[]{:S(2)}) collective-permute-start(f32[16,72,128]{2,1,0:T(8,128)S(1)} %back_tile.5), channel_id=1, source_target_pairs={{0,16},{16,0},{1,17},{17,1},{2,18},{18,2},{3,19},{19,3},{4,20},{20... | collective-permute-start | bytes 1769480 | tf_op jit(solution)/shard_map/ppermute | solution.py:40
  124.6 3.4 %back_tile.4 = f32[16,72,128]{2,1,0:T(8,128)S(1)} custom-call(bf16[16,48,128]{2,1,0:T(8,128)(2,1)S(1)} %all_to_all.51.u_ref, bf16[4096,1024]{1,0:T(8,128)(2,1)} %get-tuple-element.11.tile_ref), custom_call_target="tpu_custom_call" | custom-call | flops 268435456 | bytes 4194304 | tf_op jit(solution)/shard_map/back_tile/pallas_call | solution.py:292
  128.1 15.0 %all_to_all.52.v_ref = f32[16,72,128]{2,1,0:T(8,128)S(1)} all-to-all(f32[16,72,128]{2,1,0:T(8,128)S(1)} %add.15), channel_id=1, replica_groups=mesh['z'=16,'core'=2,'ctr'=16] {'ctr'}, dimensions={0} | all-to-all | bytes 1179648 | tf_op jit(solution)/shard_map/all_to_all | solution.py:31
  143.1 0.2 first_kernel.1
  143.2 0.3 fusion.5
  143.5 0.3 multiply_reduce_fusion
  143.9 2.7 %collective-permute-start.2 = (f32[8,128]{1,0:T(8,128)S(1)}, f32[8,128]{1,0:T(8,128)S(1)}, u32[]{:S(2)}, u32[]{:S(2)}) collective-permute-start(f32[8,128]{1,0:T(8,128)S(1)} %stack.35), channel_id=1, source_target_pairs={{0,16},{16,0},{1,17},{17,1},{2,18},{18,2},{3,19},{19,3},{4,20},{20... | collective-permute-start | bytes 12296 | tf_op jit(solution)/shard_map/ppermute | solution.py:40
  146.6 0.8 collective-permute-done.2
  147.4 14.3 %all_to_all.53.z_ref = f32[16,72,128]{2,1,0:T(8,128)S(1)} all-to-all(f32[16,72,128]{2,1,0:T(8,128)S(1)} %broadcast_in_dim.12), channel_id=1, replica_groups=mesh['z'=16,'core'=2,'ctr'=16] {'ctr'}, dimensions={0} | all-to-all | bytes 1179648 | tf_op jit(solution)/shard_map/all_to_all | solution.py:31
  161.8 3.7 %collective-permute-start.3 = (f32[16,72,128]{2,1,0:T(8,128)S(1)}, f32[16,72,128]{2,1,0:T(8,128)S(1)}, u32[]{:S(2)}, u32[]{:S(2)}) collective-permute-start(f32[16,72,128]{2,1,0:T(8,128)S(1)} %all_to_all.53.z_ref), channel_id=1, source_target_pairs={{0,16},{16,0},{1,17},{17,1},{2,18},{18,2},{3,19},{19,3},{4,20},{20... | collective-permute-start | bytes 1769480 | tf_op jit(solution)/shard_map/ppermute | solution.py:40
  165.5 16.1 %all_to_all.54.sums_ref = f32[16,8,128]{2,1,0:T(8,128)S(1)} all-to-all(f32[16,8,128]{2,1,0:T(8,128)S(1)} %broadcast_in_dim.13), channel_id=1, replica_groups=mesh['z'=16,'core'=2,'ctr'=16] {'z'}, dimensions={0} | all-to-all | bytes 131072 | tf_op jit(solution)/shard_map/all_to_all | solution.py:31
  181.5 4.2 %apply_tile.1 = f32[16,32,128]{2,1,0:T(8,128)S(1)} custom-call(f32[16,8,128]{2,1,0:T(8,128)S(1)} %all_to_all.54.sums_ref, f32[8,128]{1,0:T(8,128)S(1)} %get-tuple-element.13.scalars_ref, f32[16,72,128]{2,1,0:T(8,128)S(1)} %all_to_all.53.z_ref, bf16[16,256,128]{2,1,0:T(8,128)(2,1)S(1)} %all-to-all-done.1.own_ref.p_ref, ...), custom_call_target="tpu_custom_call" | custom-call | flops 536870912 | bytes 8388608 | tf_op jit(solution)/shard_map/apply_tile/pallas_call | solution.py:279
  185.7 16.8 %all_to_all.55 = f32[16,32,128]{2,1,0:T(8,128)S(1)} all-to-all(f32[16,32,128]{2,1,0:T(8,128)S(1)} %apply_tile.1), channel_id=1, replica_groups=mesh['z'=16,'core'=2,'ctr'=16] {'z'}, dimensions={0} | all-to-all | bytes 524288 | tf_op jit(solution)/shard_map/all_to_all | solution.py:31
  202.6 22.8 %all_to_all.56.u_ref = bf16[16,32,128]{2,1,0:T(8,128)(2,1)S(1)} all-to-all(bf16[16,32,128]{2,1,0:T(8,128)(2,1)S(1)} %broadcast_in_dim.14), channel_id=1, replica_groups=mesh['z'=16,'core'=2,'ctr'=16] {'z'}, dimensions={0} | all-to-all | bytes 262144 | tf_op jit(solution)/shard_map/all_to_all | solution.py:31
  225.4 3.4 %back_tile.7 = f32[16,72,128]{2,1,0:T(8,128)S(1)} custom-call(bf16[16,32,128]{2,1,0:T(8,128)(2,1)S(1)} %all_to_all.56.u_ref, bf16[4096,1024]{1,0:T(8,128)(2,1)} %get-tuple-element.11.tile_ref), custom_call_target="tpu_custom_call" | custom-call | flops 268435456 | bytes 4194304 | tf_op jit(solution)/shard_map/back_tile/pallas_call | solution.py:292
  228.8 5.7 %collective-permute-start.4 = (f32[16,72,128]{2,1,0:T(8,128)S(1)}, f32[16,72,128]{2,1,0:T(8,128)S(1)}, u32[]{:S(2)}, u32[]{:S(2)}) collective-permute-start(f32[16,72,128]{2,1,0:T(8,128)S(1)} %back_tile.7), channel_id=1, source_target_pairs={{0,16},{16,0},{1,17},{17,1},{2,18},{18,2},{3,19},{19,3},{4,20},{20... | collective-permute-start | bytes 1769480 | tf_op jit(solution)/shard_map/ppermute | solution.py:40
  234.5 3.4 %back_tile.6 = f32[16,72,128]{2,1,0:T(8,128)S(1)} custom-call(bf16[16,32,128]{2,1,0:T(8,128)(2,1)S(1)} %all_to_all.56.u_ref, bf16[4096,1024]{1,0:T(8,128)(2,1)} %get-tuple-element.11.tile_ref), custom_call_target="tpu_custom_call" | custom-call | flops 268435456 | bytes 4194304 | tf_op jit(solution)/shard_map/back_tile/pallas_call | solution.py:292
  238.0 14.9 %all_to_all.57.v_ref = f32[16,72,128]{2,1,0:T(8,128)S(1)} all-to-all(f32[16,72,128]{2,1,0:T(8,128)S(1)} %add.17), channel_id=1, replica_groups=mesh['z'=16,'core'=2,'ctr'=16] {'ctr'}, dimensions={0} | all-to-all | bytes 1179648 | tf_op jit(solution)/shard_map/all_to_all | solution.py:31
  252.9 0.8 last_kernel.1
  (37 shorter events, 0.5 us)
Async XLA Ops:
  0.6 30.1 %copy-start = (bf16[1024,128]{1,0:T(8,128)(2,1)S(1)}, bf16[1024,128]{1,0:T(8,128)(2,1)}, u32[]{:S(2)}) copy-start(bf16[1024,128]{1,0:T(8,128)(2,1)} %param.10) | copy-start | bytes 786436
  0.6 87.0 %copy-start.1 = (f32[128,64]{0,1:T(8,128)S(1)}, f32[128,64]{0,1:T(8,128)}, u32[]{:S(2)}) copy-start(f32[128,64]{0,1:T(8,128)} %param.15) | copy-start | bytes 98308
  0.7 77.2 %copy-start.4 = (f32[128,128]{1,0:T(8,128)S(1)}, f32[128,128]{1,0:T(8,128)}, u32[]{:S(2)}) copy-start(f32[128,128]{1,0:T(8,128)} %param.12) | copy-start | bytes 196612
  0.7 87.1 %copy-start.2 = (f32[128,64]{0,1:T(8,128)S(1)}, f32[128,64]{0,1:T(8,128)}, u32[]{:S(2)}) copy-start(f32[128,64]{0,1:T(8,128)} %param.14) | copy-start | bytes 98308
  2.6 22.1 %all-to-all-start.1 = ((bf16[16,256,128]{2,1,0:T(8,128)(2,1)}), bf16[16,256,128]{2,1,0:T(8,128)(2,1)S(1)}, u32[]{:S(2)}, u32[]{:S(2)}) async-start(bf16[16,256,128]{2,1,0:T(8,128)(2,1)} %start_kernel.1), calls=%async_computation.1 | async-start | bytes 2097152 | tf_op jit(solution)/shard_map/all_to_all | solution.py:31
  24.7 35.3 %collective-permute-start = (bf16[16,256,128]{2,1,0:T(8,128)(2,1)S(1)}, bf16[16,256,128]{2,1,0:T(8,128)(2,1)S(1)}, u32[]{:S(2)}, u32[]{:S(2)}) collective-permute-start(bf16[16,256,128]{2,1,0:T(8,128)(2,1)S(1)} %all-to-all-done.1.own_ref.p_ref), channel_id=1, source_target_pairs={{0,16},{16,0},{1,17},{17,1},{2,18},{18,2},{3,19},{19,3},{4,20},{20... | collective-permute-start | bytes 3145736 | tf_op jit(solution)/shard_map/ppermute | solution.py:40
  67.9 23.6 %all-to-all-start.2 = ((f32[16,32,128]{2,1,0:T(8,128)}), f32[16,32,128]{2,1,0:T(8,128)S(1)}, u32[]{:S(2)}, u32[]{:S(2)}) async-start(f32[16,32,128]{2,1,0:T(8,128)} %get-tuple-element.10), calls=%async_computation.2 | async-start | bytes 524288 | tf_op jit(solution)/shard_map/all_to_all | solution.py:31
  117.7 10.3 %collective-permute-start.1 = (f32[16,72,128]{2,1,0:T(8,128)S(1)}, f32[16,72,128]{2,1,0:T(8,128)S(1)}, u32[]{:S(2)}, u32[]{:S(2)}) collective-permute-start(f32[16,72,128]{2,1,0:T(8,128)S(1)} %back_tile.5), channel_id=1, source_target_pairs={{0,16},{16,0},{1,17},{17,1},{2,18},{18,2},{3,19},{19,3},{4,20},{20... | collective-permute-start | bytes 1769480 | tf_op jit(solution)/shard_map/ppermute | solution.py:40
  143.9 3.5 %collective-permute-start.2 = (f32[8,128]{1,0:T(8,128)S(1)}, f32[8,128]{1,0:T(8,128)S(1)}, u32[]{:S(2)}, u32[]{:S(2)}) collective-permute-start(f32[8,128]{1,0:T(8,128)S(1)} %stack.35), channel_id=1, source_target_pairs={{0,16},{16,0},{1,17},{17,1},{2,18},{18,2},{3,19},{19,3},{4,20},{20... | collective-permute-start | bytes 12296 | tf_op jit(solution)/shard_map/ppermute | solution.py:40
  161.8 19.8 %collective-permute-start.3 = (f32[16,72,128]{2,1,0:T(8,128)S(1)}, f32[16,72,128]{2,1,0:T(8,128)S(1)}, u32[]{:S(2)}, u32[]{:S(2)}) collective-permute-start(f32[16,72,128]{2,1,0:T(8,128)S(1)} %all_to_all.53.z_ref), channel_id=1, source_target_pairs={{0,16},{16,0},{1,17},{17,1},{2,18},{18,2},{3,19},{19,3},{4,20},{20... | collective-permute-start | bytes 1769480 | tf_op jit(solution)/shard_map/ppermute | solution.py:40
  225.4 27.5 %copy-start.3 = (f32[128,64]{0,1:T(8,128)S(1)}, f32[128,64]{0,1:T(8,128)}, u32[]{:S(2)}) copy-start(f32[128,64]{0,1:T(8,128)} %param.13) | copy-start | bytes 98308
  228.8 9.1 %collective-permute-start.4 = (f32[16,72,128]{2,1,0:T(8,128)S(1)}, f32[16,72,128]{2,1,0:T(8,128)S(1)}, u32[]{:S(2)}, u32[]{:S(2)}) collective-permute-start(f32[16,72,128]{2,1,0:T(8,128)S(1)} %back_tile.7), channel_id=1, source_target_pairs={{0,16},{16,0},{1,17},{17,1},{2,18},{18,2},{3,19},{19,3},{4,20},{20... | collective-permute-start | bytes 1769480 | tf_op jit(solution)/shard_map/ppermute | solution.py:40
